TPU v7x, 32 devices: a whole 2x2x4 slice. The times are simulated.
32 devices in a mesh: region: 4 (over z), batch: 8 (over y, x, core).
Axes of the slice: x: 2, y: 2, z: 4, core: 2. Of those that a mesh axis runs over, the one named last changes fastest.
Arguments:
- features: bfloat16 [32, 64, 1536], P('region', 'batch'), may hold values from -6 to 6
- mask: int32 [32, 512], P('region', 'batch'), may hold values 0 or 1
- owner: int32 [8], replicated, may hold values from 0 to 7, each once
- weight: bfloat16 [27, 36864], replicated, may hold values from -0.078125 to 0.078125
- bias: float32 [192], replicated, may hold values from -3 to 3
- cotangent: bfloat16 [32, 64, 1536], P('region', 'batch'), may hold values from -6 to 6
Outputs:
- activation: bfloat16 [32, 64, 1536], P('region', 'batch')
- grad_input: bfloat16 [32, 64, 1536], P('region', 'batch')
- grad_weight: bfloat16 [27, 36864], replicated
- grad_bias: float32 [192], replicated
Inputs may be any that keep to these rules, and one draw needn't show every extreme that they name: owner is a permutation: each batch index holds exactly one tile of the grid of 4 rows by 2 tiles.
All inputs are finite; a program needn't handle non-finite values. No bound on the sum of `mask` on one device may be relied on, other than what follows from the above.
Results may differ from a plain program's by a relative error of at most 0.006.
Values may be sent and summed in bfloat16 or wider, within the bound.
No kernel may reach another device: no remote copies, remote signals or barrier semaphores. Data moves between devices by JAX's collectives and lax.ppermute only.
A program may use at most 128 MiB of HBM per device.

v0:
```python
import functools

import jax
import jax.numpy as jnp
from jax import lax
from jax.experimental import pallas as pl
from jax.experimental.pallas import tpu as pltpu
from jax.sharding import PartitionSpec as P

BF = jnp.bfloat16
F32 = jnp.float32
STEPS = ((0, 1), (0, -1), (1, 0), (-1, 0), (1, 1), (1, -1), (-1, 1), (-1, -1))
EDGE = 8
ROWS = 16
VMEM = pl.BlockSpec(memory_space=pltpu.VMEM)
SMEM = pl.BlockSpec(memory_space=pltpu.SMEM)
PARAMS = pltpu.CompilerParams(vmem_limit_bytes=48 * 2**20)


def pairs(count, flip):
    return [(i, i ^ flip) for i in range(count)]


def gather_windows(where, x_ref, recv_ref, rim, patch):
    depth, _, channels = x_ref.shape
    rim[:, 1:9, 8:16, :] = x_ref[...].reshape(depth, EDGE, EDGE, channels).astype(F32)
    lines = [recv_ref[where[n]].astype(F32) for n in range(8)]
    rim[:, 1:9, 16, :] = lines[0]
    rim[:, 1:9, 7, :] = lines[1]
    rim[:, 9, 8:16, :] = lines[2]
    rim[:, 0, 8:16, :] = lines[3]
    rim[:, 9, 16, :] = lines[4][:, 0]
    rim[:, 9, 7, :] = lines[5][:, 0]
    rim[:, 0, 16, :] = lines[6][:, 7]
    rim[:, 0, 7, :] = lines[7][:, 7]

    def plane(z, carry):
        for dx in range(3):
            for dy in range(3):
                seen = rim[z, dx : dx + 8, 7 + dy : 15 + dy, :]
                row = pl.multiple_of(z * 64, 64)
                patch[dx * 3 + dy, pl.ds(row, 64), :] = seen.reshape(64, channels).astype(BF)
        return carry

    lax.fori_loop(0, depth, plane, 0)


def forward_kernel(leaf_units, n_leaves, where, x_ref, recv_ref, w_ref, bias_ref, cot_ref,
                   act_ref, gp_ref, gb_ref, gw_ref, rim, patch):
    voxels, channels = cot_ref.shape
    gather_windows(where, x_ref, recv_ref, rim, patch)
    pre = jnp.broadcast_to(bias_ref[...], (voxels, channels))
    for dz in range(3):
        for k in range(9):
            pre += jnp.dot(
                patch[k, dz * 64 : dz * 64 + voxels, :],
                w_ref[dz * 9 + k],
                preferred_element_type=F32,
            )
    sigma = jax.nn.sigmoid(pre)
    act_ref[...] = (pre * sigma).astype(BF)
    grad = (cot_ref[...].astype(F32) * sigma * (1.0 + pre * (1.0 - sigma))).astype(BF)
    gp_ref[...] = grad
    gb_ref[...] = jnp.sum(grad.astype(F32), axis=0, keepdims=True)
    half = channels // 2
    per_offset = half // ROWS
    lanes = 2 * channels // 128
    code = (where[8], where[9])

    def put(unit, value):
        leaf, inner = divmod(unit, leaf_units)
        colour = (leaf // (n_leaves // 4)) % 2
        gw_ref[(leaf ^ code[colour]) * leaf_units + inner] = value

    for dz in range(3):
        for k in range(9):
            o = dz * 9 + k
            part = lax.dot_general(
                patch[k, dz * 64 : dz * 64 + voxels, :],
                grad,
                (((0,), (0,)), ((), ())),
                preferred_element_type=F32,
            )
            wide = jnp.concatenate([part[:half], part[half:]], axis=1).astype(BF)
            for rows in range(per_offset):
                for lane in range(lanes):
                    put(
                        (o * per_offset + rows) * lanes + lane,
                        wide[rows * ROWS : (rows + 1) * ROWS, lane * 128 : (lane + 1) * 128],
                    )
    for unit in range(27 * per_offset * lanes, leaf_units * n_leaves):
        put(unit, jnp.zeros((ROWS, 128), BF))


def input_kernel(where, x_ref, recv_ref, w_ref, out_ref, rim, patch):
    voxels, channels = out_ref.shape
    gather_windows(where, x_ref, recv_ref, rim, patch)
    total = jnp.zeros((voxels, channels), F32)
    for dz in range(3):
        for k in range(9):
            total += lax.dot_general(
                patch[8 - k, (2 - dz) * 64 : (2 - dz) * 64 + voxels, :],
                w_ref[dz * 9 + k],
                (((1,), (1,)), ((), ())),
                preferred_element_type=F32,
            )
    out_ref[...] = total.astype(BF)


def unfold_kernel(leaf_units, n_leaves, where, near_ref, far_ref, out_ref, flat):
    code = (where[8], where[9])
    half_leaves = n_leaves // 2

    def spread(ref, first_leaf):
        for leaf in range(half_leaves):
            rel = first_leaf + leaf
            colour = (rel // (n_leaves // 4)) % 2
            base = (rel ^ code[colour]) * leaf_units

            def one(u, carry, base=base, leaf=leaf):
                row = pl.multiple_of((base + u) * ROWS, ROWS)
                flat[pl.ds(row, ROWS), :] = ref[leaf * leaf_units + u].astype(F32)
                return carry

            lax.fori_loop(0, leaf_units, one, 0, unroll=True)

    spread(near_ref, 0)
    spread(far_ref, half_leaves)
    pitch = flat.shape[0] // 32
    low = lax.broadcasted_iota(jnp.int32, (8, 128), 1) < 64

    def turned(x):
        return pltpu.roll(x, 64, 1)

    def block(base, group):
        rows = []
        for i in range(2):
            rows.append(
                [
                    flat[pl.ds(base + i + lane * ROWS + group * 8 * pitch, 8, stride=pitch), :]
                    for lane in range(3)
                ]
            )
        (a0, a1, a2), (b0, b1, b2) = rows
        rb0, rb1, ra1, ra2 = turned(b0), turned(b1), turned(a1), turned(a2)
        return (
            a0,
            jnp.where(low, a1, rb0),
            jnp.where(low, rb0, rb1),
            jnp.where(low, ra1, ra2),
            jnp.where(low, ra2, b1),
            b2,
        )

    count = out_ref.shape[0]
    span = out_ref.shape[1] // 2

    def pair(m, carry):
        i = m * 2
        base = (i // ROWS) * (3 * ROWS) + i % ROWS
        for top in range(0, count, 16):
            tiles = [block(base, top // 8), block(base, top // 8 + 1)]
            high = min(16, count - top)
            for n in range(6):
                both = jnp.concatenate([tiles[0][n], tiles[1][n]], axis=0).astype(BF)
                lane = pl.multiple_of((n // 3) * span + m * 384 + (n % 3) * 128, 128)
                out_ref[top : top + high, pl.ds(lane, 128)] = both[:high]
        return carry

    lax.fori_loop(0, span // 384, pair, 0, unroll=2)


def body(features, mask, owner, weight, bias, cotangent):
    channels = bias.shape[0]
    depth = features.shape[0]
    voxels = depth * 64
    regions = lax.axis_size("region")
    tiles = lax.axis_size("batch")
    bits = tiles.bit_length() - 1
    mine = lax.axis_index("batch")
    slab = lax.axis_index("region")

    columns = tiles // 4
    slots = jnp.arange(tiles, dtype=jnp.int32)
    places = jnp.sum(jnp.where(owner[:, None] == slots[None, :], slots[:, None], 0), axis=0)
    my_place = jnp.sum(jnp.where(slots == mine, places, 0))
    step_x = places % columns - my_place % columns
    step_y = places // columns - my_place // columns
    near = (jnp.abs(step_x) <= 1) & (jnp.abs(step_y) <= 1) & (slots != mine)
    wanted = jnp.where(
        step_y == 1, 0, jnp.where(step_y == -1, 1, jnp.where(step_x == 1, 2, 3))
    )
    send = (near[:, None] & (wanted[:, None] == jnp.arange(4)[None, :])).astype(BF)
    sources = [
        jnp.sum(jnp.where((step_x == x) & (step_y == y), slots - mine, 0)) + mine
        for x, y in STEPS
    ]

    orders = (tuple(range(1, bits)), tuple(range(bits - 1, 0, -1)))
    codes = []
    for order in orders:
        code = (mine & 1) << bits
        for n, bit in enumerate(order):
            code = code | (((mine >> bit) & 1) << (bits - 2 - n))
        codes.append(code)
    where = jnp.stack(sources + codes).astype(jnp.int32)
    n_leaves = 2 * tiles
    units = 27 * (channels // 2 // ROWS) * (2 * channels // 128)
    leaf_units = -(-units // n_leaves)

    def rims(planes):
        up = lax.ppermute(planes[-1:], "region", [(i, i + 1) for i in range(regions - 1)])
        down = lax.ppermute(planes[:1], "region", [(i + 1, i) for i in range(regions - 1)])
        return jnp.concatenate([up, planes, down], axis=0)

    def neighbours(planes):
        grid = planes.reshape(planes.shape[0], EDGE, EDGE, channels)
        lines = jnp.stack([grid[:, :, 7], grid[:, :, 0], grid[:, 7], grid[:, 0]])
        chosen = jnp.einsum("qk,kzxc->qzxc", send, lines, preferred_element_type=F32)
        return lax.all_to_all(chosen.astype(BF), "batch", 0, 0, tiled=True)

    scratch = [
        pltpu.VMEM((depth + 2, 10, 24, channels), F32),
        pltpu.VMEM((9, (depth + 2) * 64, channels), BF),
    ]
    keep = mask.reshape(depth, 64, 1).astype(BF)
    occupied = rims(features.reshape(depth, 64, channels) * keep)
    upstream = (cotangent.reshape(depth, 64, channels) * keep).reshape(voxels, channels)
    kernel = weight.reshape(27, channels, channels)

    act, grad, bias_terms, terms = pl.pallas_call(
        functools.partial(forward_kernel, leaf_units, n_leaves),
        out_shape=(
            jax.ShapeDtypeStruct((voxels, channels), BF),
            jax.ShapeDtypeStruct((voxels, channels), BF),
            jax.ShapeDtypeStruct((1, channels), F32),
            jax.ShapeDtypeStruct((n_leaves * leaf_units, ROWS, 128), BF),
        ),
        in_specs=[SMEM, VMEM, VMEM, VMEM, VMEM, VMEM],
        out_specs=(VMEM, VMEM, VMEM, VMEM),
        scratch_shapes=scratch,
        compiler_params=PARAMS,
        cost_estimate=pl.CostEstimate(
            flops=4 * 27 * voxels * channels * channels, bytes_accessed=6 << 20, transcendentals=voxels * channels
        ),
    )(where, occupied, neighbours(occupied), kernel, bias.reshape(1, channels), upstream)

    def halve(x, axis, count, flip):
        half = x.shape[0] // 2
        got = lax.ppermute(x[half:].astype(BF), axis, pairs(count, flip))
        return x[:half].astype(F32) + got.astype(F32)

    parts = halve(terms, "batch", tiles, 1)
    split = parts.shape[0] // 2
    colours = [parts[:split], parts[split:]]
    for step in range(bits - 1):
        colours = [halve(c, "batch", tiles, 1 << o[step]) for c, o in zip(colours, orders)]
    last = jnp.concatenate(colours, axis=0)
    share = -(-last.shape[0] // regions)
    spare = share * regions - last.shape[0]
    last = jnp.pad(last, ((0, spare), (0, 0), (0, 0))).reshape(regions, share, ROWS, 128)
    flips = sorted(range(1, regions), key=lambda f: -f)
    total = lax.dynamic_index_in_dim(last, slab, 0, False)
    for flip in flips:
        piece = lax.dynamic_index_in_dim(last, slab ^ flip, 0, False).astype(BF)
        total = total + lax.ppermute(piece, "region", pairs(regions, flip)).astype(F32)
    total = total.astype(BF)

    held = [total] + [
        lax.ppermute(total, "region", pairs(regions, flip)) for flip in range(1, regions)
    ]
    whole = jnp.zeros((regions, share, ROWS, 128), BF)
    for flip, block in enumerate(held):
        whole = lax.dynamic_update_index_in_dim(whole, block, slab ^ flip, 0)
    whole = whole.reshape(regions * share, ROWS, 128)
    colours = [whole[:leaf_units], whole[leaf_units : 2 * leaf_units]]
    for step in reversed(range(bits - 1)):
        colours = [
            jnp.concatenate([c, lax.ppermute(c, "batch", pairs(tiles, 1 << o[step]))], axis=0)
            for c, o in zip(colours, orders)
        ]
    own = jnp.concatenate(colours, axis=0)
    other = lax.ppermute(own, "batch", pairs(tiles, 1))
    kernel_grad = pl.pallas_call(
        functools.partial(unfold_kernel, leaf_units, n_leaves),
        out_shape=jax.ShapeDtypeStruct((27, channels * channels), BF),
        in_specs=[SMEM, VMEM, VMEM],
        out_specs=VMEM,
        scratch_shapes=[pltpu.VMEM((32 * units // 27 * ROWS, 128), F32)],
        compiler_params=PARAMS,
    )(where, own, other)

    total_bias = bias_terms
    for bit in range(bits):
        total_bias = total_bias + lax.ppermute(total_bias, "batch", pairs(tiles, 1 << bit))
    for bit in range(regions.bit_length() - 1):
        total_bias = total_bias + lax.ppermute(total_bias, "region", pairs(regions, 1 << bit))

    full_grad = rims(grad.reshape(depth, 64, channels))
    grad_input = pl.pallas_call(
        input_kernel,
        out_shape=jax.ShapeDtypeStruct((voxels, channels), BF),
        in_specs=[SMEM, VMEM, VMEM, VMEM],
        out_specs=VMEM,
        scratch_shapes=scratch,
        compiler_params=PARAMS,
        cost_estimate=pl.CostEstimate(
            flops=2 * 27 * voxels * channels * channels, bytes_accessed=3 << 20, transcendentals=0
        ),
    )(where, full_grad, neighbours(full_grad), kernel)

    def placed(rows):
        return (rows.reshape(depth, 64, channels) * keep).reshape(features.shape)

    return placed(act), placed(grad_input), kernel_grad, total_bias.reshape(channels)


def solution(mesh):
    split = P("region", "batch", None)
    return jax.shard_map(
        body,
        mesh=mesh,
        in_specs=(split, P("region", "batch"), P(), P(), P(), split),
        out_specs=(split, split, P(), P()),
        check_vma=False,
    )
```

profile of v0, /device:TPU:0, one launch (start us, length us, event | category | flops | bytes accessed | tf_op | source)
XLA Modules:
  0.0 142.0 jit_solution(12012801866636050034)
XLA Ops:
  0.6 1.2 reshape.112
  1.8 0.7 convert_element_type.65
  2.7 1.3 collective-permute-start.1
  4.0 5.6 %collective-permute-start = (bf16[1,64,192]{2,1,0:T(8,128)(2,1)S(1)}, bf16[1,64,192]{2,1,0:T(8,128)(2,1)S(1)}, u32[]{:S(2)}, u32[]{:S(2)}) collective-permute-start(bf16[1,64,192]{2,1,0:T(8,128)(2,1)S(1)} %get-tuple-element.49), channel_id=1, source_target_pairs={{0,8},{8,16},{16,24},{1,9},{9,17},{17,25},{2,10},{10,18},{18,26},{... | collective-permute-start | bytes 73736 | tf_op jit(solution)/shard_map/ppermute | solution.py:212
  9.5 0.7 select_reduce_fusion
  10.3 0.6 fusion.25
  13.5 0.8 fusion.29
  19.7 4.3 %reshape.114.w_ref = bf16[27,192,192]{2,1,0:T(8,128)(2,1)S(1)} reshape(bf16[27,36864]{1,0:T(8,128)(2,1)} %param.9) | data formatting | bytes 3981312 | tf_op jit(solution)/shard_map/reshape | solution.py:229
  24.4 0.8 fusion.39
  26.2 0.8 copy.93
  27.0 4.2 %all-to-all-start = ((bf16[8,10,8,192]{3,2,1,0:T(8,128)(2,1)}), bf16[8,10,8,192]{3,2,1,0:T(8,128)(2,1)S(1)}, u32[]{:S(2)}, u32[]{:S(2)}) async-start(bf16[8,10,8,192]{3,2,1,0:T(8,128)(2,1)} %copy.93), calls=%async_computation | async-start | bytes 655360 | tf_op jit(solution)/shard_map/all_to_all | solution.py:220
  31.2 0.9 broadcast_multiply_fusion.cot_ref
  32.0 6.8 %all-to-all-done.recv_ref = bf16[8,10,8,192]{3,2,1,0:T(8,128)(2,1)S(1)} async-done(((bf16[8,10,8,192]{3,2,1,0:T(8,128)(2,1)}), bf16[8,10,8,192]{3,2,1,0:T(8,128)(2,1)S(1)}, u32[]{:S(2)}, u32[]{:S(2)}) %all-to-all-start) | async-done | bytes 245792 | tf_op jit(solution)/shard_map/all_to_all | solution.py:220
  38.8 1.0 copy-done.1
  39.8 0.9 copy-done.2
  40.7 7.4 %shard_map.93 = (bf16[512,192]{1,0:T(8,128)(2,1)S(1)}, bf16[512,192]{1,0:T(8,128)(2,1)S(1)}, f32[1,192]{1,0:T(1,128)S(1)}, bf16[496,16,128]{2,1,0:T(8,128)(2,1)S(1)}) custom-call(s32[10]{0:T(128)S(1)} %stack.49.where, bf16[10,64,192]{2,1,0:T(8,128)(2,1)S(1)} %copy-done.1, bf16[8,10,8,192]{3,2,1,0:T(8,128)(2,1)S(1)} %all-to-all-done.recv_ref, ...), custom_call_target="tpu_custom_call" | custom-call | flops 2038431744 | bytes 6291456 | tf_op jit(solution)/shard_map/pallas_call | solution.py:231
  48.4 2.6 %collective-permute-done.4 = bf16[248,16,128]{2,1,0:T(8,128)(2,1)S(1)} collective-permute-done((bf16[248,16,128]{2,1,0:T(8,128)(2,1)S(1)}, bf16[248,16,128]{2,1,0:T(8,128)(2,1)S(1)}, u32[]{:S(2)}, u32[]{:S(2)}) %collective-permute-start.4) | collective-permute-done | bytes 1015840 | tf_op jit(solution)/shard_map/ppermute | solution.py:250
  51.0 1.6 %fusion.40 = (bf16[248,16,128]{2,1,0:T(8,128)(2,1)S(1)}, f32[248,16,128]{2,1,0:T(8,128)}) fusion(bf16[248,16,128]{2,1,0:T(8,128)(2,1)S(1)} %collective-permute-done.4, bf16[496,16,128]{2,1,0:T(8,128)(2,1)S(1)} %get-tuple-element.10), kind=kLoop, calls=%fused_computation.106 | loop fusion | flops 2031616 | bytes 5079040 | tf_op jit(solution)/shard_map/convert.3
  52.5 0.8 fusion.44
  54.5 1.3 collective-permute-start.3
  55.8 4.7 %collective-permute-start.2 = (bf16[1,64,192]{2,1,0:T(8,128)(2,1)S(1)}, bf16[1,64,192]{2,1,0:T(8,128)(2,1)S(1)}, u32[]{:S(2)}, u32[]{:S(2)}) collective-permute-start(bf16[1,64,192]{2,1,0:T(8,128)(2,1)S(1)} %get-tuple-element.47), channel_id=1, source_target_pairs={{0,8},{8,16},{16,24},{1,9},{9,17},{17,25},{2,10},{10,18},{18,26},{... | collective-permute-start | bytes 73736 | tf_op jit(solution)/shard_map/ppermute | solution.py:212
  60.5 1.2 collective-permute-done.5
  62.1 1.4 slice_add_fusion.1
  63.6 1.5 %collective-permute-start.8 = (bf16[31,16,128]{2,1,0:T(8,128)(2,1)S(1)}, bf16[31,16,128]{2,1,0:T(8,128)(2,1)S(1)}, u32[]{:S(2)}, u32[]{:S(2)}) collective-permute-start(bf16[31,16,128]{2,1,0:T(8,128)(2,1)S(1)} %slice.151), channel_id=1, source_target_pairs={{0,2},{1,3},{2,0},{3,1},{4,6},{5,7},{6,4},{7,5},{8,10},{9,11},{10,... | collective-permute-start | bytes 380936 | tf_op jit(solution)/shard_map/ppermute | solution.py:250
  65.8 2.8 %collective-permute-done.8 = bf16[31,16,128]{2,1,0:T(8,128)(2,1)S(1)} collective-permute-done((bf16[31,16,128]{2,1,0:T(8,128)(2,1)S(1)}, bf16[31,16,128]{2,1,0:T(8,128)(2,1)S(1)}, u32[]{:S(2)}, u32[]{:S(2)}) %collective-permute-start.8) | collective-permute-done | bytes 127008 | tf_op jit(solution)/shard_map/ppermute | solution.py:250
  68.6 1.5 %collective-permute-done.6 = bf16[31,16,128]{2,1,0:T(8,128)(2,1)S(1)} collective-permute-done((bf16[31,16,128]{2,1,0:T(8,128)(2,1)S(1)}, bf16[31,16,128]{2,1,0:T(8,128)(2,1)S(1)}, u32[]{:S(2)}, u32[]{:S(2)}) %collective-permute-start.6) | collective-permute-done | bytes 127008 | tf_op jit(solution)/shard_map/ppermute | solution.py:250
  70.2 1.6 %collective-permute-start.11 = (bf16[16,16,128]{2,1,0:T(8,128)(2,1)S(1)}, bf16[16,16,128]{2,1,0:T(8,128)(2,1)S(1)}, u32[]{:S(2)}, u32[]{:S(2)}) collective-permute-start(bf16[16,16,128]{2,1,0:T(8,128)(2,1)S(1)} %get-tuple-element.32), channel_id=1, source_target_pairs={{0,8},{8,0},{16,24},{24,16},{1,9},{9,1},{17,25},{25,17},{2,10},{10... | collective-permute-start | bytes 196616 | tf_op jit(solution)/shard_map/ppermute | solution.py:266
  71.9 1.1 collective-permute-start.10
  73.0 1.7 %collective-permute-start.9 = (bf16[16,16,128]{2,1,0:T(8,128)(2,1)S(1)}, bf16[16,16,128]{2,1,0:T(8,128)(2,1)S(1)}, u32[]{:S(2)}, u32[]{:S(2)}) collective-permute-start(bf16[16,16,128]{2,1,0:T(8,128)(2,1)S(1)} %get-tuple-element.31), channel_id=1, source_target_pairs={{0,24},{8,16},{16,8},{24,0},{1,25},{9,17},{17,9},{25,1},{2,26},{10... | collective-permute-start | bytes 196616 | tf_op jit(solution)/shard_map/ppermute | solution.py:266
  74.7 3.0 %collective-permute-done.10 = bf16[16,16,128]{2,1,0:T(8,128)(2,1)S(1)} collective-permute-done((bf16[16,16,128]{2,1,0:T(8,128)(2,1)S(1)}, bf16[16,16,128]{2,1,0:T(8,128)(2,1)S(1)}, u32[]{:S(2)}, u32[]{:S(2)}) %collective-permute-start.10) | collective-permute-done | bytes 65568 | tf_op jit(solution)/shard_map/ppermute | solution.py:266
  77.7 1.4 %collective-permute-done.9 = bf16[16,16,128]{2,1,0:T(8,128)(2,1)S(1)} collective-permute-done((bf16[16,16,128]{2,1,0:T(8,128)(2,1)S(1)}, bf16[16,16,128]{2,1,0:T(8,128)(2,1)S(1)}, u32[]{:S(2)}, u32[]{:S(2)}) %collective-permute-start.9) | collective-permute-done | bytes 65568 | tf_op jit(solution)/shard_map/ppermute | solution.py:266
  79.3 0.8 collective-permute-start.12
  80.1 1.7 %collective-permute-start.13 = (bf16[16,16,128]{2,1,0:T(8,128)(2,1)S(1)}, bf16[16,16,128]{2,1,0:T(8,128)(2,1)S(1)}, u32[]{:S(2)}, u32[]{:S(2)}) collective-permute-start(bf16[16,16,128]{2,1,0:T(8,128)(2,1)S(1)} %get-tuple-element.21), channel_id=1, source_target_pairs={{0,16},{8,24},{16,0},{24,8},{1,17},{9,25},{17,1},{25,9},{2,18},{10... | collective-permute-start | bytes 196616 | tf_op jit(solution)/shard_map/ppermute | solution.py:270
  81.7 2.1 %collective-permute-start.14 = (bf16[16,16,128]{2,1,0:T(8,128)(2,1)S(1)}, bf16[16,16,128]{2,1,0:T(8,128)(2,1)S(1)}, u32[]{:S(2)}, u32[]{:S(2)}) collective-permute-start(bf16[16,16,128]{2,1,0:T(8,128)(2,1)S(1)} %get-tuple-element.21), channel_id=1, source_target_pairs={{0,24},{8,16},{16,8},{24,0},{1,25},{9,17},{17,9},{25,1},{2,26},{10... | collective-permute-start | bytes 196616 | tf_op jit(solution)/shard_map/ppermute | solution.py:270
  83.8 1.5 %collective-permute-done.13 = bf16[16,16,128]{2,1,0:T(8,128)(2,1)S(1)} collective-permute-done((bf16[16,16,128]{2,1,0:T(8,128)(2,1)S(1)}, bf16[16,16,128]{2,1,0:T(8,128)(2,1)S(1)}, u32[]{:S(2)}, u32[]{:S(2)}) %collective-permute-start.13) | collective-permute-done | bytes 65568 | tf_op jit(solution)/shard_map/ppermute | solution.py:270
  85.3 2.5 %collective-permute-done.14 = bf16[16,16,128]{2,1,0:T(8,128)(2,1)S(1)} collective-permute-done((bf16[16,16,128]{2,1,0:T(8,128)(2,1)S(1)}, bf16[16,16,128]{2,1,0:T(8,128)(2,1)S(1)}, u32[]{:S(2)}, u32[]{:S(2)}) %collective-permute-start.14) | collective-permute-done | bytes 65568 | tf_op jit(solution)/shard_map/ppermute | solution.py:270
  87.8 0.7 fusion.47
  89.2 0.9 collective-permute-start.17
  90.1 4.4 %collective-permute-done.15 = bf16[31,16,128]{2,1,0:T(8,128)(2,1)S(1)} collective-permute-done((bf16[31,16,128]{2,1,0:T(8,128)(2,1)S(1)}, bf16[31,16,128]{2,1,0:T(8,128)(2,1)S(1)}, u32[]{:S(2)}, u32[]{:S(2)}) %collective-permute-start.15) | collective-permute-done | bytes 127008 | tf_op jit(solution)/shard_map/ppermute | solution.py:279
  94.6 0.8 collective-permute-start.16
  95.8 1.0 collective-permute-start.18
  96.8 0.7 constant_dynamic-update-slice_fusion.4
  97.4 3.5 %collective-permute-done.16 = bf16[62,16,128]{2,1,0:T(8,128)(2,1)S(1)} collective-permute-done((bf16[62,16,128]{2,1,0:T(8,128)(2,1)S(1)}, bf16[62,16,128]{2,1,0:T(8,128)(2,1)S(1)}, u32[]{:S(2)}, u32[]{:S(2)}) %collective-permute-start.16) | collective-permute-done | bytes 253984 | tf_op jit(solution)/shard_map/ppermute | solution.py:279
  100.9 0.7 constant_dynamic-update-slice_fusion.3
  101.6 0.7 constant_dynamic-update-slice_fusion.2
  102.3 0.7 constant_dynamic-update-slice_fusion.1
  103.0 0.7 constant_dynamic-update-slice_fusion.near_ref
  104.3 0.8 copy.92
  105.1 3.4 %all-to-all-start.1 = ((bf16[8,10,8,192]{3,2,1,0:T(8,128)(2,1)}), bf16[8,10,8,192]{3,2,1,0:T(8,128)(2,1)S(1)}, u32[]{:S(2)}, u32[]{:S(2)}) async-start(bf16[8,10,8,192]{3,2,1,0:T(8,128)(2,1)} %copy.92), calls=%async_computation.1 | async-start | bytes 655360 | tf_op jit(solution)/shard_map/all_to_all | solution.py:220
  109.0 0.8 collective-permute-done.20
  109.9 1.7 %collective-permute-start.21 = (f32[1,192]{1,0:T(1,128)S(1)}, f32[1,192]{1,0:T(1,128)S(1)}, u32[]{:S(2)}, u32[]{:S(2)}) collective-permute-start(f32[1,192]{1,0:T(1,128)S(1)} %add.131), channel_id=1, source_target_pairs={{0,2},{1,3},{2,0},{3,1},{4,6},{5,7},{6,4},{7,5},{8,10},{9,11},{10,... | collective-permute-start | bytes 2312 | tf_op jit(solution)/shard_map/ppermute | solution.py:295
  111.6 3.6 %collective-permute-done.21 = f32[1,192]{1,0:T(1,128)S(1)} collective-permute-done((f32[1,192]{1,0:T(1,128)S(1)}, f32[1,192]{1,0:T(1,128)S(1)}, u32[]{:S(2)}, u32[]{:S(2)}) %collective-permute-start.21) | collective-permute-done | bytes 800 | tf_op jit(solution)/shard_map/ppermute | solution.py:295
  115.2 1.5 %collective-permute-start.22 = (f32[1,192]{1,0:T(1,128)S(1)}, f32[1,192]{1,0:T(1,128)S(1)}, u32[]{:S(2)}, u32[]{:S(2)}) collective-permute-start(f32[1,192]{1,0:T(1,128)S(1)} %add.132), channel_id=1, source_target_pairs={{0,4},{1,5},{2,6},{3,7},{4,0},{5,1},{6,2},{7,3},{8,12},{9,13},{10,... | collective-permute-start | bytes 2312 | tf_op jit(solution)/shard_map/ppermute | solution.py:295
  116.7 2.1 %collective-permute-done.22 = f32[1,192]{1,0:T(1,128)S(1)} collective-permute-done((f32[1,192]{1,0:T(1,128)S(1)}, f32[1,192]{1,0:T(1,128)S(1)}, u32[]{:S(2)}, u32[]{:S(2)}) %collective-permute-start.22) | collective-permute-done | bytes 800 | tf_op jit(solution)/shard_map/ppermute | solution.py:295
  118.7 3.6 %collective-permute-done.23 = f32[1,192]{1,0:T(1,128)S(1)} collective-permute-done((f32[1,192]{1,0:T(1,128)S(1)}, f32[1,192]{1,0:T(1,128)S(1)}, u32[]{:S(2)}, u32[]{:S(2)}) %collective-permute-start.23) | collective-permute-done | bytes 800 | tf_op jit(solution)/shard_map/ppermute | solution.py:297
  122.3 0.7 collective-permute-start.24
  123.0 0.8 mul.35
  123.8 1.9 %mul.40 = bf16[8,8,1536]{2,1,0:T(8,128)(2,1)} reshape(bf16[8,64,192]{2,1,0:T(8,128)(2,1)} %mul.35) | data formatting | bytes 393216 | tf_op jit(solution)/shard_map/mul | solution.py:227
  125.7 0.9 reshape.117
  127.3 1.5 %pad_maximum_fusion.1.x_ref = bf16[10,64,192]{2,1,0:T(8,128)(2,1)} fusion(bf16[1,64,192]{2,1,0:T(8,128)(2,1)S(1)} %collective-permute-done.3, bf16[8,64,192]{2,1,0:T(8,128)(2,1)S(1)} %bitcast.76, bf16[1,64,192]{2,1,0:T(8,128)(2,1)} %copy-done.6), kind=kLoop, calls=%fused_computation.8 | loop fusion | flops 245760 | bytes 491520 | tf_op jit(solution)/shard_map/concatenate | solution.py:214
  128.9 1.0 copy-done
  129.9 3.0 %shard_map.94 = bf16[512,192]{1,0:T(8,128)(2,1)S(1)} custom-call(s32[10]{0:T(128)S(1)} %stack.49.where, bf16[10,64,192]{2,1,0:T(8,128)(2,1)S(1)} %copy-done, bf16[8,10,8,192]{3,2,1,0:T(8,128)(2,1)S(1)} %all-to-all-done.1.recv_ref, bf16[27,192,192]{2,1,0:T(8,128)(2,1)S(1)} %reshape.114.w_ref), custom_call_target="tpu_custom_call" | custom-call | flops 1019215872 | bytes 3145728 | tf_op jit(solution)/shard_map/pallas_call | solution.py:300
  133.1 1.7 %fusion.49 = (bf16[8,8,1536]{2,1,0:T(8,128)(2,1)}, bf16[8,8,1536]{2,1,0:T(8,128)(2,1)}) fusion(bf16[8,8,1536]{2,1,0:T(8,128)(2,1)S(1)} %reshape.119, bf16[8,8,1536]{2,1,0:T(8,128)(2,1)S(1)} %copy-done.4, bf16[8,8,1536]{2,1,0:T(8,128)(2,1)} %reshape.117), kind=kLoop, calls=%fused_computation.112 | loop fusion | flops 196608 | bytes 983040 | tf_op jit(solution)/shard_map/mul | solution.py:313
  134.9 7.1 %shard_map.95 = bf16[27,36864]{1,0:T(8,128)(2,1)} custom-call(s32[10]{0:T(128)S(1)} %stack.49.where, bf16[248,16,128]{2,1,0:T(8,128)(2,1)} %constant_dynamic-update-slice_fusion.near_ref, bf16[248,16,128]{2,1,0:T(8,128)(2,1)} %collective-permute-done.19.far_ref), custom_call_target="tpu_custom_call" | custom-call | tf_op jit(solution)/shard_map/pallas_call | solution.py:284
  (82 shorter events, 7.4 us)
Async XLA Ops:
  2.7 21.7 %collective-permute-start.1 = (bf16[1,64,192]{2,1,0:T(8,128)(2,1)S(1)}, bf16[1,64,192]{2,1,0:T(8,128)(2,1)S(1)}, u32[]{:S(2)}, u32[]{:S(2)}) collective-permute-start(bf16[1,64,192]{2,1,0:T(8,128)(2,1)S(1)} %get-tuple-element.50), channel_id=1, source_target_pairs={{8,0},{16,8},{24,16},{9,1},{17,9},{25,17},{10,2},{18,10},{26,18},{... | collective-permute-start | bytes 73736 | tf_op jit(solution)/shard_map/ppermute | solution.py:213
  4.0 20.4 %collective-permute-start = (bf16[1,64,192]{2,1,0:T(8,128)(2,1)S(1)}, bf16[1,64,192]{2,1,0:T(8,128)(2,1)S(1)}, u32[]{:S(2)}, u32[]{:S(2)}) collective-permute-start(bf16[1,64,192]{2,1,0:T(8,128)(2,1)S(1)} %get-tuple-element.49), channel_id=1, source_target_pairs={{0,8},{8,16},{16,24},{1,9},{9,17},{17,25},{2,10},{10,18},{18,26},{... | collective-permute-start | bytes 73736 | tf_op jit(solution)/shard_map/ppermute | solution.py:212
  14.4 11.3 %copy-start.7 = (s32[8]{0:T(128)}, s32[8]{0:T(128)S(1)}, u32[]{:S(2)}) copy-start(s32[8]{0:T(128)S(1)} %get-tuple-element.53) | copy-start | bytes 100
  19.6 4.4 %copy-start.5 = (bf16[8,8,1536]{2,1,0:T(8,128)(2,1)S(1)}, bf16[8,8,1536]{2,1,0:T(8,128)(2,1)}, u32[]{:S(2)}) copy-start(bf16[8,8,1536]{2,1,0:T(8,128)(2,1)} %param.11) | copy-start | bytes 589828
  25.2 13.6 %copy-start.3 = (f32[192]{0:T(256)S(1)}, f32[192]{0:T(256)}, u32[]{:S(2)}) copy-start(f32[192]{0:T(256)} %param.10) | copy-start | bytes 2308
  27.0 11.8 %all-to-all-start = ((bf16[8,10,8,192]{3,2,1,0:T(8,128)(2,1)}), bf16[8,10,8,192]{3,2,1,0:T(8,128)(2,1)S(1)}, u32[]{:S(2)}, u32[]{:S(2)}) async-start(bf16[8,10,8,192]{3,2,1,0:T(8,128)(2,1)} %copy.93), calls=%async_computation | async-start | bytes 655360 | tf_op jit(solution)/shard_map/all_to_all | solution.py:220
  38.8 1.0 copy-start.1
  39.8 0.9 copy-start.2
  48.3 2.7 %collective-permute-start.4 = (bf16[248,16,128]{2,1,0:T(8,128)(2,1)S(1)}, bf16[248,16,128]{2,1,0:T(8,128)(2,1)S(1)}, u32[]{:S(2)}, u32[]{:S(2)}) collective-permute-start(bf16[248,16,128]{2,1,0:T(8,128)(2,1)S(1)} %slice.103), channel_id=1, source_target_pairs={{0,1},{1,0},{2,3},{3,2},{4,5},{5,4},{6,7},{7,6},{8,9},{9,8},{10,11... | collective-permute-start | bytes 3047432 | tf_op jit(solution)/shard_map/ppermute | solution.py:250
  53.4 8.4 %collective-permute-start.5 = (bf16[62,16,128]{2,1,0:T(8,128)(2,1)}, bf16[62,16,128]{2,1,0:T(8,128)(2,1)S(1)}, u32[]{:S(2)}, u32[]{:S(2)}) collective-permute-start(bf16[62,16,128]{2,1,0:T(8,128)(2,1)} %get-tuple-element.29), channel_id=1, source_target_pairs={{0,2},{1,3},{2,0},{3,1},{4,6},{5,7},{6,4},{7,5},{8,10},{9,11},{10,... | collective-permute-start | bytes 761864 | tf_op jit(solution)/shard_map/ppermute | solution.py:250
  53.9 8.2 %collective-permute-start.7 = (bf16[62,16,128]{2,1,0:T(8,128)(2,1)}, bf16[62,16,128]{2,1,0:T(8,128)(2,1)}, u32[]{:S(2)}, u32[]{:S(2)}) collective-permute-start(bf16[62,16,128]{2,1,0:T(8,128)(2,1)} %get-tuple-element.30), channel_id=1, source_target_pairs={{0,4},{1,5},{2,6},{3,7},{4,0},{5,1},{6,2},{7,3},{8,12},{9,13},{10,... | collective-permute-start | bytes 761864 | tf_op jit(solution)/shard_map/ppermute | solution.py:250
  54.5 25.6 %collective-permute-start.3 = (bf16[1,64,192]{2,1,0:T(8,128)(2,1)S(1)}, bf16[1,64,192]{2,1,0:T(8,128)(2,1)S(1)}, u32[]{:S(2)}, u32[]{:S(2)}) collective-permute-start(bf16[1,64,192]{2,1,0:T(8,128)(2,1)S(1)} %get-tuple-element.48), channel_id=1, source_target_pairs={{8,0},{16,8},{24,16},{9,1},{17,9},{25,17},{10,2},{18,10},{26,18},{... | collective-permute-start | bytes 73736 | tf_op jit(solution)/shard_map/ppermute | solution.py:213
  55.8 9.3 %collective-permute-start.2 = (bf16[1,64,192]{2,1,0:T(8,128)(2,1)S(1)}, bf16[1,64,192]{2,1,0:T(8,128)(2,1)S(1)}, u32[]{:S(2)}, u32[]{:S(2)}) collective-permute-start(bf16[1,64,192]{2,1,0:T(8,128)(2,1)S(1)} %get-tuple-element.47), channel_id=1, source_target_pairs={{0,8},{8,16},{16,24},{1,9},{9,17},{17,25},{2,10},{10,18},{18,26},{... | collective-permute-start | bytes 73736 | tf_op jit(solution)/shard_map/ppermute | solution.py:212
  63.6 5.0 %collective-permute-start.8 = (bf16[31,16,128]{2,1,0:T(8,128)(2,1)S(1)}, bf16[31,16,128]{2,1,0:T(8,128)(2,1)S(1)}, u32[]{:S(2)}, u32[]{:S(2)}) collective-permute-start(bf16[31,16,128]{2,1,0:T(8,128)(2,1)S(1)} %slice.151), channel_id=1, source_target_pairs={{0,2},{1,3},{2,0},{3,1},{4,6},{5,7},{6,4},{7,5},{8,10},{9,11},{10,... | collective-permute-start | bytes 380936 | tf_op jit(solution)/shard_map/ppermute | solution.py:250
  65.1 14.2 %copy-start.6 = (bf16[1,64,192]{2,1,0:T(8,128)(2,1)}, bf16[1,64,192]{2,1,0:T(8,128)(2,1)S(1)}, u32[]{:S(2)}) copy-start(bf16[1,64,192]{2,1,0:T(8,128)(2,1)S(1)} %collective-permute-done.2) | copy-start | bytes 73732
  65.1 5.0 %collective-permute-start.6 = (bf16[31,16,128]{2,1,0:T(8,128)(2,1)S(1)}, bf16[31,16,128]{2,1,0:T(8,128)(2,1)S(1)}, u32[]{:S(2)}, u32[]{:S(2)}) collective-permute-start(bf16[31,16,128]{2,1,0:T(8,128)(2,1)S(1)} %slice.152), channel_id=1, source_target_pairs={{0,4},{1,5},{2,6},{3,7},{4,0},{5,1},{6,2},{7,3},{8,12},{9,13},{10,... | collective-permute-start | bytes 380936 | tf_op jit(solution)/shard_map/ppermute | solution.py:250
  70.2 4.5 %collective-permute-start.11 = (bf16[16,16,128]{2,1,0:T(8,128)(2,1)S(1)}, bf16[16,16,128]{2,1,0:T(8,128)(2,1)S(1)}, u32[]{:S(2)}, u32[]{:S(2)}) collective-permute-start(bf16[16,16,128]{2,1,0:T(8,128)(2,1)S(1)} %get-tuple-element.32), channel_id=1, source_target_pairs={{0,8},{8,0},{16,24},{24,16},{1,9},{9,1},{17,25},{25,17},{2,10},{10... | collective-permute-start | bytes 196616 | tf_op jit(solution)/shard_map/ppermute | solution.py:266
  71.9 5.9 %collective-permute-start.10 = (bf16[16,16,128]{2,1,0:T(8,128)(2,1)S(1)}, bf16[16,16,128]{2,1,0:T(8,128)(2,1)S(1)}, u32[]{:S(2)}, u32[]{:S(2)}) collective-permute-start(bf16[16,16,128]{2,1,0:T(8,128)(2,1)S(1)} %get-tuple-element.33), channel_id=1, source_target_pairs={{0,16},{8,24},{16,0},{24,8},{1,17},{9,25},{17,1},{25,9},{2,18},{10... | collective-permute-start | bytes 196616 | tf_op jit(solution)/shard_map/ppermute | solution.py:266
  73.0 6.2 %collective-permute-start.9 = (bf16[16,16,128]{2,1,0:T(8,128)(2,1)S(1)}, bf16[16,16,128]{2,1,0:T(8,128)(2,1)S(1)}, u32[]{:S(2)}, u32[]{:S(2)}) collective-permute-start(bf16[16,16,128]{2,1,0:T(8,128)(2,1)S(1)} %get-tuple-element.31), channel_id=1, source_target_pairs={{0,24},{8,16},{16,8},{24,0},{1,25},{9,17},{17,9},{25,1},{2,26},{10... | collective-permute-start | bytes 196616 | tf_op jit(solution)/shard_map/ppermute | solution.py:266
  79.3 4.5 %collective-permute-start.12 = (bf16[16,16,128]{2,1,0:T(8,128)(2,1)S(1)}, bf16[16,16,128]{2,1,0:T(8,128)(2,1)S(1)}, u32[]{:S(2)}, u32[]{:S(2)}) collective-permute-start(bf16[16,16,128]{2,1,0:T(8,128)(2,1)S(1)} %get-tuple-element.21), channel_id=1, source_target_pairs={{0,8},{8,0},{16,24},{24,16},{1,9},{9,1},{17,25},{25,17},{2,10},{10... | collective-permute-start | bytes 196616 | tf_op jit(solution)/shard_map/ppermute | solution.py:270
  80.1 5.2 %collective-permute-start.13 = (bf16[16,16,128]{2,1,0:T(8,128)(2,1)S(1)}, bf16[16,16,128]{2,1,0:T(8,128)(2,1)S(1)}, u32[]{:S(2)}, u32[]{:S(2)}) collective-permute-start(bf16[16,16,128]{2,1,0:T(8,128)(2,1)S(1)} %get-tuple-element.21), channel_id=1, source_target_pairs={{0,16},{8,24},{16,0},{24,8},{1,17},{9,25},{17,1},{25,9},{2,18},{10... | collective-permute-start | bytes 196616 | tf_op jit(solution)/shard_map/ppermute | solution.py:270
  81.7 6.1 %collective-permute-start.14 = (bf16[16,16,128]{2,1,0:T(8,128)(2,1)S(1)}, bf16[16,16,128]{2,1,0:T(8,128)(2,1)S(1)}, u32[]{:S(2)}, u32[]{:S(2)}) collective-permute-start(bf16[16,16,128]{2,1,0:T(8,128)(2,1)S(1)} %get-tuple-element.21), channel_id=1, source_target_pairs={{0,24},{8,16},{16,8},{24,0},{1,25},{9,17},{17,9},{25,1},{2,26},{10... | collective-permute-start | bytes 196616 | tf_op jit(solution)/shard_map/ppermute | solution.py:270
  88.5 15.2 %copy-start.8 = (s32[8]{0:T(128)S(1)}, s32[8]{0:T(128)}, u32[]{:S(2)}) copy-start(s32[8]{0:T(128)} %copy-done.7) | copy-start | bytes 100
  88.5 6.0 %collective-permute-start.15 = (bf16[31,16,128]{2,1,0:T(8,128)(2,1)S(1)}, bf16[31,16,128]{2,1,0:T(8,128)(2,1)S(1)}, u32[]{:S(2)}, u32[]{:S(2)}) collective-permute-start(bf16[31,16,128]{2,1,0:T(8,128)(2,1)S(1)} %get-tuple-element.46), channel_id=1, source_target_pairs={{0,4},{1,5},{2,6},{3,7},{4,0},{5,1},{6,2},{7,3},{8,12},{9,13},{10,... | collective-permute-start | bytes 380936 | tf_op jit(solution)/shard_map/ppermute | solution.py:279
  89.2 6.5 %collective-permute-start.17 = (bf16[31,16,128]{2,1,0:T(8,128)(2,1)S(1)}, bf16[31,16,128]{2,1,0:T(8,128)(2,1)S(1)}, u32[]{:S(2)}, u32[]{:S(2)}) collective-permute-start(bf16[31,16,128]{2,1,0:T(8,128)(2,1)S(1)} %get-tuple-element.44), channel_id=1, source_target_pairs={{0,2},{1,3},{2,0},{3,1},{4,6},{5,7},{6,4},{7,5},{8,10},{9,11},{10,... | collective-permute-start | bytes 380936 | tf_op jit(solution)/shard_map/ppermute | solution.py:279
  94.6 6.3 %collective-permute-start.16 = (bf16[62,16,128]{2,1,0:T(8,128)(2,1)S(1)}, bf16[62,16,128]{2,1,0:T(8,128)(2,1)S(1)}, u32[]{:S(2)}, u32[]{:S(2)}) collective-permute-start(bf16[62,16,128]{2,1,0:T(8,128)(2,1)S(1)} %pad_maximum_fusion.2), channel_id=1, source_target_pairs={{0,2},{1,3},{2,0},{3,1},{4,6},{5,7},{6,4},{7,5},{8,10},{9,11},{10,... | collective-permute-start | bytes 761864 | tf_op jit(solution)/shard_map/ppermute | solution.py:279
  95.8 7.2 %collective-permute-start.18 = (bf16[62,16,128]{2,1,0:T(8,128)(2,1)S(1)}, bf16[62,16,128]{2,1,0:T(8,128)(2,1)S(1)}, u32[]{:S(2)}, u32[]{:S(2)}) collective-permute-start(bf16[62,16,128]{2,1,0:T(8,128)(2,1)S(1)} %pad_maximum_fusion.3), channel_id=1, source_target_pairs={{0,4},{1,5},{2,6},{3,7},{4,0},{5,1},{6,2},{7,3},{8,12},{9,13},{10,... | collective-permute-start | bytes 761864 | tf_op jit(solution)/shard_map/ppermute | solution.py:279
  103.7 31.2 %collective-permute-start.19 = (bf16[248,16,128]{2,1,0:T(8,128)(2,1)}, bf16[248,16,128]{2,1,0:T(8,128)(2,1)}, u32[]{:S(2)}, u32[]{:S(2)}) collective-permute-start(bf16[248,16,128]{2,1,0:T(8,128)(2,1)} %constant_dynamic-update-slice_fusion.near_ref), channel_id=1, source_target_pairs={{0,1},{1,0},{2,3},{3,2},{4,5},{5,4},{6,7},{7,6},{8,9},{9,8},{10,11... | collective-permute-start | bytes 3047432 | tf_op jit(solution)/shard_map/ppermute | solution.py:283
  105.1 23.8 %all-to-all-start.1 = ((bf16[8,10,8,192]{3,2,1,0:T(8,128)(2,1)}), bf16[8,10,8,192]{3,2,1,0:T(8,128)(2,1)S(1)}, u32[]{:S(2)}, u32[]{:S(2)}) async-start(bf16[8,10,8,192]{3,2,1,0:T(8,128)(2,1)} %copy.92), calls=%async_computation.1 | async-start | bytes 655360 | tf_op jit(solution)/shard_map/all_to_all | solution.py:220
  108.5 1.3 collective-permute-start.20
  109.9 5.3 %collective-permute-start.21 = (f32[1,192]{1,0:T(1,128)S(1)}, f32[1,192]{1,0:T(1,128)S(1)}, u32[]{:S(2)}, u32[]{:S(2)}) collective-permute-start(f32[1,192]{1,0:T(1,128)S(1)} %add.131), channel_id=1, source_target_pairs={{0,2},{1,3},{2,0},{3,1},{4,6},{5,7},{6,4},{7,5},{8,10},{9,11},{10,... | collective-permute-start | bytes 2312 | tf_op jit(solution)/shard_map/ppermute | solution.py:295
  115.2 3.6 %collective-permute-start.22 = (f32[1,192]{1,0:T(1,128)S(1)}, f32[1,192]{1,0:T(1,128)S(1)}, u32[]{:S(2)}, u32[]{:S(2)}) collective-permute-start(f32[1,192]{1,0:T(1,128)S(1)} %add.132), channel_id=1, source_target_pairs={{0,4},{1,5},{2,6},{3,7},{4,0},{5,1},{6,2},{7,3},{8,12},{9,13},{10,... | collective-permute-start | bytes 2312 | tf_op jit(solution)/shard_map/ppermute | solution.py:295
  118.7 3.6 %collective-permute-start.23 = (f32[1,192]{1,0:T(1,128)S(1)}, f32[1,192]{1,0:T(1,128)S(1)}, u32[]{:S(2)}, u32[]{:S(2)}) collective-permute-start(f32[1,192]{1,0:T(1,128)S(1)} %add.133), channel_id=1, source_target_pairs={{0,8},{8,0},{16,24},{24,16},{1,9},{9,1},{17,25},{25,17},{2,10},{10... | collective-permute-start | bytes 2312 | tf_op jit(solution)/shard_map/ppermute | solution.py:297
  122.3 4.5 %collective-permute-start.24 = (f32[1,192]{1,0:T(1,128)S(1)}, f32[1,192]{1,0:T(1,128)S(1)}, u32[]{:S(2)}, u32[]{:S(2)}) collective-permute-start(f32[1,192]{1,0:T(1,128)S(1)} %add.134), channel_id=1, source_target_pairs={{0,16},{8,24},{16,0},{24,8},{1,17},{9,25},{17,1},{25,9},{2,18},{10... | collective-permute-start | bytes 2312 | tf_op jit(solution)/shard_map/ppermute | solution.py:297
  128.9 1.0 copy-start
  129.9 3.3 %copy-start.4 = (bf16[8,8,1536]{2,1,0:T(8,128)(2,1)S(1)}, bf16[8,8,1536]{2,1,0:T(8,128)(2,1)}, u32[]{:S(2)}) copy-start(bf16[8,8,1536]{2,1,0:T(8,128)(2,1)} %mul.40) | copy-start | bytes 589828
where the time goes:
time: 143 us; the launch traced here: 142 us
  waiting for transfers between devices  41.9 us (29%)
  starting transfers between devices  40.5 us (28%)
  local copies, waits for them, and re-layouts  20.4 us (14%)
  Pallas kernels  17.5 us (12%)
  other arithmetic  11.7 us (8%)
  between operations  8.86 us (6%)
    ppermute x2, starting transfers between devices, rims(): lax.ppermute(planes[-1:], 'region', [(i, i + 1) for i in range(regions -...  10.3 us
    ppermute x5, waiting for transfers between devices, halve(): got = lax.ppermute(x[half:].astype(BF), axis, pairs(count, flip))  8.54 us
    ppermute x4, waiting for transfers between devices, body(): lax.ppermute(c, 'batch', pairs(tiles, 1 << o[step]))  7.94 us
    all_to_all x2, starting transfers between devices, neighbours(): return lax.all_to_all(chosen.astype(BF), 'batch', 0, 0, tiled=True)  7.59 us
    pallas_call x1, Pallas kernels, body(): pl.pallas_call(functools.partial(forward_kernel, leaf_units, n_leaves), o...  7.38 us
    pallas_call x1, Pallas kernels, body(): pl.pallas_call(functools.partial(unfold_kernel, leaf_units, n_leaves), ou...  7.11 us
    all_to_all x2, waiting for transfers between devices, neighbours(): return lax.all_to_all(chosen.astype(BF), 'batch', 0, 0, tiled=True)  6.79 us
    ppermute x3, waiting for transfers between devices, body(): lax.ppermute(total_bias, 'batch', pairs(tiles, 1 << bit))  6.49 us
  transfers between devices with their start and end apart: 27, of which 17 were waited for; matrix products, arithmetic and copies ran while one was open for 15% of the time, Pallas kernels for 2%

commit v1 on v0

v1 whole, which is shorter than its diff:
```python
import functools

import jax
import jax.numpy as jnp
from jax import lax
from jax.experimental import pallas as pl
from jax.experimental.pallas import tpu as pltpu
from jax.sharding import PartitionSpec as P

BF = jnp.bfloat16
F32 = jnp.float32
STEPS = ((0, 1), (0, -1), (1, 0), (-1, 0), (1, 1), (1, -1), (-1, 1), (-1, -1))
EDGE = 8
ROWS = 16
VMEM = pl.BlockSpec(memory_space=pltpu.VMEM)
SMEM = pl.BlockSpec(memory_space=pltpu.SMEM)
PARAMS = pltpu.CompilerParams(vmem_limit_bytes=48 * 2**20)


def pairs(count, flip):
    return [(i, i ^ flip) for i in range(count)]


def placed_at(owner):
    tiles = owner.shape[0]
    mine = lax.axis_index("batch")
    place = 0
    for q in range(tiles):
        place = place + jnp.where(owner[q] == mine, q, 0)
    return place, tiles // 4, 4


def neighbour(spot, step):
    place, columns, rows = spot
    column = place % columns + step[0]
    row = place // columns + step[1]
    there = (column >= 0) & (column < columns) & (row >= 0) & (row < rows)
    return there, jnp.where(there, place + step[1] * columns + step[0], place)


def leaf_codes(tiles):
    bits = tiles.bit_length() - 1
    mine = lax.axis_index("batch")
    codes = []
    for order in send_orders(tiles):
        code = (mine & 1) << bits
        for n, bit in enumerate(order):
            code = code | (((mine >> bit) & 1) << (bits - 2 - n))
        codes.append(code)
    return codes


def send_orders(tiles):
    bits = tiles.bit_length() - 1
    return tuple(range(1, bits)), tuple(range(bits - 1, 0, -1))


def lines_kernel(owner, below_ref, x_ref, above_ref, extra_ref, out_ref, rim):
    depth, _, channels = x_ref.shape
    grid = (EDGE, EDGE, channels)
    rim[0] = below_ref[0].reshape(grid).astype(F32)
    rim[1 : depth + 1] = x_ref[...].reshape((depth,) + grid).astype(F32)
    rim[depth + 1] = above_ref[0].reshape(grid).astype(F32)
    out_ref[...] = jnp.zeros(out_ref.shape, BF)
    for q in range(out_ref.shape[0]):
        out_ref[q, depth + 2] = extra_ref[...]
    spot = placed_at(owner)
    lines = {
        (0, 1): rim[:, :, 7, :].astype(BF),
        (0, -1): rim[:, :, 0, :].astype(BF),
        (1, 0): rim[:, 7].astype(BF),
        (-1, 0): rim[:, 0].astype(BF),
    }
    for step in STEPS:
        there, place = neighbour(spot, step)
        line = lines[(0, step[1]) if step[1] else step]

        @pl.when(there)
        def _(line=line, place=place):
            out_ref[owner[place], : depth + 2] = line


def gather_windows(owner, below_ref, x_ref, above_ref, recv_ref, rim, patch):
    depth, _, channels = x_ref.shape
    grid = (EDGE, EDGE, channels)
    rim[0, 1:9, 8:16, :] = below_ref[0].reshape(grid).astype(F32)
    rim[1 : depth + 1, 1:9, 8:16, :] = x_ref[...].reshape((depth,) + grid).astype(F32)
    rim[depth + 1, 1:9, 8:16, :] = above_ref[0].reshape(grid).astype(F32)
    spot = placed_at(owner)
    lines = [
        recv_ref[owner[neighbour(spot, step)[1]], : depth + 2].astype(F32) for step in STEPS
    ]
    rim[:, 1:9, 16, :] = lines[0]
    rim[:, 1:9, 7, :] = lines[1]
    rim[:, 9, 8:16, :] = lines[2]
    rim[:, 0, 8:16, :] = lines[3]
    rim[:, 9, 16, :] = lines[4][:, 0]
    rim[:, 9, 7, :] = lines[5][:, 0]
    rim[:, 0, 16, :] = lines[6][:, 7]
    rim[:, 0, 7, :] = lines[7][:, 7]

    def plane(z, carry):
        for dx in range(3):
            for dy in range(3):
                seen = rim[z, dx : dx + 8, 7 + dy : 15 + dy, :]
                row = pl.multiple_of(z * 64, 64)
                patch[dx * 3 + dy, pl.ds(row, 64), :] = seen.reshape(64, channels).astype(BF)
        return carry

    lax.fori_loop(0, depth + 2, plane, 0)


def forward_kernel(leaf_units, n_leaves, owner, below_ref, x_ref, above_ref, recv_ref, w_ref,
                   bias_ref, cot_ref, act_ref, gp_ref, gb_ref, gw_ref, rim, patch):
    voxels, channels = cot_ref.shape
    gather_windows(owner, below_ref, x_ref, above_ref, recv_ref, rim, patch)
    pre = jnp.broadcast_to(bias_ref[...], (voxels, channels))
    for dz in range(3):
        for k in range(9):
            pre += jnp.dot(
                patch[k, dz * 64 : dz * 64 + voxels, :],
                w_ref[dz * 9 + k],
                preferred_element_type=F32,
            )
    sigma = jax.nn.sigmoid(pre)
    act_ref[...] = (pre * sigma).astype(BF)
    grad = (cot_ref[...].astype(F32) * sigma * (1.0 + pre * (1.0 - sigma))).astype(BF)
    gp_ref[...] = grad
    rest = jnp.sum(grad.astype(F32), axis=0, keepdims=True)
    slices = []
    for _ in range(3):
        slices.append(rest.astype(BF).astype(F32))
        rest = rest - slices[-1]
    slices.append(jnp.zeros((5, channels), F32))
    gb_ref[...] = jnp.concatenate(slices, axis=0).astype(BF)
    half = channels // 2
    per_offset = half // ROWS
    lanes = 2 * channels // 128
    code = leaf_codes(owner.shape[0])

    def put(unit, value):
        leaf, inner = divmod(unit, leaf_units)
        colour = (leaf // (n_leaves // 4)) % 2
        gw_ref[(leaf ^ code[colour]) * leaf_units + inner] = value

    for dz in range(3):
        for k in range(9):
            o = dz * 9 + k
            part = lax.dot_general(
                patch[k, dz * 64 : dz * 64 + voxels, :],
                grad,
                (((0,), (0,)), ((), ())),
                preferred_element_type=F32,
            )
            wide = jnp.concatenate([part[:half], part[half:]], axis=1).astype(BF)
            for rows in range(per_offset):
                for lane in range(lanes):
                    put(
                        (o * per_offset + rows) * lanes + lane,
                        wide[rows * ROWS : (rows + 1) * ROWS, lane * 128 : (lane + 1) * 128],
                    )
    for unit in range(27 * per_offset * lanes, leaf_units * n_leaves):
        put(unit, jnp.zeros((ROWS, 128), BF))


def input_kernel(owner, below_ref, x_ref, above_ref, recv_ref, w_ref, out_ref, gb_ref, rim, patch):
    voxels, channels = out_ref.shape
    gather_windows(owner, below_ref, x_ref, above_ref, recv_ref, rim, patch)
    last = recv_ref.shape[1] - 1
    terms = recv_ref[0, last].astype(F32)
    for q in range(1, recv_ref.shape[0]):
        terms = terms + recv_ref[q, last].astype(F32)
    gb_ref[...] = jnp.sum(terms, axis=0, keepdims=True)
    total = jnp.zeros((voxels, channels), F32)
    for dz in range(3):
        for k in range(9):
            total += lax.dot_general(
                patch[8 - k, (2 - dz) * 64 : (2 - dz) * 64 + voxels, :],
                w_ref[dz * 9 + k],
                (((1,), (1,)), ((), ())),
                preferred_element_type=F32,
            )
    out_ref[...] = total.astype(BF)


def unfold_kernel(leaf_units, n_leaves, owner, *refs):
    *pieces, out_ref, flat = refs
    code = leaf_codes(owner.shape[0])
    rel = 0
    for piece in pieces:
        for leaf in range(piece.shape[0] // leaf_units):
            colour = (rel // (n_leaves // 4)) % 2
            row = pl.multiple_of((rel ^ code[colour]) * (leaf_units * ROWS), ROWS)
            block = piece[leaf * leaf_units : (leaf + 1) * leaf_units]
            flat[pl.ds(row, leaf_units * ROWS), :] = block.reshape(-1, 128).astype(F32)
            rel += 1
    pitch = flat.shape[0] // 32
    low = lax.broadcasted_iota(jnp.int32, (8, 128), 1) < 64

    def turned(x):
        return pltpu.roll(x, 64, 1)

    def block(base, group):
        rows = []
        for i in range(2):
            rows.append(
                [
                    flat[pl.ds(base + i + lane * ROWS + group * 8 * pitch, 8, stride=pitch), :]
                    for lane in range(3)
                ]
            )
        (a0, a1, a2), (b0, b1, b2) = rows
        rb0, rb1, ra1, ra2 = turned(b0), turned(b1), turned(a1), turned(a2)
        return (
            a0,
            jnp.where(low, a1, rb0),
            jnp.where(low, rb0, rb1),
            jnp.where(low, ra1, ra2),
            jnp.where(low, ra2, b1),
            b2,
        )

    count = out_ref.shape[0]
    span = out_ref.shape[1] // 2

    def pair(m, carry):
        i = m * 2
        base = (i // ROWS) * (3 * ROWS) + i % ROWS
        for top in range(0, count, 16):
            tiles = [block(base, top // 8), block(base, top // 8 + 1)]
            high = min(16, count - top)
            for n in range(6):
                both = jnp.concatenate([tiles[0][n], tiles[1][n]], axis=0).astype(BF)
                lane = pl.multiple_of((n // 3) * span + m * 384 + (n % 3) * 128, 128)
                out_ref[top : top + high, pl.ds(lane, 128)] = both[:high]
        return carry

    lax.fori_loop(0, span // 384, pair, 0, unroll=8)


def body(features, mask, owner, weight, bias, cotangent):
    channels = bias.shape[0]
    depth = features.shape[0]
    voxels = depth * 64
    regions = lax.axis_size("region")
    tiles = lax.axis_size("batch")
    bits = tiles.bit_length() - 1
    slab = lax.axis_index("region")
    orders = send_orders(tiles)
    n_leaves = 2 * tiles
    units = 27 * (channels // 2 // ROWS) * (2 * channels // 128)
    leaf_units = -(-units // n_leaves)
    barrier = lax.optimization_barrier

    def rims(first, last):
        up = lax.ppermute(last, "region", [(i, i + 1) for i in range(regions - 1)])
        down = lax.ppermute(first, "region", [(i + 1, i) for i in range(regions - 1)])
        return up, down

    def lines_for(below, planes, above, extra):
        return pl.pallas_call(
            lines_kernel,
            out_shape=jax.ShapeDtypeStruct((tiles, depth + 3, EDGE, channels), BF),
            in_specs=[SMEM] + [VMEM] * 4,
            out_specs=VMEM,
            scratch_shapes=[pltpu.VMEM((depth + 2, EDGE, EDGE, channels), F32)],
            compiler_params=PARAMS,
        )(owner, below, planes, above, extra)

    def exchanged(lines):
        return lax.all_to_all(lines, "batch", 0, 0, tiled=True)

    scratch = [
        pltpu.VMEM((depth + 2, 10, 24, channels), F32),
        pltpu.VMEM((9, (depth + 2) * 64, channels), BF),
    ]
    keep = mask.reshape(depth, 64, 1).astype(BF)

    def plane(z):
        return features[z : z + 1].reshape(1, 64, channels) * keep[z : z + 1]

    below, above = rims(plane(0), plane(depth - 1))
    occupied = features.reshape(depth, 64, channels) * keep
    upstream = (cotangent.reshape(depth, 64, channels) * keep).reshape(voxels, channels)
    kernel = weight.reshape(27, channels, channels)
    occupied, kernel, below, above = barrier((occupied, kernel, below, above))
    arrived = exchanged(lines_for(below, occupied, above, jnp.zeros((EDGE, channels), BF)))

    act, grad, bias_terms, terms = pl.pallas_call(
        functools.partial(forward_kernel, leaf_units, n_leaves),
        out_shape=(
            jax.ShapeDtypeStruct((voxels, channels), BF),
            jax.ShapeDtypeStruct((voxels, channels), BF),
            jax.ShapeDtypeStruct((EDGE, channels), BF),
            jax.ShapeDtypeStruct((n_leaves * leaf_units, ROWS, 128), BF),
        ),
        in_specs=[SMEM] + [VMEM] * 7,
        out_specs=(VMEM, VMEM, VMEM, VMEM),
        scratch_shapes=scratch,
        compiler_params=PARAMS,
        cost_estimate=pl.CostEstimate(
            flops=4 * 27 * voxels * channels * channels,
            bytes_accessed=6 << 20,
            transcendentals=voxels * channels,
        ),
    )(owner, below, occupied, above, arrived, kernel, bias.reshape(1, channels), upstream)
    grad = grad.reshape(depth, 64, channels)

    def halve(x, axis, count, flip):
        half = x.shape[0] // 2
        got = lax.ppermute(x[half:].astype(BF), axis, pairs(count, flip))
        return x[:half].astype(F32) + got.astype(F32)

    parts = halve(terms, "batch", tiles, 1)
    split = parts.shape[0] // 2
    colours = [parts[:split], parts[split:]]
    below, above = rims(grad[:1], grad[depth - 1 :])
    for step in range(bits - 1):
        colours = [halve(c, "batch", tiles, 1 << o[step]) for c, o in zip(colours, orders)]
        if step == 0:
            colours, below, above = barrier((colours, below, above))
            lines = lines_for(below, grad, above, bias_terms)
    last = jnp.concatenate(colours, axis=0)
    last, lines = barrier((last, lines))
    arrived = exchanged(lines)
    share = -(-last.shape[0] // regions)
    spare = share * regions - last.shape[0]
    last = jnp.pad(last, ((0, spare), (0, 0), (0, 0))).reshape(regions, share, ROWS, 128)
    flips = sorted(range(1, regions), key=lambda f: -f)
    total = lax.dynamic_index_in_dim(last, slab, 0, False)
    for flip in flips:
        piece = lax.dynamic_index_in_dim(last, slab ^ flip, 0, False).astype(BF)
        total = total + lax.ppermute(piece, "region", pairs(regions, flip)).astype(F32)
    total = total.astype(BF)
    total, arrived = barrier((total, arrived))

    held = [total] + [
        lax.ppermute(total, "region", pairs(regions, flip)) for flip in range(1, regions)
    ]
    whole = jnp.zeros((regions, share, ROWS, 128), BF)
    for flip, block in enumerate(held):
        whole = lax.dynamic_update_index_in_dim(whole, block, slab ^ flip, 0)
    whole = whole.reshape(regions * share, ROWS, 128)

    grad_input, total_bias = pl.pallas_call(
        input_kernel,
        out_shape=(
            jax.ShapeDtypeStruct((voxels, channels), BF),
            jax.ShapeDtypeStruct((1, channels), F32),
        ),
        in_specs=[SMEM] + [VMEM] * 5,
        out_specs=(VMEM, VMEM),
        scratch_shapes=scratch,
        compiler_params=PARAMS,
        cost_estimate=pl.CostEstimate(
            flops=2 * 27 * voxels * channels * channels, bytes_accessed=3 << 20, transcendentals=0
        ),
    )(owner, below, grad, above, arrived, kernel)

    colours = [[whole[:leaf_units]], [whole[leaf_units : 2 * leaf_units]]]
    for step in reversed(range(bits - 1)):
        colours = [
            [jnp.concatenate(c, axis=0) if len(c) > 1 else c[0]] for c in colours
        ]
        colours = [
            c + [lax.ppermute(c[0], "batch", pairs(tiles, 1 << o[step]))]
            for c, o in zip(colours, orders)
        ]
        if step == bits - 2:
            total_bias, grad_input, colours = barrier((total_bias, grad_input, colours))
            for bit in range(regions.bit_length() - 1):
                sent = lax.ppermute(total_bias, "region", pairs(regions, 1 << bit))
                total_bias = total_bias + sent
    near = colours[0] + colours[1]
    far = [lax.ppermute(c, "batch", pairs(tiles, 1)) for c in near]
    kernel_grad = pl.pallas_call(
        functools.partial(unfold_kernel, leaf_units, n_leaves),
        out_shape=jax.ShapeDtypeStruct((27, channels * channels), BF),
        in_specs=[SMEM] + [VMEM] * len(near + far),
        out_specs=VMEM,
        scratch_shapes=[pltpu.VMEM((32 * units // 27 * ROWS, 128), F32)],
        compiler_params=PARAMS,
    )(owner, *near, *far)

    def placed(rows):
        return (rows.reshape(depth, 64, channels) * keep).reshape(features.shape)

    return placed(act), placed(grad_input), kernel_grad, total_bias.reshape(channels)


def solution(mesh):
    split = P("region", "batch", None)
    return jax.shard_map(
        body,
        mesh=mesh,
        in_specs=(split, P("region", "batch"), P(), P(), P(), split),
        out_specs=(split, split, P(), P()),
        check_vma=False,
    )
```

time: 143 us -> 111 us (0.78)
  waiting for transfers between devices: 41.9 us -> 28.3 us
  between operations: 8.86 us -> 1.07 us
  other arithmetic: 11.7 us -> 6.58 us
  local copies, waits for them, and re-layouts: 20.4 us -> 15.8 us
  starting transfers between devices: 40.5 us -> 38.8 us
  Pallas kernels: 17.5 us -> 19.2 us
    ppermute x14, waiting for transfers between devices: 18.2 us -> 6.12 us  [the longest x2 2.88 us: rims(): lax.ppermute(first, 'region', [(i + 1, i) for i in range(regions - 1)])]
    all_to_all x2, waiting for transfers between devices: 6.79 us -> 11.9 us  [exchanged(): return lax.all_to_all(lines, 'batch', 0, 0, tiled=True)]
    ppermute x5, waiting for transfers between devices: 8.54 us -> 4.77 us  [halve(): got = lax.ppermute(x[half:].astype(BF), axis, pairs(count, flip))]
    pallas_call x1 -> x3, Pallas kernels: 3.02 us -> 6.46 us  [the longest x2 3.44 us: lines_for(): pl.pallas_call(lines_kernel, out_shape=jax.ShapeDtypeStruct((tiles, depth...]
    ppermute x3, waiting for transfers between devices: 4.44 us -> 1.09 us  [body(): lax.ppermute(piece, 'region', pairs(regions, flip)).astype(F32)]
    mul x3, local copies, waits for them, and re-layouts: 2.79 us -> 0.44 us  [body(): occupied = features.reshape(depth, 64, channels) * keep]
    reduce_sum x3 -> x0, other arithmetic: 2.2 us -> none  [the longest x1 0.83 us: body(): jnp.sum(jnp.where((step_x == x) & (step_y == y), slots - mine, 0)) + mine]
    ppermute x14, starting transfers between devices: 20.6 us -> 18.5 us  [the longest x2 9.46 us: rims(): up = lax.ppermute(last, 'region', [(i, i + 1) for i in range(regions - 1)])]
  transfers between devices with their start and end apart: 27 -> 27, of which waited for: 17 -> 14; matrix products, arithmetic and copies ran while one was open for 15% -> 13% of each run, Pallas kernels for 2% -> 4%
where the time goes in v1:
time: 111 us; the launch traced here: 110 us
  starting transfers between devices  38.8 us (35%)
  waiting for transfers between devices  28.3 us (25%)
  Pallas kernels  19.2 us (17%)
  local copies, waits for them, and re-layouts  15.8 us (14%)
  other arithmetic  6.58 us (6%)
    all_to_all x2, waiting for transfers between devices, exchanged(): return lax.all_to_all(lines, 'batch', 0, 0, tiled=True)  11.9 us
    ppermute x2, starting transfers between devices, rims(): up = lax.ppermute(last, 'region', [(i, i + 1) for i in range(regions - 1)])  9.46 us
    pallas_call x1, Pallas kernels, body(): pl.pallas_call(functools.partial(forward_kernel, leaf_units, n_leaves), o...  7.4 us
    all_to_all x2, starting transfers between devices, exchanged(): return lax.all_to_all(lines, 'batch', 0, 0, tiled=True)  7.23 us
    pallas_call x1, Pallas kernels, body(): pl.pallas_call(functools.partial(unfold_kernel, leaf_units, n_leaves), ou...  5.33 us
    unnamed x36, local copies, waits for them, and re-layouts  4.83 us
    ppermute x5, waiting for transfers between devices, halve(): got = lax.ppermute(x[half:].astype(BF), axis, pairs(count, flip))  4.77 us
    ppermute x3, waiting for transfers between devices, body(): lax.ppermute(total, 'region', pairs(regions, flip))  4.41 us
  transfers between devices with their start and end apart: 27, of which 14 were waited for; matrix products, arithmetic and copies ran while one was open for 13% of the time, Pallas kernels for 4%

profile of v1, /device:TPU:0, one launch (start us, length us, event | category | flops | bytes accessed | tf_op | source)
XLA Modules:
  0.0 109.8 jit_solution(4444270924400489498)
XLA Ops:
  0.6 0.7 convert_element_type.58
  1.3 0.8 fusion.10
  2.3 4.9 %collective-permute-start = (bf16[1,64,192]{2,1,0:T(8,128)(2,1)S(1)}, bf16[1,64,192]{2,1,0:T(8,128)(2,1)S(1)}, u32[]{:S(2)}, u32[]{:S(2)}) collective-permute-start(bf16[1,64,192]{2,1,0:T(8,128)(2,1)S(1)} %broadcast_multiply_fusion.3), channel_id=1, source_target_pairs={{0,8},{8,16},{16,24},{1,9},{9,17},{17,25},{2,10},{10,18},{18,26},{... | collective-permute-start | bytes 73736 | tf_op jit(solution)/shard_map/ppermute | solution.py:256
  7.4 1.3 %collective-permute-start.1 = (bf16[1,64,192]{2,1,0:T(8,128)(2,1)S(1)}, bf16[1,64,192]{2,1,0:T(8,128)(2,1)S(1)}, u32[]{:S(2)}, u32[]{:S(2)}) collective-permute-start(bf16[1,64,192]{2,1,0:T(8,128)(2,1)S(1)} %broadcast_multiply_fusion.2), channel_id=1, source_target_pairs={{8,0},{16,8},{24,16},{9,1},{17,9},{25,17},{10,2},{18,10},{26,18},{... | collective-permute-start | bytes 73736 | tf_op jit(solution)/shard_map/ppermute | solution.py:257
  8.7 1.2 %reshape.141 = bf16[8,64,192]{2,1,0:T(8,128)(2,1)S(1)} reshape(bf16[8,8,1536]{2,1,0:T(8,128)(2,1)} %param.6) | data formatting | bytes 393216 | tf_op jit(solution)/shard_map/reshape | solution.py:283
  10.1 4.3 %reshape.142.w_ref = bf16[27,192,192]{2,1,0:T(8,128)(2,1)S(1)} reshape(bf16[27,36864]{1,0:T(8,128)(2,1)} %param.9) | data formatting | bytes 3981312 | tf_op jit(solution)/shard_map/reshape | solution.py:285
  14.4 0.9 reshape.146
  15.4 1.7 %shard_map.93 = bf16[8,11,8,192]{3,2,1,0:T(8,128)(2,1)} custom-call(s32[8]{0:T(128)S(1)} %copy-done.12, bf16[1,64,192]{2,1,0:T(8,128)(2,1)S(1)} %collective-permute-done.below_ref, bf16[8,64,192]{2,1,0:T(8,128)(2,1)S(1)} %broadcast_multiply_fusion.1.x_ref, bf16[1,64,192]{2,1,0:T(8,128)(2,1)S(1)} %collective-permute-done.1.above_ref, ...), custom_call_target="tpu_custom_call" | custom-call | tf_op jit(solution)/shard_map/pallas_call | solution.py:261
  17.1 3.6 %all-to-all-start = ((bf16[8,11,8,192]{3,2,1,0:T(8,128)(2,1)}), bf16[8,11,8,192]{3,2,1,0:T(8,128)(2,1)S(1)}, u32[]{:S(2)}, u32[]{:S(2)}) async-start(bf16[8,11,8,192]{3,2,1,0:T(8,128)(2,1)} %shard_map.93), calls=%async_computation | async-start | bytes 720896 | tf_op jit(solution)/shard_map/all_to_all | solution.py:271
  20.7 1.8 %broadcast_multiply_fusion.cot_ref = bf16[512,192]{1,0:T(8,128)(2,1)} fusion(bf16[512,192]{1,0:T(8,128)(2,1)} %reshape.146, bf16[512]{0:T(512)(128)(2,1)S(1)} %mul.73), kind=kLoop, calls=%fused_computation.15 | loop fusion | flops 98304 | bytes 394240 | tf_op jit(solution)/shard_map/mul | solution.py:284
  22.5 6.2 %all-to-all-done.recv_ref = bf16[8,11,8,192]{3,2,1,0:T(8,128)(2,1)S(1)} async-done(((bf16[8,11,8,192]{3,2,1,0:T(8,128)(2,1)}), bf16[8,11,8,192]{3,2,1,0:T(8,128)(2,1)S(1)}, u32[]{:S(2)}, u32[]{:S(2)}) %all-to-all-start) | async-done | bytes 270368 | tf_op jit(solution)/shard_map/all_to_all | solution.py:271
  28.7 0.9 copy-done.3
  29.7 0.8 copy-done.9
  30.4 0.8 copy-done.11
  31.2 7.4 %shard_map.94 = (bf16[512,192]{1,0:T(8,128)(2,1)S(1)}, bf16[512,192]{1,0:T(8,128)(2,1)S(1)}, bf16[8,192]{1,0:T(8,128)(2,1)S(1)}, bf16[496,16,128]{2,1,0:T(8,128)(2,1)S(1)}) custom-call(s32[8]{0:T(128)S(1)} %copy-done.12, bf16[1,64,192]{2,1,0:T(8,128)(2,1)S(1)} %copy-done.9, bf16[8,64,192]{2,1,0:T(8,128)(2,1)S(1)} %broadcast_multiply_fusion.1.x_ref, ...), custom_call_target="tpu_custom_call" | custom-call | flops 2038431744 | bytes 6291456 | tf_op jit(solution)/shard_map/pallas_call | solution.py:289
  38.9 2.6 %collective-permute-done.2 = bf16[248,16,128]{2,1,0:T(8,128)(2,1)S(1)} collective-permute-done((bf16[248,16,128]{2,1,0:T(8,128)(2,1)S(1)}, bf16[248,16,128]{2,1,0:T(8,128)(2,1)S(1)}, u32[]{:S(2)}, u32[]{:S(2)}) %collective-permute-start.2) | collective-permute-done | bytes 1015840 | tf_op jit(solution)/shard_map/ppermute | solution.py:311
  41.5 0.3 fusion.6
  41.8 0.6 collective-permute-start.3
  42.4 0.6 collective-permute-start.4
  43.0 4.5 %collective-permute-start.5 = (bf16[1,64,192]{2,1,0:T(8,128)(2,1)S(1)}, bf16[1,64,192]{2,1,0:T(8,128)(2,1)S(1)}, u32[]{:S(2)}, u32[]{:S(2)}) collective-permute-start(bf16[1,64,192]{2,1,0:T(8,128)(2,1)S(1)} %get-tuple-element.64), channel_id=1, source_target_pairs={{0,8},{8,16},{16,24},{1,9},{9,17},{17,25},{2,10},{10,18},{18,26},{... | collective-permute-start | bytes 73736 | tf_op jit(solution)/shard_map/ppermute | solution.py:256
  47.6 1.3 %collective-permute-start.6 = (bf16[1,64,192]{2,1,0:T(8,128)(2,1)S(1)}, bf16[1,64,192]{2,1,0:T(8,128)(2,1)S(1)}, u32[]{:S(2)}, u32[]{:S(2)}) collective-permute-start(bf16[1,64,192]{2,1,0:T(8,128)(2,1)S(1)} %get-tuple-element.63), channel_id=1, source_target_pairs={{8,0},{16,8},{24,16},{9,1},{17,9},{25,17},{10,2},{18,10},{26,18},{... | collective-permute-start | bytes 73736 | tf_op jit(solution)/shard_map/ppermute | solution.py:257
  48.9 1.2 %collective-permute-done.3 = bf16[62,16,128]{2,1,0:T(8,128)(2,1)S(1)} collective-permute-done((bf16[62,16,128]{2,1,0:T(8,128)(2,1)S(1)}, bf16[62,16,128]{2,1,0:T(8,128)(2,1)S(1)}, u32[]{:S(2)}, u32[]{:S(2)}) %collective-permute-start.3) | collective-permute-done | bytes 253984 | tf_op jit(solution)/shard_map/ppermute | solution.py:311
  50.1 0.3 collective-permute-done.4
  50.5 2.9 %collective-permute-done.6.above_ref = bf16[1,64,192]{2,1,0:T(8,128)(2,1)S(1)} collective-permute-done((bf16[1,64,192]{2,1,0:T(8,128)(2,1)S(1)}, bf16[1,64,192]{2,1,0:T(8,128)(2,1)S(1)}, u32[]{:S(2)}, u32[]{:S(2)}) %collective-permute-start.6) | collective-permute-done | bytes 24608 | tf_op jit(solution)/shard_map/ppermute | solution.py:257
  53.4 0.7 slice.120
  54.0 1.5 %collective-permute-start.7 = (bf16[31,16,128]{2,1,0:T(8,128)(2,1)}, bf16[31,16,128]{2,1,0:T(8,128)(2,1)}, u32[]{:S(2)}, u32[]{:S(2)}) collective-permute-start(bf16[31,16,128]{2,1,0:T(8,128)(2,1)} %slice.120), channel_id=1, source_target_pairs={{0,4},{1,5},{2,6},{3,7},{4,0},{5,1},{6,2},{7,3},{8,12},{9,13},{10,... | collective-permute-start | bytes 380936 | tf_op jit(solution)/shard_map/ppermute | solution.py:311
  55.5 1.5 %collective-permute-start.8 = (bf16[31,16,128]{2,1,0:T(8,128)(2,1)S(1)}, bf16[31,16,128]{2,1,0:T(8,128)(2,1)S(1)}, u32[]{:S(2)}, u32[]{:S(2)}) collective-permute-start(bf16[31,16,128]{2,1,0:T(8,128)(2,1)S(1)} %slice.119), channel_id=1, source_target_pairs={{0,2},{1,3},{2,0},{3,1},{4,6},{5,7},{6,4},{7,5},{8,10},{9,11},{10,... | collective-permute-start | bytes 380936 | tf_op jit(solution)/shard_map/ppermute | solution.py:311
  57.1 1.7 %shard_map.95 = bf16[8,11,8,192]{3,2,1,0:T(8,128)(2,1)} custom-call(s32[8]{0:T(128)S(1)} %copy-done.12, bf16[1,64,192]{2,1,0:T(8,128)(2,1)S(1)} %collective-permute-done.5.below_ref, bf16[8,64,192]{2,1,0:T(8,128)(2,1)S(1)} %bitcast.35, bf16[1,64,192]{2,1,0:T(8,128)(2,1)S(1)} %collective-permute-done.6.above_ref, bf16[8,192]{1,0:T(8,128)(2,1)S(1)} %get-tuple-element.39.extra_ref), custom_call_target="tpu_custom_call" | custom-call | tf_op jit(solution)/shard_map/pallas_call | solution.py:261
  58.8 0.5 collective-permute-done.7
  59.3 1.0 convert_add_fusion.2
  60.3 0.2 collective-permute-done.8
  60.7 0.8 copy-done.15
  61.5 0.7 fusion.3
  62.1 2.6 %collective-permute-start.10 = (bf16[16,16,128]{2,1,0:T(8,128)(2,1)}, bf16[16,16,128]{2,1,0:T(8,128)(2,1)S(1)}, u32[]{:S(2)}, u32[]{:S(2)}) collective-permute-start(bf16[16,16,128]{2,1,0:T(8,128)(2,1)} %get-tuple-element.60), channel_id=1, source_target_pairs={{0,16},{8,24},{16,0},{24,8},{1,17},{9,25},{17,1},{25,9},{2,18},{10... | collective-permute-start | bytes 196616 | tf_op jit(solution)/shard_map/ppermute | solution.py:333
  64.7 0.3 collective-permute-start.11
  65.0 1.5 %collective-permute-start.9 = (bf16[16,16,128]{2,1,0:T(8,128)(2,1)S(1)}, bf16[16,16,128]{2,1,0:T(8,128)(2,1)}, u32[]{:S(2)}, u32[]{:S(2)}) collective-permute-start(bf16[16,16,128]{2,1,0:T(8,128)(2,1)S(1)} %get-tuple-element.58), channel_id=1, source_target_pairs={{0,24},{8,16},{16,8},{24,0},{1,25},{9,17},{17,9},{25,1},{2,26},{10... | collective-permute-start | bytes 196616 | tf_op jit(solution)/shard_map/ppermute | solution.py:333
  66.5 3.6 %all-to-all-start.1 = ((bf16[8,11,8,192]{3,2,1,0:T(8,128)(2,1)}), bf16[8,11,8,192]{3,2,1,0:T(8,128)(2,1)S(1)}, u32[]{:S(2)}, u32[]{:S(2)}) async-start(bf16[8,11,8,192]{3,2,1,0:T(8,128)(2,1)} %shard_map.95), calls=%async_computation.1 | async-start | bytes 720896 | tf_op jit(solution)/shard_map/all_to_all | solution.py:271
  70.1 1.1 collective-permute-done.9
  71.2 1.0 fusion.2
  72.2 5.7 %all-to-all-done.1.recv_ref = bf16[8,11,8,192]{3,2,1,0:T(8,128)(2,1)S(1)} async-done(((bf16[8,11,8,192]{3,2,1,0:T(8,128)(2,1)}), bf16[8,11,8,192]{3,2,1,0:T(8,128)(2,1)S(1)}, u32[]{:S(2)}, u32[]{:S(2)}) %all-to-all-start.1) | async-done | bytes 270368 | tf_op jit(solution)/shard_map/all_to_all | solution.py:271
  77.9 0.7 collective-permute-start.12
  78.6 2.2 %collective-permute-start.13 = (bf16[16,16,128]{2,1,0:T(8,128)(2,1)S(1)}, bf16[16,16,128]{2,1,0:T(8,128)(2,1)S(1)}, u32[]{:S(2)}, u32[]{:S(2)}) collective-permute-start(bf16[16,16,128]{2,1,0:T(8,128)(2,1)S(1)} %fusion.2), channel_id=1, source_target_pairs={{0,16},{8,24},{16,0},{24,8},{1,17},{9,25},{17,1},{25,9},{2,18},{10... | collective-permute-start | bytes 196616 | tf_op jit(solution)/shard_map/ppermute | solution.py:338
  80.8 1.6 %collective-permute-start.14 = (bf16[16,16,128]{2,1,0:T(8,128)(2,1)S(1)}, bf16[16,16,128]{2,1,0:T(8,128)(2,1)S(1)}, u32[]{:S(2)}, u32[]{:S(2)}) collective-permute-start(bf16[16,16,128]{2,1,0:T(8,128)(2,1)S(1)} %fusion.2), channel_id=1, source_target_pairs={{0,24},{8,16},{16,8},{24,0},{1,25},{9,17},{17,9},{25,1},{2,26},{10... | collective-permute-start | bytes 196616 | tf_op jit(solution)/shard_map/ppermute | solution.py:338
  82.4 2.7 %collective-permute-done.13 = bf16[16,16,128]{2,1,0:T(8,128)(2,1)S(1)} collective-permute-done((bf16[16,16,128]{2,1,0:T(8,128)(2,1)S(1)}, bf16[16,16,128]{2,1,0:T(8,128)(2,1)S(1)}, u32[]{:S(2)}, u32[]{:S(2)}) %collective-permute-start.13) | collective-permute-done | bytes 65568 | tf_op jit(solution)/shard_map/ppermute | solution.py:338
  85.1 1.7 %collective-permute-done.14 = bf16[16,16,128]{2,1,0:T(8,128)(2,1)S(1)} collective-permute-done((bf16[16,16,128]{2,1,0:T(8,128)(2,1)S(1)}, bf16[16,16,128]{2,1,0:T(8,128)(2,1)S(1)}, u32[]{:S(2)}, u32[]{:S(2)}) %collective-permute-start.14) | collective-permute-done | bytes 65568 | tf_op jit(solution)/shard_map/ppermute | solution.py:338
  86.9 0.6 collective-permute-start.15
  87.5 0.7 collective-permute-start.16
  88.2 0.8 copy-done.5
  88.9 0.8 copy-done.7
  89.7 3.0 %shard_map.96 = (bf16[512,192]{1,0:T(8,128)(2,1)S(1)}, f32[1,192]{1,0:T(1,128)S(1)}) custom-call(s32[8]{0:T(128)S(1)} %copy-done.12, bf16[1,64,192]{2,1,0:T(8,128)(2,1)S(1)} %copy-done.5, bf16[8,64,192]{2,1,0:T(8,128)(2,1)S(1)} %bitcast.36, bf16[1,64,192]{2,1,0:T(8,128)(2,1)S(1)} %copy-done.7, bf16[8,11,8,192]{3,2,1,0:T(8,128)(2,1)S(1)} %all-to-all-done.1.recv_ref, ...), custom_call_target="tpu_custom_call" | custom-call | flops 1019215872 | bytes 3145728 | tf_op jit(solution)/shard_map/pallas_call | solution.py:345
  92.8 1.7 %collective-permute-start.18 = (bf16[62,16,128]{2,1,0:T(8,128)(2,1)S(1)}, bf16[62,16,128]{2,1,0:T(8,128)(2,1)S(1)}, u32[]{:S(2)}, u32[]{:S(2)}) collective-permute-start(bf16[62,16,128]{2,1,0:T(8,128)(2,1)S(1)} %constant_dynamic-update-slice_fusion.2.refs_2_), channel_id=1, source_target_pairs={{0,4},{1,5},{2,6},{3,7},{4,0},{5,1},{6,2},{7,3},{8,12},{9,13},{10,... | collective-permute-start | bytes 761864 | tf_op jit(solution)/shard_map/ppermute | solution.py:366
  94.5 1.3 %collective-permute-start.17 = (bf16[62,16,128]{2,1,0:T(8,128)(2,1)S(1)}, bf16[62,16,128]{2,1,0:T(8,128)(2,1)S(1)}, u32[]{:S(2)}, u32[]{:S(2)}) collective-permute-start(bf16[62,16,128]{2,1,0:T(8,128)(2,1)S(1)} %constant_dynamic-update-slice_fusion.refs_0_), channel_id=1, source_target_pairs={{0,2},{1,3},{2,0},{3,1},{4,6},{5,7},{6,4},{7,5},{8,10},{9,11},{10,... | collective-permute-start | bytes 761864 | tf_op jit(solution)/shard_map/ppermute | solution.py:366
  95.8 0.4 collective-permute-start.23
  96.3 0.2 mul.76
  96.6 0.2 reshape.147
  96.9 0.5 collective-permute-start.19
  97.4 1.2 %reshape.151 = bf16[8,8,1536]{2,1,0:T(8,128)(2,1)S(1)} reshape(bf16[512,192]{1,0:T(8,128)(2,1)} %copy-done.2) | data formatting | bytes 393216 | tf_op jit(solution)/shard_map/reshape | solution.py:386
  98.6 0.8 collective-permute-done.23
  99.4 1.1 %collective-permute-start.24 = (f32[1,192]{1,0:T(1,128)S(1)}, f32[1,192]{1,0:T(1,128)S(1)}, u32[]{:S(2)}, u32[]{:S(2)}) collective-permute-start(f32[1,192]{1,0:T(1,128)S(1)} %add.62), channel_id=1, source_target_pairs={{0,16},{8,24},{16,0},{24,8},{1,17},{9,25},{17,1},{25,9},{2,18},{10... | collective-permute-start | bytes 2312 | tf_op jit(solution)/shard_map/ppermute | solution.py:372
  100.5 0.4 collective-permute-done.17.refs_1_
  101.0 0.8 fusion.9
  101.8 2.1 %collective-permute-done.24 = f32[1,192]{1,0:T(1,128)S(1)} collective-permute-done((f32[1,192]{1,0:T(1,128)S(1)}, f32[1,192]{1,0:T(1,128)S(1)}, u32[]{:S(2)}, u32[]{:S(2)}) %collective-permute-start.24) | collective-permute-done | bytes 800 | tf_op jit(solution)/shard_map/ppermute | solution.py:372
  103.8 0.6 add.63
  104.4 5.3 %shard_map.97 = bf16[27,36864]{1,0:T(8,128)(2,1)} custom-call(s32[8]{0:T(128)S(1)} %copy-done.12, bf16[62,16,128]{2,1,0:T(8,128)(2,1)S(1)} %constant_dynamic-update-slice_fusion.refs_0_, bf16[62,16,128]{2,1,0:T(8,128)(2,1)S(1)} %collective-permute-done.17.refs_1_, bf16[62,16,128]{2,1,0:T(8,128)(2,1)S(1)} %constant_dynamic-update-slice_fusion.2.refs_2_, ...), custom_call_target="tpu_custom_call" | custom-call | tf_op jit(solution)/shard_map/pallas_call | solution.py:376
  (73 shorter events, 1.7 us)
Async XLA Ops:
  2.3 13.1 %collective-permute-start = (bf16[1,64,192]{2,1,0:T(8,128)(2,1)S(1)}, bf16[1,64,192]{2,1,0:T(8,128)(2,1)S(1)}, u32[]{:S(2)}, u32[]{:S(2)}) collective-permute-start(bf16[1,64,192]{2,1,0:T(8,128)(2,1)S(1)} %broadcast_multiply_fusion.3), channel_id=1, source_target_pairs={{0,8},{8,16},{16,24},{1,9},{9,17},{17,25},{2,10},{10,18},{18,26},{... | collective-permute-start | bytes 73736 | tf_op jit(solution)/shard_map/ppermute | solution.py:256
  7.4 8.0 %collective-permute-start.1 = (bf16[1,64,192]{2,1,0:T(8,128)(2,1)S(1)}, bf16[1,64,192]{2,1,0:T(8,128)(2,1)S(1)}, u32[]{:S(2)}, u32[]{:S(2)}) collective-permute-start(bf16[1,64,192]{2,1,0:T(8,128)(2,1)S(1)} %broadcast_multiply_fusion.2), channel_id=1, source_target_pairs={{8,0},{16,8},{24,16},{9,1},{17,9},{25,17},{10,2},{18,10},{26,18},{... | collective-permute-start | bytes 73736 | tf_op jit(solution)/shard_map/ppermute | solution.py:257
  10.1 4.4 %copy-start.16 = (bf16[8,8,1536]{2,1,0:T(8,128)(2,1)S(1)}, bf16[8,8,1536]{2,1,0:T(8,128)(2,1)}, u32[]{:S(2)}) copy-start(bf16[8,8,1536]{2,1,0:T(8,128)(2,1)} %param.11) | copy-start | bytes 589828
  10.1 5.3 %copy-start.12 = (s32[8]{0:T(128)S(1)}, s32[8]{0:T(128)}, u32[]{:S(2)}) copy-start(s32[8]{0:T(128)} %owner.9) | copy-start | bytes 100
  14.4 14.3 %copy-start.13 = (f32[192]{0:T(256)S(1)}, f32[192]{0:T(256)}, u32[]{:S(2)}) copy-start(f32[192]{0:T(256)} %param.10) | copy-start | bytes 2308
  15.4 13.4 %copy-start.8 = (bf16[1,64,192]{2,1,0:T(8,128)(2,1)}, bf16[1,64,192]{2,1,0:T(8,128)(2,1)S(1)}, u32[]{:S(2)}) copy-start(bf16[1,64,192]{2,1,0:T(8,128)(2,1)S(1)} %collective-permute-done.below_ref) | copy-start | bytes 73732
  15.4 13.3 %copy-start.10 = (bf16[1,64,192]{2,1,0:T(8,128)(2,1)}, bf16[1,64,192]{2,1,0:T(8,128)(2,1)S(1)}, u32[]{:S(2)}) copy-start(bf16[1,64,192]{2,1,0:T(8,128)(2,1)S(1)} %collective-permute-done.1.above_ref) | copy-start | bytes 73732
  17.1 11.6 %all-to-all-start = ((bf16[8,11,8,192]{3,2,1,0:T(8,128)(2,1)}), bf16[8,11,8,192]{3,2,1,0:T(8,128)(2,1)S(1)}, u32[]{:S(2)}, u32[]{:S(2)}) async-start(bf16[8,11,8,192]{3,2,1,0:T(8,128)(2,1)} %shard_map.93), calls=%async_computation | async-start | bytes 720896 | tf_op jit(solution)/shard_map/all_to_all | solution.py:271
  28.7 1.0 copy-start.3
  29.7 0.8 copy-start.9
  30.4 0.8 copy-start.11
  38.6 3.2 %copy-start = (bf16[512,192]{1,0:T(8,128)(2,1)}, bf16[512,192]{1,0:T(8,128)(2,1)S(1)}, u32[]{:S(2)}) copy-start(bf16[512,192]{1,0:T(8,128)(2,1)S(1)} %get-tuple-element.32) | copy-start | bytes 589828
  38.8 2.7 %collective-permute-start.2 = (bf16[248,16,128]{2,1,0:T(8,128)(2,1)S(1)}, bf16[248,16,128]{2,1,0:T(8,128)(2,1)S(1)}, u32[]{:S(2)}, u32[]{:S(2)}) collective-permute-start(bf16[248,16,128]{2,1,0:T(8,128)(2,1)S(1)} %slice.83), channel_id=1, source_target_pairs={{0,1},{1,0},{2,3},{3,2},{4,5},{5,4},{6,7},{7,6},{8,9},{9,8},{10,11... | collective-permute-start | bytes 3047432 | tf_op jit(solution)/shard_map/ppermute | solution.py:311
  41.8 8.2 %collective-permute-start.3 = (bf16[62,16,128]{2,1,0:T(8,128)(2,1)S(1)}, bf16[62,16,128]{2,1,0:T(8,128)(2,1)S(1)}, u32[]{:S(2)}, u32[]{:S(2)}) collective-permute-start(bf16[62,16,128]{2,1,0:T(8,128)(2,1)S(1)} %get-tuple-element.57), channel_id=1, source_target_pairs={{0,2},{1,3},{2,0},{3,1},{4,6},{5,7},{6,4},{7,5},{8,10},{9,11},{10,... | collective-permute-start | bytes 761864 | tf_op jit(solution)/shard_map/ppermute | solution.py:311
  42.4 7.9 %collective-permute-start.4 = (bf16[62,16,128]{2,1,0:T(8,128)(2,1)S(1)}, bf16[62,16,128]{2,1,0:T(8,128)(2,1)S(1)}, u32[]{:S(2)}, u32[]{:S(2)}) collective-permute-start(bf16[62,16,128]{2,1,0:T(8,128)(2,1)S(1)} %get-tuple-element.56), channel_id=1, source_target_pairs={{0,4},{1,5},{2,6},{3,7},{4,0},{5,1},{6,2},{7,3},{8,12},{9,13},{10,... | collective-permute-start | bytes 761864 | tf_op jit(solution)/shard_map/ppermute | solution.py:311
  43.0 7.5 %collective-permute-start.5 = (bf16[1,64,192]{2,1,0:T(8,128)(2,1)S(1)}, bf16[1,64,192]{2,1,0:T(8,128)(2,1)S(1)}, u32[]{:S(2)}, u32[]{:S(2)}) collective-permute-start(bf16[1,64,192]{2,1,0:T(8,128)(2,1)S(1)} %get-tuple-element.64), channel_id=1, source_target_pairs={{0,8},{8,16},{16,24},{1,9},{9,17},{17,25},{2,10},{10,18},{18,26},{... | collective-permute-start | bytes 73736 | tf_op jit(solution)/shard_map/ppermute | solution.py:256
  47.6 5.8 %collective-permute-start.6 = (bf16[1,64,192]{2,1,0:T(8,128)(2,1)S(1)}, bf16[1,64,192]{2,1,0:T(8,128)(2,1)S(1)}, u32[]{:S(2)}, u32[]{:S(2)}) collective-permute-start(bf16[1,64,192]{2,1,0:T(8,128)(2,1)S(1)} %get-tuple-element.63), channel_id=1, source_target_pairs={{8,0},{16,8},{24,16},{9,1},{17,9},{25,17},{10,2},{18,10},{26,18},{... | collective-permute-start | bytes 73736 | tf_op jit(solution)/shard_map/ppermute | solution.py:257
  50.5 2.9 %copy-start.14 = (f32[62,16,128]{2,1,0:T(8,128)}, f32[62,16,128]{2,1,0:T(8,128)S(1)}, u32[]{:S(2)}) copy-start(f32[62,16,128]{2,1,0:T(8,128)S(1)} %get-tuple-element.37) | copy-start | bytes 1523716
  50.5 10.2 %copy-start.4 = (bf16[1,64,192]{2,1,0:T(8,128)(2,1)}, bf16[1,64,192]{2,1,0:T(8,128)(2,1)S(1)}, u32[]{:S(2)}) copy-start(bf16[1,64,192]{2,1,0:T(8,128)(2,1)S(1)} %collective-permute-done.5.below_ref) | copy-start | bytes 73732
  53.4 7.3 %copy-start.6 = (bf16[1,64,192]{2,1,0:T(8,128)(2,1)}, bf16[1,64,192]{2,1,0:T(8,128)(2,1)S(1)}, u32[]{:S(2)}) copy-start(bf16[1,64,192]{2,1,0:T(8,128)(2,1)S(1)} %collective-permute-done.6.above_ref) | copy-start | bytes 73732
  54.0 5.2 %collective-permute-start.7 = (bf16[31,16,128]{2,1,0:T(8,128)(2,1)}, bf16[31,16,128]{2,1,0:T(8,128)(2,1)}, u32[]{:S(2)}, u32[]{:S(2)}) collective-permute-start(bf16[31,16,128]{2,1,0:T(8,128)(2,1)} %slice.120), channel_id=1, source_target_pairs={{0,4},{1,5},{2,6},{3,7},{4,0},{5,1},{6,2},{7,3},{8,12},{9,13},{10,... | collective-permute-start | bytes 380936 | tf_op jit(solution)/shard_map/ppermute | solution.py:311
  55.5 5.0 %collective-permute-start.8 = (bf16[31,16,128]{2,1,0:T(8,128)(2,1)S(1)}, bf16[31,16,128]{2,1,0:T(8,128)(2,1)S(1)}, u32[]{:S(2)}, u32[]{:S(2)}) collective-permute-start(bf16[31,16,128]{2,1,0:T(8,128)(2,1)S(1)} %slice.119), channel_id=1, source_target_pairs={{0,2},{1,3},{2,0},{3,1},{4,6},{5,7},{6,4},{7,5},{8,10},{9,11},{10,... | collective-permute-start | bytes 380936 | tf_op jit(solution)/shard_map/ppermute | solution.py:311
  60.7 0.8 copy-start.15
  62.1 8.0 %collective-permute-start.10 = (bf16[16,16,128]{2,1,0:T(8,128)(2,1)}, bf16[16,16,128]{2,1,0:T(8,128)(2,1)S(1)}, u32[]{:S(2)}, u32[]{:S(2)}) collective-permute-start(bf16[16,16,128]{2,1,0:T(8,128)(2,1)} %get-tuple-element.60), channel_id=1, source_target_pairs={{0,16},{8,24},{16,0},{24,8},{1,17},{9,25},{17,1},{25,9},{2,18},{10... | collective-permute-start | bytes 196616 | tf_op jit(solution)/shard_map/ppermute | solution.py:333
  64.7 5.4 %collective-permute-start.11 = (bf16[16,16,128]{2,1,0:T(8,128)(2,1)S(1)}, bf16[16,16,128]{2,1,0:T(8,128)(2,1)S(1)}, u32[]{:S(2)}, u32[]{:S(2)}) collective-permute-start(bf16[16,16,128]{2,1,0:T(8,128)(2,1)S(1)} %get-tuple-element.59), channel_id=1, source_target_pairs={{0,8},{8,0},{16,24},{24,16},{1,9},{9,1},{17,25},{25,17},{2,10},{10... | collective-permute-start | bytes 196616 | tf_op jit(solution)/shard_map/ppermute | solution.py:333
  65.0 6.2 %collective-permute-start.9 = (bf16[16,16,128]{2,1,0:T(8,128)(2,1)S(1)}, bf16[16,16,128]{2,1,0:T(8,128)(2,1)}, u32[]{:S(2)}, u32[]{:S(2)}) collective-permute-start(bf16[16,16,128]{2,1,0:T(8,128)(2,1)S(1)} %get-tuple-element.58), channel_id=1, source_target_pairs={{0,24},{8,16},{16,8},{24,0},{1,25},{9,17},{17,9},{25,1},{2,26},{10... | collective-permute-start | bytes 196616 | tf_op jit(solution)/shard_map/ppermute | solution.py:333
  66.5 11.4 %all-to-all-start.1 = ((bf16[8,11,8,192]{3,2,1,0:T(8,128)(2,1)}), bf16[8,11,8,192]{3,2,1,0:T(8,128)(2,1)S(1)}, u32[]{:S(2)}, u32[]{:S(2)}) async-start(bf16[8,11,8,192]{3,2,1,0:T(8,128)(2,1)} %shard_map.95), calls=%async_computation.1 | async-start | bytes 720896 | tf_op jit(solution)/shard_map/all_to_all | solution.py:271
  77.9 4.5 %collective-permute-start.12 = (bf16[16,16,128]{2,1,0:T(8,128)(2,1)S(1)}, bf16[16,16,128]{2,1,0:T(8,128)(2,1)S(1)}, u32[]{:S(2)}, u32[]{:S(2)}) collective-permute-start(bf16[16,16,128]{2,1,0:T(8,128)(2,1)S(1)} %fusion.2), channel_id=1, source_target_pairs={{0,8},{8,0},{16,24},{24,16},{1,9},{9,1},{17,25},{25,17},{2,10},{10... | collective-permute-start | bytes 196616 | tf_op jit(solution)/shard_map/ppermute | solution.py:338
  78.6 6.5 %collective-permute-start.13 = (bf16[16,16,128]{2,1,0:T(8,128)(2,1)S(1)}, bf16[16,16,128]{2,1,0:T(8,128)(2,1)S(1)}, u32[]{:S(2)}, u32[]{:S(2)}) collective-permute-start(bf16[16,16,128]{2,1,0:T(8,128)(2,1)S(1)} %fusion.2), channel_id=1, source_target_pairs={{0,16},{8,24},{16,0},{24,8},{1,17},{9,25},{17,1},{25,9},{2,18},{10... | collective-permute-start | bytes 196616 | tf_op jit(solution)/shard_map/ppermute | solution.py:338
  80.8 6.1 %collective-permute-start.14 = (bf16[16,16,128]{2,1,0:T(8,128)(2,1)S(1)}, bf16[16,16,128]{2,1,0:T(8,128)(2,1)S(1)}, u32[]{:S(2)}, u32[]{:S(2)}) collective-permute-start(bf16[16,16,128]{2,1,0:T(8,128)(2,1)S(1)} %fusion.2), channel_id=1, source_target_pairs={{0,24},{8,16},{16,8},{24,0},{1,25},{9,17},{17,9},{25,1},{2,26},{10... | collective-permute-start | bytes 196616 | tf_op jit(solution)/shard_map/ppermute | solution.py:338
  86.9 5.8 %collective-permute-start.15 = (bf16[31,16,128]{2,1,0:T(8,128)(2,1)S(1)}, bf16[31,16,128]{2,1,0:T(8,128)(2,1)S(1)}, u32[]{:S(2)}, u32[]{:S(2)}) collective-permute-start(bf16[31,16,128]{2,1,0:T(8,128)(2,1)S(1)} %get-tuple-element.47), channel_id=1, source_target_pairs={{0,4},{1,5},{2,6},{3,7},{4,0},{5,1},{6,2},{7,3},{8,12},{9,13},{10,... | collective-permute-start | bytes 380936 | tf_op jit(solution)/shard_map/ppermute | solution.py:366
  87.5 9.1 %copy-start.1 = (bf16[512,192]{1,0:T(8,128)(2,1)S(1)}, bf16[512,192]{1,0:T(8,128)(2,1)}, u32[]{:S(2)}) copy-start(bf16[512,192]{1,0:T(8,128)(2,1)} %copy-done) | copy-start | bytes 589828
  87.5 5.3 %collective-permute-start.16 = (bf16[31,16,128]{2,1,0:T(8,128)(2,1)S(1)}, bf16[31,16,128]{2,1,0:T(8,128)(2,1)S(1)}, u32[]{:S(2)}, u32[]{:S(2)}) collective-permute-start(bf16[31,16,128]{2,1,0:T(8,128)(2,1)S(1)} %get-tuple-element.49), channel_id=1, source_target_pairs={{0,2},{1,3},{2,0},{3,1},{4,6},{5,7},{6,4},{7,5},{8,10},{9,11},{10,... | collective-permute-start | bytes 380936 | tf_op jit(solution)/shard_map/ppermute | solution.py:366
  88.2 0.8 copy-start.5
  88.9 0.8 copy-start.7
  92.7 1.8 %copy-start.2 = (bf16[512,192]{1,0:T(8,128)(2,1)}, bf16[512,192]{1,0:T(8,128)(2,1)S(1)}, u32[]{:S(2)}) copy-start(bf16[512,192]{1,0:T(8,128)(2,1)S(1)} %get-tuple-element.46) | copy-start | bytes 589828
  92.8 7.7 %collective-permute-start.18 = (bf16[62,16,128]{2,1,0:T(8,128)(2,1)S(1)}, bf16[62,16,128]{2,1,0:T(8,128)(2,1)S(1)}, u32[]{:S(2)}, u32[]{:S(2)}) collective-permute-start(bf16[62,16,128]{2,1,0:T(8,128)(2,1)S(1)} %constant_dynamic-update-slice_fusion.2.refs_2_), channel_id=1, source_target_pairs={{0,4},{1,5},{2,6},{3,7},{4,0},{5,1},{6,2},{7,3},{8,12},{9,13},{10,... | collective-permute-start | bytes 761864 | tf_op jit(solution)/shard_map/ppermute | solution.py:366
  94.5 6.3 %collective-permute-start.17 = (bf16[62,16,128]{2,1,0:T(8,128)(2,1)S(1)}, bf16[62,16,128]{2,1,0:T(8,128)(2,1)S(1)}, u32[]{:S(2)}, u32[]{:S(2)}) collective-permute-start(bf16[62,16,128]{2,1,0:T(8,128)(2,1)S(1)} %constant_dynamic-update-slice_fusion.refs_0_), channel_id=1, source_target_pairs={{0,2},{1,3},{2,0},{3,1},{4,6},{5,7},{6,4},{7,5},{8,10},{9,11},{10,... | collective-permute-start | bytes 761864 | tf_op jit(solution)/shard_map/ppermute | solution.py:366
  95.8 3.6 %collective-permute-start.23 = (f32[1,192]{1,0:T(1,128)S(1)}, f32[1,192]{1,0:T(1,128)S(1)}, u32[]{:S(2)}, u32[]{:S(2)}) collective-permute-start(f32[1,192]{1,0:T(1,128)S(1)} %get-tuple-element.51), channel_id=1, source_target_pairs={{0,8},{8,0},{16,24},{24,16},{1,9},{9,1},{17,25},{25,17},{2,10},{10... | collective-permute-start | bytes 2312 | tf_op jit(solution)/shard_map/ppermute | solution.py:372
  96.8 7.6 %collective-permute-start.21 = (bf16[62,16,128]{2,1,0:T(8,128)(2,1)S(1)}, bf16[62,16,128]{2,1,0:T(8,128)(2,1)S(1)}, u32[]{:S(2)}, u32[]{:S(2)}) collective-permute-start(bf16[62,16,128]{2,1,0:T(8,128)(2,1)S(1)} %constant_dynamic-update-slice_fusion.2.refs_2_), channel_id=1, source_target_pairs={{0,1},{1,0},{2,3},{3,2},{4,5},{5,4},{6,7},{7,6},{8,9},{9,8},{10,11... | collective-permute-start | bytes 761864 | tf_op jit(solution)/shard_map/ppermute | solution.py:375
  96.9 7.5 %collective-permute-start.19 = (bf16[62,16,128]{2,1,0:T(8,128)(2,1)S(1)}, bf16[62,16,128]{2,1,0:T(8,128)(2,1)S(1)}, u32[]{:S(2)}, u32[]{:S(2)}) collective-permute-start(bf16[62,16,128]{2,1,0:T(8,128)(2,1)S(1)} %constant_dynamic-update-slice_fusion.refs_0_), channel_id=1, source_target_pairs={{0,1},{1,0},{2,3},{3,2},{4,5},{5,4},{6,7},{7,6},{8,9},{9,8},{10,11... | collective-permute-start | bytes 761864 | tf_op jit(solution)/shard_map/ppermute | solution.py:375
  99.4 4.5 %collective-permute-start.24 = (f32[1,192]{1,0:T(1,128)S(1)}, f32[1,192]{1,0:T(1,128)S(1)}, u32[]{:S(2)}, u32[]{:S(2)}) collective-permute-start(f32[1,192]{1,0:T(1,128)S(1)} %add.62), channel_id=1, source_target_pairs={{0,16},{8,24},{16,0},{24,8},{1,17},{9,25},{17,1},{25,9},{2,18},{10... | collective-permute-start | bytes 2312 | tf_op jit(solution)/shard_map/ppermute | solution.py:372
  100.5 3.9 %collective-permute-start.22 = (bf16[62,16,128]{2,1,0:T(8,128)(2,1)S(1)}, bf16[62,16,128]{2,1,0:T(8,128)(2,1)S(1)}, u32[]{:S(2)}, u32[]{:S(2)}) collective-permute-start(bf16[62,16,128]{2,1,0:T(8,128)(2,1)S(1)} %collective-permute-done.18.refs_3_), channel_id=1, source_target_pairs={{0,1},{1,0},{2,3},{3,2},{4,5},{5,4},{6,7},{7,6},{8,9},{9,8},{10,11... | collective-permute-start | bytes 761864 | tf_op jit(solution)/shard_map/ppermute | solution.py:375
  100.9 3.6 %collective-permute-start.20 = (bf16[62,16,128]{2,1,0:T(8,128)(2,1)S(1)}, bf16[62,16,128]{2,1,0:T(8,128)(2,1)S(1)}, u32[]{:S(2)}, u32[]{:S(2)}) collective-permute-start(bf16[62,16,128]{2,1,0:T(8,128)(2,1)S(1)} %collective-permute-done.17.refs_1_), channel_id=1, source_target_pairs={{0,1},{1,0},{2,3},{3,2},{4,5},{5,4},{6,7},{7,6},{8,9},{9,8},{10,11... | collective-permute-start | bytes 761864 | tf_op jit(solution)/shard_map/ppermute | solution.py:375

commit v2 on v1

v2 whole, which is shorter than its diff:
```python
import functools

import jax
import jax.numpy as jnp
from jax import lax
from jax.experimental import pallas as pl
from jax.experimental.pallas import tpu as pltpu
from jax.sharding import PartitionSpec as P

BF = jnp.bfloat16
F32 = jnp.float32
STEPS = ((0, 1), (0, -1), (1, 0), (-1, 0), (1, 1), (1, -1), (-1, 1), (-1, -1))
EDGE = 8
ROWS = 16
VMEM = pl.BlockSpec(memory_space=pltpu.VMEM)
SMEM = pl.BlockSpec(memory_space=pltpu.SMEM)


def vmem(mib):
    return pltpu.CompilerParams(vmem_limit_bytes=mib * 2**20)


def pairs(count, flip):
    return [(i, i ^ flip) for i in range(count)]


def placed_at(owner):
    tiles = owner.shape[0]
    mine = lax.axis_index("batch")
    place = 0
    for q in range(tiles):
        place = place + jnp.where(owner[q] == mine, q, 0)
    return place, tiles // 4, 4


def neighbour(spot, step):
    place, columns, rows = spot
    column = place % columns + step[0]
    row = place // columns + step[1]
    there = (column >= 0) & (column < columns) & (row >= 0) & (row < rows)
    return there, jnp.where(there, place + step[1] * columns + step[0], place)


def leaf_codes(tiles):
    bits = tiles.bit_length() - 1
    mine = lax.axis_index("batch")
    codes = []
    for order in send_orders(tiles):
        code = (mine & 1) << bits
        for n, bit in enumerate(order):
            code = code | (((mine >> bit) & 1) << (bits - 2 - n))
        codes.append(code)
    return codes


def send_orders(tiles):
    bits = tiles.bit_length() - 1
    return tuple(range(1, bits)), tuple(range(bits - 1, 0, -1))


def split_in_three(x):
    terms = []
    for _ in range(3):
        terms.append(x.astype(BF).astype(F32))
        x = x - terms[-1]
    return terms


def unrolled(raw_ref, mask_ref, store):
    count = mask_ref.shape[1]
    wide = raw_ref[...].astype(F32)
    kept = mask_ref[...].astype(F32)
    channels = wide.shape[1] // count
    for y in range(count):
        store(y, wide[:, y * channels : (y + 1) * channels] * kept[:, y : y + 1])


def rolled(rows, mask_ref):
    kept = mask_ref[...].astype(F32)
    parts = [rows[:, y, :] * kept[:, y : y + 1] for y in range(mask_ref.shape[1])]
    return jnp.concatenate(parts, axis=1).astype(BF)


def cut_lines(owner, inner_ref, outer_ref, lines_ref, planes_ref, rim):
    thick, _, _, channels = rim.shape
    odd = lax.axis_index("region") & 1
    for ref, z in ((inner_ref, (thick - 1) * (1 - odd)), (outer_ref, (thick - 1) * odd)):
        planes_ref[z] = ref[0]
        rim[z] = ref[0].reshape(EDGE, EDGE, channels).astype(F32)
    spot = placed_at(owner)
    lines = {
        (0, 1): rim[:, :, 7, :].astype(BF),
        (0, -1): rim[:, :, 0, :].astype(BF),
        (1, 0): rim[:, 7].astype(BF),
        (-1, 0): rim[:, 0].astype(BF),
    }
    for step in STEPS:
        there, place = neighbour(spot, step)
        line = lines[(0, step[1]) if step[1] else step]

        @pl.when(there)
        def _(line=line, place=place):
            lines_ref[owner[place], :thick] = line


def input_lines_kernel(owner, inner_ref, raw_ref, mask_ref, outer_ref, lines_ref, planes_ref, rim):
    depth = rim.shape[0] - 2
    channels = rim.shape[3]

    def store(y, rows):
        rim[1 : depth + 1, :, y, :] = rows.reshape(depth, EDGE, channels)

    unrolled(raw_ref, mask_ref, store)
    planes_ref[1 : depth + 1] = rim[1 : depth + 1].reshape(depth, 64, channels).astype(BF)
    lines_ref[...] = jnp.zeros(lines_ref.shape, BF)
    cut_lines(owner, inner_ref, outer_ref, lines_ref, planes_ref, rim)


def grad_lines_kernel(owner, inner_ref, x_ref, outer_ref, bias_ref, *refs):
    *got_refs, lines_ref, planes_ref, rim = refs
    depth, _, channels = x_ref.shape
    planes_ref[1 : depth + 1] = x_ref[...]
    rim[1 : depth + 1] = x_ref[...].reshape(depth, EDGE, EDGE, channels).astype(F32)
    lines_ref[...] = jnp.zeros(lines_ref.shape, BF)
    terms = bias_ref[0].astype(F32)
    for ref in got_refs:
        terms = terms + ref[ref.shape[0] - 1].astype(F32)
    low = split_in_three(terms[0:1] + terms[2:3] + terms[4:5])
    high = split_in_three(terms[1:2] + terms[3:4] + terms[5:6])
    rows = [jnp.concatenate([a, b[:, : channels - 128]], axis=1) for a, b in zip(low, high)]
    extra = jnp.concatenate(rows + [jnp.zeros((EDGE - 3, channels), F32)], axis=0).astype(BF)
    for q in range(lines_ref.shape[0]):
        lines_ref[q, depth + 2] = extra
    cut_lines(owner, inner_ref, outer_ref, lines_ref, planes_ref, rim)


def gather_windows(owner, x_ref, recv_ref, rim, patch):
    thick, _, channels = x_ref.shape
    rim[:, 1:9, 8:16, :] = x_ref[...].reshape(thick, EDGE, EDGE, channels).astype(F32)
    spot = placed_at(owner)
    lines = [
        recv_ref[owner[neighbour(spot, step)[1]], :thick].astype(F32) for step in STEPS
    ]
    rim[:, 1:9, 16, :] = lines[0]
    rim[:, 1:9, 7, :] = lines[1]
    rim[:, 9, 8:16, :] = lines[2]
    rim[:, 0, 8:16, :] = lines[3]
    rim[:, 9, 16, :] = lines[4][:, 0]
    rim[:, 9, 7, :] = lines[5][:, 0]
    rim[:, 0, 16, :] = lines[6][:, 7]
    rim[:, 0, 7, :] = lines[7][:, 7]

    def plane(z, carry):
        for dx in range(3):
            for dy in range(3):
                seen = rim[z, dx : dx + 8, 7 + dy : 15 + dy, :]
                row = pl.multiple_of(z * 64, 64)
                patch[dx * 3 + dy, pl.ds(row, 64), :] = seen.reshape(64, channels).astype(BF)
        return carry

    lax.fori_loop(0, thick, plane, 0)


def forward_kernel(share, regions, n_leaves, owner, x_ref, recv_ref, w_ref, bias_ref,
                   cot_ref, mask_ref, act_ref, gp_ref, gb_ref, gw_ref, rim, patch, cot):
    voxels, channels = gp_ref.shape

    def store(y, rows):
        cot[:, y, :] = rows

    unrolled(cot_ref, mask_ref, store)
    gather_windows(owner, x_ref, recv_ref, rim, patch)
    pre = jnp.broadcast_to(bias_ref[...], (voxels, channels))
    for dz in range(3):
        for k in range(9):
            pre += jnp.dot(
                patch[k, dz * 64 : dz * 64 + voxels, :],
                w_ref[dz * 9 + k],
                preferred_element_type=F32,
            )
    sigma = jax.nn.sigmoid(pre)
    upstream = cot[...].reshape(voxels, channels)
    grad = (upstream * sigma * (1.0 + pre * (1.0 - sigma))).astype(BF)
    gp_ref[...] = grad
    cot[...] = (pre * sigma).reshape(cot.shape)
    act_ref[...] = rolled(cot, mask_ref)
    rest = jnp.sum(grad.astype(F32), axis=0, keepdims=True)
    rows = []
    for term in split_in_three(rest):
        tail = jnp.zeros((1, 256 - channels), F32)
        rows += [term[:, :128], jnp.concatenate([term[:, 128:], tail], axis=1)]
    rows.append(jnp.zeros((ROWS - len(rows), 128), F32))
    gb_ref[0] = jnp.concatenate(rows, axis=0).astype(BF)
    half = channels // 2
    per_offset = half // ROWS
    lanes = 2 * channels // 128
    code = leaf_codes(owner.shape[0])

    slab = lax.axis_index("region")

    def put(unit, value):
        part, inner = divmod(unit, share)
        leaf, level = divmod(part, regions)
        colour = (leaf // (n_leaves // 4)) % 2
        gw_ref[((leaf ^ code[colour]) * regions + (level ^ slab)) * share + inner] = value

    for dz in range(3):
        for k in range(9):
            o = dz * 9 + k
            part = lax.dot_general(
                patch[k, dz * 64 : dz * 64 + voxels, :],
                grad,
                (((0,), (0,)), ((), ())),
                preferred_element_type=F32,
            )
            wide = jnp.concatenate([part[:half], part[half:]], axis=1).astype(BF)
            for rows in range(per_offset):
                for lane in range(lanes):
                    put(
                        (o * per_offset + rows) * lanes + lane,
                        wide[rows * ROWS : (rows + 1) * ROWS, lane * 128 : (lane + 1) * 128],
                    )
    for unit in range(27 * per_offset * lanes, share * regions * n_leaves):
        put(unit, jnp.zeros((ROWS, 128), BF))


def input_kernel(owner, x_ref, recv_ref, w_ref, mask_ref, out_ref, gb_ref, rim, patch, rows):
    channels = w_ref.shape[1]
    voxels = (x_ref.shape[0] - 2) * 64
    gather_windows(owner, x_ref, recv_ref, rim, patch)
    last = recv_ref.shape[1] - 1
    terms = recv_ref[0, last].astype(F32)
    for q in range(1, recv_ref.shape[0]):
        terms = terms + recv_ref[q, last].astype(F32)
    gb_ref[...] = jnp.sum(terms, axis=0, keepdims=True)
    total = jnp.zeros((voxels, channels), F32)
    for dz in range(3):
        for k in range(9):
            total += lax.dot_general(
                patch[8 - k, (2 - dz) * 64 : (2 - dz) * 64 + voxels, :],
                w_ref[dz * 9 + k],
                (((1,), (1,)), ((), ())),
                preferred_element_type=F32,
            )
    rows[...] = total.reshape(rows.shape)
    out_ref[...] = rolled(rows, mask_ref)


def unfold_kernel(share, regions, n_leaves, owner, *refs):
    *pieces, out_ref, flat = refs
    code = leaf_codes(owner.shape[0])
    slab = lax.axis_index("region")
    part = 0
    for piece in pieces:
        for first in range(0, piece.shape[0], share):
            rel, level = divmod(part, regions)
            colour = (rel // (n_leaves // 4)) % 2
            row = ((rel ^ code[colour]) * regions + (level ^ slab)) * (share * ROWS)
            block = piece[first : first + share]
            flat[pl.ds(pl.multiple_of(row, ROWS), share * ROWS), :] = block.reshape(
                share * ROWS, 128
            ).astype(F32)
            part += 1
    pitch = out_ref.shape[1] // 128
    low = lax.broadcasted_iota(jnp.int32, (8, 128), 1) < 64

    def turned(x):
        return pltpu.roll(x, 64, 1)

    def block(base, group):
        rows = []
        for i in range(2):
            rows.append(
                [
                    flat[pl.ds(base + i + lane * ROWS + group * 8 * pitch, 8, stride=pitch), :]
                    for lane in range(3)
                ]
            )
        (a0, a1, a2), (b0, b1, b2) = rows
        rb0, rb1, ra1, ra2 = turned(b0), turned(b1), turned(a1), turned(a2)
        return (
            a0,
            jnp.where(low, a1, rb0),
            jnp.where(low, rb0, rb1),
            jnp.where(low, ra1, ra2),
            jnp.where(low, ra2, b1),
            b2,
        )

    count = out_ref.shape[0]
    span = out_ref.shape[1] // 2

    def pair(m, carry):
        i = m * 2
        base = (i // ROWS) * (3 * ROWS) + i % ROWS
        for top in range(0, count, 16):
            tiles = [block(base, top // 8), block(base, top // 8 + 1)]
            high = min(16, count - top)
            for n in range(6):
                both = jnp.concatenate([tiles[0][n], tiles[1][n]], axis=0).astype(BF)
                lane = pl.multiple_of((n // 3) * span + m * 384 + (n % 3) * 128, 128)
                out_ref[top : top + high, pl.ds(lane, 128)] = both[:high]
        return carry

    lax.fori_loop(0, span // 384, pair, 0, unroll=8)


def body(features, mask, owner, weight, bias, cotangent):
    channels = bias.shape[0]
    depth = features.shape[0]
    voxels = depth * 64
    regions = lax.axis_size("region")
    tiles = lax.axis_size("batch")
    bits = tiles.bit_length() - 1
    slab = lax.axis_index("region")
    orders = send_orders(tiles)
    n_leaves = 2 * tiles
    units = 27 * (channels // 2 // ROWS) * (2 * channels // 128)
    leaf_units = -(-units // (n_leaves * regions)) * regions
    share = leaf_units // regions
    barrier = lax.optimization_barrier

    odd = slab & 1
    joined = [[(i, i ^ 1) for i in range(regions)]]
    joined.append([(i, i + 1 - 2 * (1 - i % 2)) for i in range(1, regions - 1)])

    def rims(plane):
        top = depth - 1
        inner = lax.ppermute(plane(top * (1 - odd)), "region", joined[0])
        outer = lax.ppermute(plane(top * odd), "region", joined[1])
        return inner, outer

    def cut(kernel, extra_planes, operands):
        return pl.pallas_call(
            kernel,
            out_shape=(
                jax.ShapeDtypeStruct((tiles, depth + 2 + extra_planes, EDGE, channels), BF),
                jax.ShapeDtypeStruct((depth + 2, 64, channels), BF),
            ),
            in_specs=[SMEM] + [VMEM] * len(operands),
            out_specs=(VMEM, VMEM),
            scratch_shapes=[pltpu.VMEM((depth + 2, EDGE, EDGE, channels), F32)],
            compiler_params=vmem(12),
        )(owner, *operands)

    def exchanged(lines):
        return lax.all_to_all(lines, "batch", 0, 0, tiled=True)

    scratch = [
        pltpu.VMEM((depth + 2, 10, 24, channels), F32),
        pltpu.VMEM((9, (depth + 2) * 64, channels), BF),
        pltpu.VMEM((depth * EDGE, EDGE, channels), F32),
    ]
    marks = mask.reshape(depth * EDGE, EDGE)
    flat = (depth * EDGE, EDGE * channels)

    def own_plane(z):
        seen = lax.dynamic_slice_in_dim(features, z, 1, 0).reshape(1, 64, channels)
        kept = lax.dynamic_slice_in_dim(mask, z, 1, 0).reshape(1, 64, 1)
        return seen * kept.astype(BF)

    inner, outer = rims(own_plane)
    lines, planes = cut(input_lines_kernel, 0, (inner, features.reshape(flat), marks, outer))
    lines, weight = barrier((lines, weight))
    arrived = exchanged(lines)
    kernel = weight.reshape(27, channels, channels)

    act, grad, bias_terms, terms = pl.pallas_call(
        functools.partial(forward_kernel, share, regions, n_leaves),
        out_shape=(
            jax.ShapeDtypeStruct(flat, BF),
            jax.ShapeDtypeStruct((voxels, channels), BF),
            jax.ShapeDtypeStruct((1, ROWS, 128), BF),
            jax.ShapeDtypeStruct((n_leaves * leaf_units, ROWS, 128), BF),
        ),
        in_specs=[SMEM] + [VMEM] * 6,
        out_specs=(VMEM, VMEM, VMEM, VMEM),
        scratch_shapes=scratch,
        compiler_params=vmem(24),
        cost_estimate=pl.CostEstimate(
            flops=4 * 27 * voxels * channels * channels,
            bytes_accessed=6 << 20,
            transcendentals=voxels * channels,
        ),
    )(owner, planes, arrived, kernel, bias.reshape(1, channels), cotangent.reshape(flat), marks)
    grad = grad.reshape(depth, 64, channels)

    def halve(x, axis, count, flip):
        half = x.shape[0] // 2
        got = lax.ppermute(x[half:].astype(BF), axis, pairs(count, flip))
        return x[:half].astype(F32) + got.astype(F32)

    parts = halve(terms, "batch", tiles, 1)
    split = parts.shape[0] // 2
    colours = [parts[:split], parts[split:]]
    inner, outer = rims(lambda z: lax.dynamic_slice_in_dim(grad, z, 1, 0))
    for step in range(bits - 1):
        colours = [halve(c, "batch", tiles, 1 << o[step]) for c, o in zip(colours, orders)]
        if step == 0:
            colours, inner, outer = barrier((colours, inner, outer))

    def level(k):
        return [c[k * share : (k + 1) * share] for c in colours]

    total = jnp.concatenate(level(0), axis=0)
    gots = []
    for flip in sorted(range(1, regions), key=lambda f: -f):
        sent = jnp.concatenate([x.astype(BF) for x in level(flip)] + [bias_terms], axis=0)
        gots.append(lax.ppermute(sent, "region", pairs(regions, flip)))
        total = total + gots[-1][:-1].astype(F32)
    total = total.astype(BF)
    lines, grad_planes = cut(grad_lines_kernel, 1, (inner, grad, outer, bias_terms, *gots))
    arrived = exchanged(lines)

    held = [total] + [
        lax.ppermute(total, "region", pairs(regions, flip)) for flip in range(1, regions)
    ]
    grad_input, total_bias = pl.pallas_call(
        input_kernel,
        out_shape=(
            jax.ShapeDtypeStruct(flat, BF),
            jax.ShapeDtypeStruct((1, channels), F32),
        ),
        in_specs=[SMEM] + [VMEM] * 4,
        out_specs=(VMEM, VMEM),
        scratch_shapes=scratch,
        compiler_params=vmem(20),
        cost_estimate=pl.CostEstimate(
            flops=2 * 27 * voxels * channels * channels, bytes_accessed=3 << 20, transcendentals=0
        ),
    )(owner, grad_planes, arrived, kernel, marks)

    colours = [
        [jnp.concatenate([h[c * share : (c + 1) * share] for h in held], axis=0)] for c in range(2)
    ]
    for step in reversed(range(bits - 1)):
        colours = [
            c + [lax.ppermute(x, "batch", pairs(tiles, 1 << o[step])) for x in c]
            for c, o in zip(colours, orders)
        ]
        if step == bits - 2:
            first = [c[1] for c in colours]
            first, grad_input = barrier((first, grad_input))
            colours = [[c[0], f] for c, f in zip(colours, first)]
    near = colours[0] + colours[1]
    far = [lax.ppermute(c, "batch", pairs(tiles, 1)) for c in near]
    kernel_grad = pl.pallas_call(
        functools.partial(unfold_kernel, share, regions, n_leaves),
        out_shape=jax.ShapeDtypeStruct((27, channels * channels), BF),
        in_specs=[SMEM] + [VMEM] * len(near + far),
        out_specs=VMEM,
        scratch_shapes=[pltpu.VMEM((max(32 * units // 27, n_leaves * leaf_units) * ROWS, 128), F32)],
        compiler_params=vmem(20),
    )(owner, *near, *far)

    shape = features.shape
    return act.reshape(shape), grad_input.reshape(shape), kernel_grad, total_bias.reshape(channels)


def solution(mesh):
    split = P("region", "batch", None)
    return jax.shard_map(
        body,
        mesh=mesh,
        in_specs=(split, P("region", "batch"), P(), P(), P(), split),
        out_specs=(split, split, P(), P()),
        check_vma=False,
    )
```

time: 111 us -> 101 us (0.910)
  other arithmetic: 6.58 us -> 2.26 us
  local copies, waits for them, and re-layouts: 15.8 us -> 11.8 us
  starting transfers between devices: 38.8 us -> 35.7 us
  Pallas kernels: 19.2 us -> 21.7 us
    ppermute x5, waiting for transfers between devices: 4.77 us -> 10.9 us  [halve(): got = lax.ppermute(x[half:].astype(BF), axis, pairs(count, flip))]
    all_to_all x2, waiting for transfers between devices: 11.9 us -> 6.5 us  [exchanged(): return lax.all_to_all(lines, 'batch', 0, 0, tiled=True)]
    ppermute x3, waiting for transfers between devices: 4.41 us -> 0.01 us  [body(): lax.ppermute(total, 'region', pairs(regions, flip))]
    ppermute x13, starting transfers between devices: 22.2 us -> 19 us  [the longest x2 7.87 us: rims(): inner = lax.ppermute(plane(top * (1 - odd)), 'region', joined[0])]
    reshape x6 -> x3, local copies, waits for them, and re-layouts: 3.7 us -> 0.96 us  [the longest x1 0.76 us: body(): marks = mask.reshape(depth * EDGE, EDGE)]
    mul x5 -> x2, other arithmetic: 2.85 us -> 0.15 us  [own_plane(): return seen * kept.astype(BF)]
    pallas_call x5, Pallas kernels: 19.2 us -> 21.7 us  [the longest x1 8.62 us: body(): pl.pallas_call(functools.partial(forward_kernel, share, regions, n_leaves...]
    ppermute x13, waiting for transfers between devices: 7.2 us -> 9.08 us  [the longest x6 3.98 us: body(): lax.ppermute(x, 'batch', pairs(tiles, 1 << o[step]))]
  transfers between devices with their start and end apart: 27 -> 31, of which waited for: 14 -> 14; matrix products, arithmetic and copies ran while one was open for 13% -> 7% of each run, Pallas kernels for 4% -> 5%
where the time goes in v2:
time: 101 us; the launch traced here: 99.9 us
  starting transfers between devices  35.7 us (35%)
  waiting for transfers between devices  27.5 us (27%)
  Pallas kernels  21.7 us (21%)
  local copies, waits for them, and re-layouts  11.8 us (12%)
  other arithmetic  2.26 us (2%)
    ppermute x5, waiting for transfers between devices, halve(): got = lax.ppermute(x[half:].astype(BF), axis, pairs(count, flip))  10.9 us
    pallas_call x1, Pallas kernels, body(): pl.pallas_call(functools.partial(forward_kernel, share, regions, n_leaves...  8.62 us
    ppermute x2, starting transfers between devices, rims(): inner = lax.ppermute(plane(top * (1 - odd)), 'region', joined[0])  7.87 us
    all_to_all x2, starting transfers between devices, exchanged(): return lax.all_to_all(lines, 'batch', 0, 0, tiled=True)  7.23 us
    all_to_all x2, waiting for transfers between devices, exchanged(): return lax.all_to_all(lines, 'batch', 0, 0, tiled=True)  6.5 us
    pallas_call x1, Pallas kernels, body(): pl.pallas_call(functools.partial(unfold_kernel, share, regions, n_leaves)...  5.84 us
    ppermute x6, starting transfers between devices, body(): lax.ppermute(x, 'batch', pairs(tiles, 1 << o[step]))  5.35 us
    unnamed x20, local copies, waits for them, and re-layouts  4.79 us
  transfers between devices with their start and end apart: 31, of which 14 were waited for; matrix products, arithmetic and copies ran while one was open for 7% of the time, Pallas kernels for 5%

profile of v2, /device:TPU:0, one launch (start us, length us, event | category | flops | bytes accessed | tf_op | source)
XLA Modules:
  0.0 99.9 jit_solution(13004320870902198935)
XLA Ops:
  0.6 0.8 constant_dynamic-slice_fusion.3
  1.4 0.1 reshape.128
  1.5 0.8 fusion.6
  2.3 0.1 broadcast_multiply_fusion
  2.4 0.7 collective-permute-start.1
  3.0 0.1 reshape.125
  3.1 0.1 broadcast_multiply_fusion.1
  3.2 5.9 %collective-permute-start = (bf16[1,64,192]{2,1,0:T(8,128)(2,1)S(1)}, bf16[1,64,192]{2,1,0:T(8,128)(2,1)S(1)}, u32[]{:S(2)}, u32[]{:S(2)}) collective-permute-start(bf16[1,64,192]{2,1,0:T(8,128)(2,1)S(1)} %broadcast_multiply_fusion.1), channel_id=1, source_target_pairs={{0,8},{8,0},{16,24},{24,16},{1,9},{9,1},{17,25},{25,17},{2,10},{10... | collective-permute-start | bytes 73736 | tf_op jit(solution)/shard_map/ppermute | solution.py:329
  9.1 0.8 reshape.127.mask_ref
  9.8 1.1 %collective-permute-done.inner_ref = bf16[1,64,192]{2,1,0:T(8,128)(2,1)S(1)} collective-permute-done((bf16[1,64,192]{2,1,0:T(8,128)(2,1)S(1)}, bf16[1,64,192]{2,1,0:T(8,128)(2,1)S(1)}, u32[]{:S(2)}, u32[]{:S(2)}) %collective-permute-start) | collective-permute-done | bytes 24608 | tf_op jit(solution)/shard_map/ppermute | solution.py:329
  11.0 0.9 copy-done.1
  11.9 0.7 copy-done.4
  12.5 2.4 %shard_map.93 = (bf16[8,10,8,192]{3,2,1,0:T(8,128)(2,1)}, bf16[10,64,192]{2,1,0:T(8,128)(2,1)S(1)}) custom-call(s32[8]{0:T(128)S(1)} %copy-done.4, bf16[1,64,192]{2,1,0:T(8,128)(2,1)S(1)} %collective-permute-done.inner_ref, bf16[64,1536]{1,0:T(8,128)(2,1)S(1)} %bitcast.13, s32[64,8]{1,0:T(8,128)S(1)} %reshape.127.mask_ref, ...), custom_call_target="tpu_custom_call" | custom-call | tf_op jit(solution)/shard_map/pallas_call | solution.py:334
  14.9 3.6 %all-to-all-start = ((bf16[8,10,8,192]{3,2,1,0:T(8,128)(2,1)}), bf16[8,10,8,192]{3,2,1,0:T(8,128)(2,1)S(1)}, u32[]{:S(2)}, u32[]{:S(2)}) async-start(bf16[8,10,8,192]{3,2,1,0:T(8,128)(2,1)} %get-tuple-element.25), calls=%async_computation | async-start | bytes 655360 | tf_op jit(solution)/shard_map/all_to_all | solution.py:347
  18.6 4.4 %reshape.129.w_ref = bf16[27,192,192]{2,1,0:T(8,128)(2,1)S(1)} reshape(bf16[27,36864]{1,0:T(8,128)(2,1)} %param.9) | data formatting | bytes 3981312 | tf_op jit(solution)/shard_map/reshape | solution.py:366
  22.9 3.2 %all-to-all-done.recv_ref = bf16[8,10,8,192]{3,2,1,0:T(8,128)(2,1)S(1)} async-done(((bf16[8,10,8,192]{3,2,1,0:T(8,128)(2,1)}), bf16[8,10,8,192]{3,2,1,0:T(8,128)(2,1)S(1)}, u32[]{:S(2)}, u32[]{:S(2)}) %all-to-all-start) | async-done | bytes 245792 | tf_op jit(solution)/shard_map/all_to_all | solution.py:347
  26.2 8.6 %shard_map.94 = (bf16[64,1536]{1,0:T(8,128)(2,1)}, bf16[512,192]{1,0:T(8,128)(2,1)S(1)}, bf16[1,16,128]{2,1,0:T(8,128)(2,1)S(1)}, bf16[512,16,128]{2,1,0:T(8,128)(2,1)S(1)}) custom-call(s32[8]{0:T(128)S(1)} %copy-done.5, bf16[10,64,192]{2,1,0:T(8,128)(2,1)S(1)} %get-tuple-element.23.x_ref, bf16[8,10,8,192]{3,2,1,0:T(8,128)(2,1)S(1)} %all-to-all-done.recv_ref, ...), custom_call_target="tpu_custom_call" | custom-call | flops 2038431744 | bytes 6291456 | tf_op jit(solution)/shard_map/pallas_call | solution.py:368
  34.8 0.2 slice.104
  35.0 0.1 collective-permute-start.2
  35.1 2.6 %collective-permute-done.2 = bf16[256,16,128]{2,1,0:T(8,128)(2,1)S(1)} collective-permute-done((bf16[256,16,128]{2,1,0:T(8,128)(2,1)S(1)}, bf16[256,16,128]{2,1,0:T(8,128)(2,1)S(1)}, u32[]{:S(2)}, u32[]{:S(2)}) %collective-permute-start.2) | collective-permute-done | bytes 1048608 | tf_op jit(solution)/shard_map/ppermute | solution.py:390
  37.7 0.3 fusion.7
  38.0 0.6 collective-permute-start.3
  38.7 0.6 collective-permute-start.4
  39.2 2.0 %collective-permute-start.5 = (bf16[1,64,192]{2,1,0:T(8,128)(2,1)S(1)}, bf16[1,64,192]{2,1,0:T(8,128)(2,1)S(1)}, u32[]{:S(2)}, u32[]{:S(2)}) collective-permute-start(bf16[1,64,192]{2,1,0:T(8,128)(2,1)S(1)} %get-tuple-element.53), channel_id=1, source_target_pairs={{0,8},{8,0},{16,24},{24,16},{1,9},{9,1},{17,25},{25,17},{2,10},{10... | collective-permute-start | bytes 73736 | tf_op jit(solution)/shard_map/ppermute | solution.py:329
  41.3 0.7 collective-permute-start.6
  41.9 4.5 %collective-permute-done.3 = bf16[64,16,128]{2,1,0:T(8,128)(2,1)S(1)} collective-permute-done((bf16[64,16,128]{2,1,0:T(8,128)(2,1)S(1)}, bf16[64,16,128]{2,1,0:T(8,128)(2,1)S(1)}, u32[]{:S(2)}, u32[]{:S(2)}) %collective-permute-start.3) | collective-permute-done | bytes 262176 | tf_op jit(solution)/shard_map/ppermute | solution.py:390
  46.5 0.3 collective-permute-done.4
  46.7 0.1 slice_add_fusion
  46.9 0.6 collective-permute-start.7
  47.6 1.5 %collective-permute-start.8 = (bf16[32,16,128]{2,1,0:T(8,128)(2,1)S(1)}, bf16[32,16,128]{2,1,0:T(8,128)(2,1)S(1)}, u32[]{:S(2)}, u32[]{:S(2)}) collective-permute-start(bf16[32,16,128]{2,1,0:T(8,128)(2,1)S(1)} %slice.169), channel_id=1, source_target_pairs={{0,2},{1,3},{2,0},{3,1},{4,6},{5,7},{6,4},{7,5},{8,10},{9,11},{10,... | collective-permute-start | bytes 393224 | tf_op jit(solution)/shard_map/ppermute | solution.py:390
  49.1 2.9 %collective-permute-done.7 = bf16[32,16,128]{2,1,0:T(8,128)(2,1)S(1)} collective-permute-done((bf16[32,16,128]{2,1,0:T(8,128)(2,1)S(1)}, bf16[32,16,128]{2,1,0:T(8,128)(2,1)S(1)}, u32[]{:S(2)}, u32[]{:S(2)}) %collective-permute-start.7) | collective-permute-done | bytes 131104 | tf_op jit(solution)/shard_map/ppermute | solution.py:390
  52.0 0.6 collective-permute-done.8
  52.7 2.0 %collective-permute-start.10 = (bf16[17,16,128]{2,1,0:T(8,128)(2,1)S(1)}, bf16[17,16,128]{2,1,0:T(8,128)(2,1)S(1)}, u32[]{:S(2)}, u32[]{:S(2)}) collective-permute-start(bf16[17,16,128]{2,1,0:T(8,128)(2,1)S(1)} %get-tuple-element.71), channel_id=1, source_target_pairs={{0,16},{8,24},{16,0},{24,8},{1,17},{9,25},{17,1},{25,9},{2,18},{10... | collective-permute-start | bytes 208904 | tf_op jit(solution)/shard_map/ppermute | solution.py:409
  54.7 0.2 collective-permute-start.11
  54.9 2.3 %collective-permute-start.9 = (bf16[17,16,128]{2,1,0:T(8,128)(2,1)S(1)}, bf16[17,16,128]{2,1,0:T(8,128)(2,1)S(1)}, u32[]{:S(2)}, u32[]{:S(2)}) collective-permute-start(bf16[17,16,128]{2,1,0:T(8,128)(2,1)S(1)} %get-tuple-element.70), channel_id=1, source_target_pairs={{0,24},{8,16},{16,8},{24,0},{1,25},{9,17},{17,9},{25,1},{2,26},{10... | collective-permute-start | bytes 208904 | tf_op jit(solution)/shard_map/ppermute | solution.py:409
  57.2 1.1 %collective-permute-done.10.refs_1_ = bf16[17,16,128]{2,1,0:T(8,128)(2,1)S(1)} collective-permute-done((bf16[17,16,128]{2,1,0:T(8,128)(2,1)S(1)}, bf16[17,16,128]{2,1,0:T(8,128)(2,1)S(1)}, u32[]{:S(2)}, u32[]{:S(2)}) %collective-permute-start.10) | collective-permute-done | bytes 69664 | tf_op jit(solution)/shard_map/ppermute | solution.py:409
  58.3 0.7 collective-permute-done.11.refs_2_
  59.0 2.1 %collective-permute-done.9.refs_0_ = bf16[17,16,128]{2,1,0:T(8,128)(2,1)S(1)} collective-permute-done((bf16[17,16,128]{2,1,0:T(8,128)(2,1)S(1)}, bf16[17,16,128]{2,1,0:T(8,128)(2,1)S(1)}, u32[]{:S(2)}, u32[]{:S(2)}) %collective-permute-start.9) | collective-permute-done | bytes 69664 | tf_op jit(solution)/shard_map/ppermute | solution.py:409
  61.2 0.7 collective-permute-start.12
  61.9 2.5 %collective-permute-start.13 = (bf16[16,16,128]{2,1,0:T(8,128)(2,1)S(1)}, bf16[16,16,128]{2,1,0:T(8,128)(2,1)S(1)}, u32[]{:S(2)}, u32[]{:S(2)}) collective-permute-start(bf16[16,16,128]{2,1,0:T(8,128)(2,1)S(1)} %fusion.2), channel_id=1, source_target_pairs={{0,16},{8,24},{16,0},{24,8},{1,17},{9,25},{17,1},{25,9},{2,18},{10... | collective-permute-start | bytes 196616 | tf_op jit(solution)/shard_map/ppermute | solution.py:416
  64.4 1.2 %collective-permute-start.14 = (bf16[16,16,128]{2,1,0:T(8,128)(2,1)S(1)}, bf16[16,16,128]{2,1,0:T(8,128)(2,1)S(1)}, u32[]{:S(2)}, u32[]{:S(2)}) collective-permute-start(bf16[16,16,128]{2,1,0:T(8,128)(2,1)S(1)} %fusion.2), channel_id=1, source_target_pairs={{0,24},{8,16},{16,8},{24,0},{1,25},{9,17},{17,9},{25,1},{2,26},{10... | collective-permute-start | bytes 196616 | tf_op jit(solution)/shard_map/ppermute | solution.py:416
  65.6 0.6 fusion.13
  66.2 1.0 %shard_map.95 = (bf16[8,11,8,192]{3,2,1,0:T(8,128)(2,1)S(1)}, bf16[10,64,192]{2,1,0:T(8,128)(2,1)S(1)}) custom-call(s32[8]{0:T(128)S(1)} %copy-done.5, bf16[1,64,192]{2,1,0:T(8,128)(2,1)S(1)} %collective-permute-done.5.inner_ref, bf16[8,64,192]{2,1,0:T(8,128)(2,1)S(1)} %bitcast.12, bf16[1,64,192]{2,1,0:T(8,128)(2,1)S(1)} %collective-permute-done.6.outer_ref, ...), custom_call_target="tpu_custom_call" | custom-call | tf_op jit(solution)/shard_map/pallas_call | solution.py:334
  67.3 0.7 copy-done
  68.0 0.7 copy-done.6
  68.7 3.6 %all-to-all-start.1 = ((bf16[8,11,8,192]{3,2,1,0:T(8,128)(2,1)}), bf16[8,11,8,192]{3,2,1,0:T(8,128)(2,1)S(1)}, u32[]{:S(2)}, u32[]{:S(2)}) async-start(bf16[8,11,8,192]{3,2,1,0:T(8,128)(2,1)} %copy-done), calls=%async_computation.1 | async-start | bytes 720896 | tf_op jit(solution)/shard_map/all_to_all | solution.py:347
  72.5 2.0 %collective-permute-start.16 = (bf16[32,16,128]{2,1,0:T(8,128)(2,1)S(1)}, bf16[32,16,128]{2,1,0:T(8,128)(2,1)S(1)}, u32[]{:S(2)}, u32[]{:S(2)}) collective-permute-start(bf16[32,16,128]{2,1,0:T(8,128)(2,1)S(1)} %pad_maximum_fusion.1.refs_4_), channel_id=1, source_target_pairs={{0,2},{1,3},{2,0},{3,1},{4,6},{5,7},{6,4},{7,5},{8,10},{9,11},{10,... | collective-permute-start | bytes 393224 | tf_op jit(solution)/shard_map/ppermute | solution.py:438
  74.4 1.5 %collective-permute-start.19 = (bf16[32,16,128]{2,1,0:T(8,128)(2,1)S(1)}, bf16[32,16,128]{2,1,0:T(8,128)(2,1)S(1)}, u32[]{:S(2)}, u32[]{:S(2)}) collective-permute-start(bf16[32,16,128]{2,1,0:T(8,128)(2,1)S(1)} %pad_maximum_fusion.1.refs_4_), channel_id=1, source_target_pairs={{0,4},{1,5},{2,6},{3,7},{4,0},{5,1},{6,2},{7,3},{8,12},{9,13},{10,... | collective-permute-start | bytes 393224 | tf_op jit(solution)/shard_map/ppermute | solution.py:438
  75.9 0.8 pad_maximum_fusion.refs_0_
  76.7 0.6 collective-permute-start.15
  77.3 0.2 collective-permute-start.17
  77.5 3.3 %all-to-all-done.1.recv_ref = bf16[8,11,8,192]{3,2,1,0:T(8,128)(2,1)S(1)} async-done(((bf16[8,11,8,192]{3,2,1,0:T(8,128)(2,1)}), bf16[8,11,8,192]{3,2,1,0:T(8,128)(2,1)S(1)}, u32[]{:S(2)}, u32[]{:S(2)}) %all-to-all-start.1) | async-done | bytes 270368 | tf_op jit(solution)/shard_map/all_to_all | solution.py:347
  80.7 0.8 copy-done.3
  81.5 1.0 copy-done.7
  82.5 3.9 %shard_map.96 = (bf16[64,1536]{1,0:T(8,128)(2,1)}, f32[1,192]{1,0:T(1,128)}) custom-call(s32[8]{0:T(128)S(1)} %copy-done.5, bf16[10,64,192]{2,1,0:T(8,128)(2,1)S(1)} %copy-done.7, bf16[8,11,8,192]{3,2,1,0:T(8,128)(2,1)S(1)} %all-to-all-done.1.recv_ref, bf16[27,192,192]{2,1,0:T(8,128)(2,1)S(1)} %reshape.129.w_ref, s32[64,8]{1,0:T(8,128)S(1)} %copy-done.3), custom_call_target="tpu_custom_call" | custom-call | flops 1019215872 | bytes 3145728 | tf_op jit(solution)/shard_map/pallas_call | solution.py:418
  86.3 0.5 collective-permute-start.27
  86.8 0.1 collective-permute-start.18
  87.0 1.0 collective-permute-start.20
  88.0 0.5 collective-permute-start.22
  88.6 4.0 %collective-permute-done.18.refs_3_ = bf16[32,16,128]{2,1,0:T(8,128)(2,1)S(1)} collective-permute-done((bf16[32,16,128]{2,1,0:T(8,128)(2,1)}, bf16[32,16,128]{2,1,0:T(8,128)(2,1)S(1)}, u32[]{:S(2)}, u32[]{:S(2)}) %collective-permute-start.18) | collective-permute-done | bytes 131104 | tf_op jit(solution)/shard_map/ppermute | solution.py:438
  92.5 0.5 collective-permute-start.28
  93.1 0.8 collective-permute-done.24.refs_11_
  93.9 0.2 collective-permute-done.28.refs_15_
  94.1 5.8 %shard_map.97 = bf16[27,36864]{1,0:T(8,128)(2,1)} custom-call(s32[8]{0:T(128)S(1)} %copy-done.5, bf16[32,16,128]{2,1,0:T(8,128)(2,1)S(1)} %pad_maximum_fusion.refs_0_, bf16[32,16,128]{2,1,0:T(8,128)(2,1)} %collective-permute-done.15.refs_1_, bf16[32,16,128]{2,1,0:T(8,128)(2,1)} %collective-permute-done.17.refs_2_, ...), custom_call_target="tpu_custom_call" | custom-call | tf_op jit(solution)/shard_map/pallas_call | solution.py:447
  (51 shorter events, 0.5 us)
Async XLA Ops:
  2.4 7.5 %collective-permute-start.1 = (bf16[1,64,192]{2,1,0:T(8,128)(2,1)S(1)}, bf16[1,64,192]{2,1,0:T(8,128)(2,1)S(1)}, u32[]{:S(2)}, u32[]{:S(2)}) collective-permute-start(bf16[1,64,192]{2,1,0:T(8,128)(2,1)S(1)} %broadcast_multiply_fusion), channel_id=1, source_target_pairs={{8,16},{16,8},{9,17},{17,9},{10,18},{18,10},{11,19},{19,11},{12,20... | collective-permute-start | bytes 73736 | tf_op jit(solution)/shard_map/ppermute | solution.py:330
  3.2 7.7 %collective-permute-start = (bf16[1,64,192]{2,1,0:T(8,128)(2,1)S(1)}, bf16[1,64,192]{2,1,0:T(8,128)(2,1)S(1)}, u32[]{:S(2)}, u32[]{:S(2)}) collective-permute-start(bf16[1,64,192]{2,1,0:T(8,128)(2,1)S(1)} %broadcast_multiply_fusion.1), channel_id=1, source_target_pairs={{0,8},{8,0},{16,24},{24,16},{1,9},{9,1},{17,25},{25,17},{2,10},{10... | collective-permute-start | bytes 73736 | tf_op jit(solution)/shard_map/ppermute | solution.py:329
  9.8 16.4 %copy-start.2 = (s32[64,8]{1,0:T(8,128)}, s32[64,8]{1,0:T(8,128)S(1)}, u32[]{:S(2)}) copy-start(s32[64,8]{1,0:T(8,128)S(1)} %reshape.127.mask_ref) | copy-start | bytes 6148
  10.9 0.9 copy-start.1
  11.9 0.7 copy-start.4
  14.9 11.2 %all-to-all-start = ((bf16[8,10,8,192]{3,2,1,0:T(8,128)(2,1)}), bf16[8,10,8,192]{3,2,1,0:T(8,128)(2,1)S(1)}, u32[]{:S(2)}, u32[]{:S(2)}) async-start(bf16[8,10,8,192]{3,2,1,0:T(8,128)(2,1)} %get-tuple-element.25), calls=%async_computation | async-start | bytes 655360 | tf_op jit(solution)/shard_map/all_to_all | solution.py:347
  18.5 7.6 %copy-start.5 = (s32[8]{0:T(128)S(1)}, s32[8]{0:T(128)}, u32[]{:S(2)}) copy-start(s32[8]{0:T(128)} %owner.9) | copy-start | bytes 100
  18.5 7.6 %copy-start.8 = (bf16[8,8,1536]{2,1,0:T(8,128)(2,1)S(1)}, bf16[8,8,1536]{2,1,0:T(8,128)(2,1)}, u32[]{:S(2)}) copy-start(bf16[8,8,1536]{2,1,0:T(8,128)(2,1)} %param.11) | copy-start | bytes 589828
  18.5 7.6 %copy-start.9 = (f32[192]{0:T(256)S(1)}, f32[192]{0:T(256)}, u32[]{:S(2)}) copy-start(f32[192]{0:T(256)} %param.10) | copy-start | bytes 2308
  35.0 2.7 %collective-permute-start.2 = (bf16[256,16,128]{2,1,0:T(8,128)(2,1)S(1)}, bf16[256,16,128]{2,1,0:T(8,128)(2,1)S(1)}, u32[]{:S(2)}, u32[]{:S(2)}) collective-permute-start(bf16[256,16,128]{2,1,0:T(8,128)(2,1)S(1)} %slice.104), channel_id=1, source_target_pairs={{0,1},{1,0},{2,3},{3,2},{4,5},{5,4},{6,7},{7,6},{8,9},{9,8},{10,11... | collective-permute-start | bytes 3145736 | tf_op jit(solution)/shard_map/ppermute | solution.py:390
  38.0 8.4 %collective-permute-start.3 = (bf16[64,16,128]{2,1,0:T(8,128)(2,1)S(1)}, bf16[64,16,128]{2,1,0:T(8,128)(2,1)S(1)}, u32[]{:S(2)}, u32[]{:S(2)}) collective-permute-start(bf16[64,16,128]{2,1,0:T(8,128)(2,1)S(1)} %get-tuple-element.51), channel_id=1, source_target_pairs={{0,2},{1,3},{2,0},{3,1},{4,6},{5,7},{6,4},{7,5},{8,10},{9,11},{10,... | collective-permute-start | bytes 786440 | tf_op jit(solution)/shard_map/ppermute | solution.py:390
  38.7 8.1 %collective-permute-start.4 = (bf16[64,16,128]{2,1,0:T(8,128)(2,1)S(1)}, bf16[64,16,128]{2,1,0:T(8,128)(2,1)S(1)}, u32[]{:S(2)}, u32[]{:S(2)}) collective-permute-start(bf16[64,16,128]{2,1,0:T(8,128)(2,1)S(1)} %get-tuple-element.50), channel_id=1, source_target_pairs={{0,4},{1,5},{2,6},{3,7},{4,0},{5,1},{6,2},{7,3},{8,12},{9,13},{10,... | collective-permute-start | bytes 786440 | tf_op jit(solution)/shard_map/ppermute | solution.py:390
  39.2 7.6 %collective-permute-start.5 = (bf16[1,64,192]{2,1,0:T(8,128)(2,1)S(1)}, bf16[1,64,192]{2,1,0:T(8,128)(2,1)S(1)}, u32[]{:S(2)}, u32[]{:S(2)}) collective-permute-start(bf16[1,64,192]{2,1,0:T(8,128)(2,1)S(1)} %get-tuple-element.53), channel_id=1, source_target_pairs={{0,8},{8,0},{16,24},{24,16},{1,9},{9,1},{17,25},{25,17},{2,10},{10... | collective-permute-start | bytes 73736 | tf_op jit(solution)/shard_map/ppermute | solution.py:329
  41.3 5.6 %collective-permute-start.6 = (bf16[1,64,192]{2,1,0:T(8,128)(2,1)S(1)}, bf16[1,64,192]{2,1,0:T(8,128)(2,1)S(1)}, u32[]{:S(2)}, u32[]{:S(2)}) collective-permute-start(bf16[1,64,192]{2,1,0:T(8,128)(2,1)S(1)} %get-tuple-element.52), channel_id=1, source_target_pairs={{8,16},{16,8},{9,17},{17,9},{10,18},{18,10},{11,19},{19,11},{12,20... | collective-permute-start | bytes 73736 | tf_op jit(solution)/shard_map/ppermute | solution.py:330
  46.9 5.0 %collective-permute-start.7 = (bf16[32,16,128]{2,1,0:T(8,128)(2,1)S(1)}, bf16[32,16,128]{2,1,0:T(8,128)(2,1)S(1)}, u32[]{:S(2)}, u32[]{:S(2)}) collective-permute-start(bf16[32,16,128]{2,1,0:T(8,128)(2,1)S(1)} %slice.170), channel_id=1, source_target_pairs={{0,4},{1,5},{2,6},{3,7},{4,0},{5,1},{6,2},{7,3},{8,12},{9,13},{10,... | collective-permute-start | bytes 393224 | tf_op jit(solution)/shard_map/ppermute | solution.py:390
  47.6 5.0 %collective-permute-start.8 = (bf16[32,16,128]{2,1,0:T(8,128)(2,1)S(1)}, bf16[32,16,128]{2,1,0:T(8,128)(2,1)S(1)}, u32[]{:S(2)}, u32[]{:S(2)}) collective-permute-start(bf16[32,16,128]{2,1,0:T(8,128)(2,1)S(1)} %slice.169), channel_id=1, source_target_pairs={{0,2},{1,3},{2,0},{3,1},{4,6},{5,7},{6,4},{7,5},{8,10},{9,11},{10,... | collective-permute-start | bytes 393224 | tf_op jit(solution)/shard_map/ppermute | solution.py:390
  52.7 5.6 %collective-permute-start.10 = (bf16[17,16,128]{2,1,0:T(8,128)(2,1)S(1)}, bf16[17,16,128]{2,1,0:T(8,128)(2,1)S(1)}, u32[]{:S(2)}, u32[]{:S(2)}) collective-permute-start(bf16[17,16,128]{2,1,0:T(8,128)(2,1)S(1)} %get-tuple-element.71), channel_id=1, source_target_pairs={{0,16},{8,24},{16,0},{24,8},{1,17},{9,25},{17,1},{25,9},{2,18},{10... | collective-permute-start | bytes 208904 | tf_op jit(solution)/shard_map/ppermute | solution.py:409
  54.7 4.4 %collective-permute-start.11 = (bf16[17,16,128]{2,1,0:T(8,128)(2,1)S(1)}, bf16[17,16,128]{2,1,0:T(8,128)(2,1)S(1)}, u32[]{:S(2)}, u32[]{:S(2)}) collective-permute-start(bf16[17,16,128]{2,1,0:T(8,128)(2,1)S(1)} %get-tuple-element.72), channel_id=1, source_target_pairs={{0,8},{8,0},{16,24},{24,16},{1,9},{9,1},{17,25},{25,17},{2,10},{10... | collective-permute-start | bytes 208904 | tf_op jit(solution)/shard_map/ppermute | solution.py:409
  54.9 6.3 %collective-permute-start.9 = (bf16[17,16,128]{2,1,0:T(8,128)(2,1)S(1)}, bf16[17,16,128]{2,1,0:T(8,128)(2,1)S(1)}, u32[]{:S(2)}, u32[]{:S(2)}) collective-permute-start(bf16[17,16,128]{2,1,0:T(8,128)(2,1)S(1)} %get-tuple-element.70), channel_id=1, source_target_pairs={{0,24},{8,16},{16,8},{24,0},{1,25},{9,17},{17,9},{25,1},{2,26},{10... | collective-permute-start | bytes 208904 | tf_op jit(solution)/shard_map/ppermute | solution.py:409
  61.2 11.2 %collective-permute-start.12 = (bf16[16,16,128]{2,1,0:T(8,128)(2,1)S(1)}, bf16[16,16,128]{2,1,0:T(8,128)(2,1)S(1)}, u32[]{:S(2)}, u32[]{:S(2)}) collective-permute-start(bf16[16,16,128]{2,1,0:T(8,128)(2,1)S(1)} %fusion.2), channel_id=1, source_target_pairs={{0,8},{8,0},{16,24},{24,16},{1,9},{9,1},{17,25},{25,17},{2,10},{10... | collective-permute-start | bytes 196616 | tf_op jit(solution)/shard_map/ppermute | solution.py:416
  61.9 10.5 %collective-permute-start.13 = (bf16[16,16,128]{2,1,0:T(8,128)(2,1)S(1)}, bf16[16,16,128]{2,1,0:T(8,128)(2,1)S(1)}, u32[]{:S(2)}, u32[]{:S(2)}) collective-permute-start(bf16[16,16,128]{2,1,0:T(8,128)(2,1)S(1)} %fusion.2), channel_id=1, source_target_pairs={{0,16},{8,24},{16,0},{24,8},{1,17},{9,25},{17,1},{25,9},{2,18},{10... | collective-permute-start | bytes 196616 | tf_op jit(solution)/shard_map/ppermute | solution.py:416
  64.4 8.0 %collective-permute-start.14 = (bf16[16,16,128]{2,1,0:T(8,128)(2,1)S(1)}, bf16[16,16,128]{2,1,0:T(8,128)(2,1)S(1)}, u32[]{:S(2)}, u32[]{:S(2)}) collective-permute-start(bf16[16,16,128]{2,1,0:T(8,128)(2,1)S(1)} %fusion.2), channel_id=1, source_target_pairs={{0,24},{8,16},{16,8},{24,0},{1,25},{9,17},{17,9},{25,1},{2,26},{10... | collective-permute-start | bytes 196616 | tf_op jit(solution)/shard_map/ppermute | solution.py:416
  67.2 0.7 copy-start
  68.0 0.7 copy-start.6
  68.7 12.0 %all-to-all-start.1 = ((bf16[8,11,8,192]{3,2,1,0:T(8,128)(2,1)}), bf16[8,11,8,192]{3,2,1,0:T(8,128)(2,1)S(1)}, u32[]{:S(2)}, u32[]{:S(2)}) async-start(bf16[8,11,8,192]{3,2,1,0:T(8,128)(2,1)} %copy-done), calls=%async_computation.1 | async-start | bytes 720896 | tf_op jit(solution)/shard_map/all_to_all | solution.py:347
  72.5 13.9 %collective-permute-start.16 = (bf16[32,16,128]{2,1,0:T(8,128)(2,1)S(1)}, bf16[32,16,128]{2,1,0:T(8,128)(2,1)S(1)}, u32[]{:S(2)}, u32[]{:S(2)}) collective-permute-start(bf16[32,16,128]{2,1,0:T(8,128)(2,1)S(1)} %pad_maximum_fusion.1.refs_4_), channel_id=1, source_target_pairs={{0,2},{1,3},{2,0},{3,1},{4,6},{5,7},{6,4},{7,5},{8,10},{9,11},{10,... | collective-permute-start | bytes 393224 | tf_op jit(solution)/shard_map/ppermute | solution.py:438
  74.4 11.9 %collective-permute-start.19 = (bf16[32,16,128]{2,1,0:T(8,128)(2,1)S(1)}, bf16[32,16,128]{2,1,0:T(8,128)(2,1)S(1)}, u32[]{:S(2)}, u32[]{:S(2)}) collective-permute-start(bf16[32,16,128]{2,1,0:T(8,128)(2,1)S(1)} %pad_maximum_fusion.1.refs_4_), channel_id=1, source_target_pairs={{0,4},{1,5},{2,6},{3,7},{4,0},{5,1},{6,2},{7,3},{8,12},{9,13},{10,... | collective-permute-start | bytes 393224 | tf_op jit(solution)/shard_map/ppermute | solution.py:438
  76.7 10.2 %collective-permute-start.15 = (bf16[32,16,128]{2,1,0:T(8,128)(2,1)S(1)}, bf16[32,16,128]{2,1,0:T(8,128)(2,1)}, u32[]{:S(2)}, u32[]{:S(2)}) collective-permute-start(bf16[32,16,128]{2,1,0:T(8,128)(2,1)S(1)} %pad_maximum_fusion.refs_0_), channel_id=1, source_target_pairs={{0,4},{1,5},{2,6},{3,7},{4,0},{5,1},{6,2},{7,3},{8,12},{9,13},{10,... | collective-permute-start | bytes 393224 | tf_op jit(solution)/shard_map/ppermute | solution.py:438
  77.3 9.7 %collective-permute-start.25 = (bf16[32,16,128]{2,1,0:T(8,128)(2,1)S(1)}, bf16[32,16,128]{2,1,0:T(8,128)(2,1)}, u32[]{:S(2)}, u32[]{:S(2)}) collective-permute-start(bf16[32,16,128]{2,1,0:T(8,128)(2,1)S(1)} %pad_maximum_fusion.1.refs_4_), channel_id=1, source_target_pairs={{0,1},{1,0},{2,3},{3,2},{4,5},{5,4},{6,7},{7,6},{8,9},{9,8},{10,11... | collective-permute-start | bytes 393224 | tf_op jit(solution)/shard_map/ppermute | solution.py:446
  77.3 10.7 %collective-permute-start.17 = (bf16[32,16,128]{2,1,0:T(8,128)(2,1)S(1)}, bf16[32,16,128]{2,1,0:T(8,128)(2,1)}, u32[]{:S(2)}, u32[]{:S(2)}) collective-permute-start(bf16[32,16,128]{2,1,0:T(8,128)(2,1)S(1)} %pad_maximum_fusion.refs_0_), channel_id=1, source_target_pairs={{0,2},{1,3},{2,0},{3,1},{4,6},{5,7},{6,4},{7,5},{8,10},{9,11},{10,... | collective-permute-start | bytes 393224 | tf_op jit(solution)/shard_map/ppermute | solution.py:438
  80.7 0.8 copy-start.3
  81.5 1.0 copy-start.7
  86.3 1.7 %collective-permute-start.21 = (bf16[32,16,128]{2,1,0:T(8,128)(2,1)S(1)}, bf16[32,16,128]{2,1,0:T(8,128)(2,1)S(1)}, u32[]{:S(2)}, u32[]{:S(2)}) collective-permute-start(bf16[32,16,128]{2,1,0:T(8,128)(2,1)S(1)} %pad_maximum_fusion.refs_0_), channel_id=1, source_target_pairs={{0,1},{1,0},{2,3},{3,2},{4,5},{5,4},{6,7},{7,6},{8,9},{9,8},{10,11... | collective-permute-start | bytes 393224 | tf_op jit(solution)/shard_map/ppermute | solution.py:446
  86.3 2.2 %collective-permute-start.27 = (bf16[32,16,128]{2,1,0:T(8,128)(2,1)S(1)}, bf16[32,16,128]{2,1,0:T(8,128)(2,1)S(1)}, u32[]{:S(2)}, u32[]{:S(2)}) collective-permute-start(bf16[32,16,128]{2,1,0:T(8,128)(2,1)S(1)} %collective-permute-done.19.refs_6_), channel_id=1, source_target_pairs={{0,1},{1,0},{2,3},{3,2},{4,5},{5,4},{6,7},{7,6},{8,9},{9,8},{10,11... | collective-permute-start | bytes 393224 | tf_op jit(solution)/shard_map/ppermute | solution.py:446
  86.8 5.7 %collective-permute-start.18 = (bf16[32,16,128]{2,1,0:T(8,128)(2,1)}, bf16[32,16,128]{2,1,0:T(8,128)(2,1)S(1)}, u32[]{:S(2)}, u32[]{:S(2)}) collective-permute-start(bf16[32,16,128]{2,1,0:T(8,128)(2,1)} %collective-permute-done.15.refs_1_), channel_id=1, source_target_pairs={{0,2},{1,3},{2,0},{3,1},{4,6},{5,7},{6,4},{7,5},{8,10},{9,11},{10,... | collective-permute-start | bytes 393224 | tf_op jit(solution)/shard_map/ppermute | solution.py:438
  87.0 5.5 %collective-permute-start.20 = (bf16[32,16,128]{2,1,0:T(8,128)(2,1)S(1)}, bf16[32,16,128]{2,1,0:T(8,128)(2,1)S(1)}, u32[]{:S(2)}, u32[]{:S(2)}) collective-permute-start(bf16[32,16,128]{2,1,0:T(8,128)(2,1)S(1)} %collective-permute-done.16.refs_5_), channel_id=1, source_target_pairs={{0,4},{1,5},{2,6},{3,7},{4,0},{5,1},{6,2},{7,3},{8,12},{9,13},{10,... | collective-permute-start | bytes 393224 | tf_op jit(solution)/shard_map/ppermute | solution.py:438
  88.0 5.1 %collective-permute-start.23 = (bf16[32,16,128]{2,1,0:T(8,128)(2,1)}, bf16[32,16,128]{2,1,0:T(8,128)(2,1)S(1)}, u32[]{:S(2)}, u32[]{:S(2)}) collective-permute-start(bf16[32,16,128]{2,1,0:T(8,128)(2,1)} %collective-permute-done.17.refs_2_), channel_id=1, source_target_pairs={{0,1},{1,0},{2,3},{3,2},{4,5},{5,4},{6,7},{7,6},{8,9},{9,8},{10,11... | collective-permute-start | bytes 393224 | tf_op jit(solution)/shard_map/ppermute | solution.py:446
  88.0 5.1 %collective-permute-start.22 = (bf16[32,16,128]{2,1,0:T(8,128)(2,1)}, bf16[32,16,128]{2,1,0:T(8,128)(2,1)S(1)}, u32[]{:S(2)}, u32[]{:S(2)}) collective-permute-start(bf16[32,16,128]{2,1,0:T(8,128)(2,1)} %collective-permute-done.15.refs_1_), channel_id=1, source_target_pairs={{0,1},{1,0},{2,3},{3,2},{4,5},{5,4},{6,7},{7,6},{8,9},{9,8},{10,11... | collective-permute-start | bytes 393224 | tf_op jit(solution)/shard_map/ppermute | solution.py:446
  88.5 4.6 %collective-permute-start.26 = (bf16[32,16,128]{2,1,0:T(8,128)(2,1)S(1)}, bf16[32,16,128]{2,1,0:T(8,128)(2,1)S(1)}, u32[]{:S(2)}, u32[]{:S(2)}) collective-permute-start(bf16[32,16,128]{2,1,0:T(8,128)(2,1)S(1)} %collective-permute-done.16.refs_5_), channel_id=1, source_target_pairs={{0,1},{1,0},{2,3},{3,2},{4,5},{5,4},{6,7},{7,6},{8,9},{9,8},{10,11... | collective-permute-start | bytes 393224 | tf_op jit(solution)/shard_map/ppermute | solution.py:446
  92.5 1.3 %collective-permute-start.24 = (bf16[32,16,128]{2,1,0:T(8,128)(2,1)S(1)}, bf16[32,16,128]{2,1,0:T(8,128)(2,1)S(1)}, u32[]{:S(2)}, u32[]{:S(2)}) collective-permute-start(bf16[32,16,128]{2,1,0:T(8,128)(2,1)S(1)} %collective-permute-done.18.refs_3_), channel_id=1, source_target_pairs={{0,1},{1,0},{2,3},{3,2},{4,5},{5,4},{6,7},{7,6},{8,9},{9,8},{10,11... | collective-permute-start | bytes 393224 | tf_op jit(solution)/shard_map/ppermute | solution.py:446
  92.5 1.5 %collective-permute-start.28 = (bf16[32,16,128]{2,1,0:T(8,128)(2,1)S(1)}, bf16[32,16,128]{2,1,0:T(8,128)(2,1)S(1)}, u32[]{:S(2)}, u32[]{:S(2)}) collective-permute-start(bf16[32,16,128]{2,1,0:T(8,128)(2,1)S(1)} %collective-permute-done.20.refs_7_), channel_id=1, source_target_pairs={{0,1},{1,0},{2,3},{3,2},{4,5},{5,4},{6,7},{7,6},{8,9},{9,8},{10,11... | collective-permute-start | bytes 393224 | tf_op jit(solution)/shard_map/ppermute | solution.py:446

commit v3 on v2

--- a/solution.py
+++ b/solution.py
@@ -12,6 +12,7 @@
 STEPS = ((0, 1), (0, -1), (1, 0), (-1, 0), (1, 1), (1, -1), (-1, 1), (-1, -1))
 EDGE = 8
 ROWS = 16
+PITCH = 17
 VMEM = pl.BlockSpec(memory_space=pltpu.VMEM)
 SMEM = pl.BlockSpec(memory_space=pltpu.SMEM)
 
@@ -103,25 +104,30 @@
             lines_ref[owner[place], :thick] = line
 
 
-def input_lines_kernel(owner, inner_ref, raw_ref, mask_ref, outer_ref, lines_ref, planes_ref, rim):
-    depth = rim.shape[0] - 2
-    channels = rim.shape[3]
-
+def occupied_kernel(owner, raw_ref, mask_ref, out_ref, rows_ref):
     def store(y, rows):
-        rim[1 : depth + 1, :, y, :] = rows.reshape(depth, EDGE, channels)
+        rows_ref[:, y, :] = rows
 
     unrolled(raw_ref, mask_ref, store)
-    planes_ref[1 : depth + 1] = rim[1 : depth + 1].reshape(depth, 64, channels).astype(BF)
-    lines_ref[...] = jnp.zeros(lines_ref.shape, BF)
-    cut_lines(owner, inner_ref, outer_ref, lines_ref, planes_ref, rim)
-
-
-def grad_lines_kernel(owner, inner_ref, x_ref, outer_ref, bias_ref, *refs):
-    *got_refs, lines_ref, planes_ref, rim = refs
+    out_ref[...] = rows_ref[...].reshape(out_ref.shape).astype(BF)
+
+
+def fill_planes(x_ref, planes_ref, lines_ref, rim):
     depth, _, channels = x_ref.shape
     planes_ref[1 : depth + 1] = x_ref[...]
     rim[1 : depth + 1] = x_ref[...].reshape(depth, EDGE, EDGE, channels).astype(F32)
     lines_ref[...] = jnp.zeros(lines_ref.shape, BF)
+
+
+def input_lines_kernel(owner, inner_ref, x_ref, outer_ref, lines_ref, planes_ref, rim):
+    fill_planes(x_ref, planes_ref, lines_ref, rim)
+    cut_lines(owner, inner_ref, outer_ref, lines_ref, planes_ref, rim)
+
+
+def grad_lines_kernel(owner, inner_ref, x_ref, outer_ref, bias_ref, *refs):
+    *got_refs, lines_ref, planes_ref, rim = refs
+    depth, _, channels = x_ref.shape
+    fill_planes(x_ref, planes_ref, lines_ref, rim)
     terms = bias_ref[0].astype(F32)
     for ref in got_refs:
         terms = terms + ref[ref.shape[0] - 1].astype(F32)
@@ -182,8 +188,7 @@
     upstream = cot[...].reshape(voxels, channels)
     grad = (upstream * sigma * (1.0 + pre * (1.0 - sigma))).astype(BF)
     gp_ref[...] = grad
-    cot[...] = (pre * sigma).reshape(cot.shape)
-    act_ref[...] = rolled(cot, mask_ref)
+    act_ref[...] = (pre * sigma).astype(BF)
     rest = jnp.sum(grad.astype(F32), axis=0, keepdims=True)
     rows = []
     for term in split_in_three(rest):
@@ -224,7 +229,8 @@
         put(unit, jnp.zeros((ROWS, 128), BF))
 
 
-def input_kernel(owner, x_ref, recv_ref, w_ref, mask_ref, out_ref, gb_ref, rim, patch, rows):
+def input_kernel(owner, x_ref, recv_ref, w_ref, mask_ref, pre_ref, out_ref, act_ref, gb_ref,
+                 rim, patch, rows):
     channels = w_ref.shape[1]
     voxels = (x_ref.shape[0] - 2) * 64
     gather_windows(owner, x_ref, recv_ref, rim, patch)
@@ -242,6 +248,8 @@
                 (((1,), (1,)), ((), ())),
                 preferred_element_type=F32,
             )
+    rows[...] = pre_ref[...].astype(F32).reshape(rows.shape)
+    act_ref[...] = rolled(rows, mask_ref)
     rows[...] = total.reshape(rows.shape)
     out_ref[...] = rolled(rows, mask_ref)
 
@@ -255,13 +263,11 @@
         for first in range(0, piece.shape[0], share):
             rel, level = divmod(part, regions)
             colour = (rel // (n_leaves // 4)) % 2
-            row = ((rel ^ code[colour]) * regions + (level ^ slab)) * (share * ROWS)
-            block = piece[first : first + share]
-            flat[pl.ds(pl.multiple_of(row, ROWS), share * ROWS), :] = block.reshape(
-                share * ROWS, 128
-            ).astype(F32)
+            row = ((rel ^ code[colour]) * regions + (level ^ slab)) * (share * PITCH)
+            for n in range(share):
+                flat[pl.ds(row + n * PITCH, ROWS), :] = piece[first + n].astype(F32)
             part += 1
-    pitch = out_ref.shape[1] // 128
+    pitch = out_ref.shape[1] // (128 * ROWS) * PITCH
     low = lax.broadcasted_iota(jnp.int32, (8, 128), 1) < 64
 
     def turned(x):
@@ -272,7 +278,7 @@
         for i in range(2):
             rows.append(
                 [
-                    flat[pl.ds(base + i + lane * ROWS + group * 8 * pitch, 8, stride=pitch), :]
+                    flat[pl.ds(base + i + lane * PITCH + group * 8 * pitch, 8, stride=pitch), :]
                     for lane in range(3)
                 ]
             )
@@ -292,7 +298,7 @@
 
     def pair(m, carry):
         i = m * 2
-        base = (i // ROWS) * (3 * ROWS) + i % ROWS
+        base = (i // ROWS) * (3 * PITCH) + i % ROWS
         for top in range(0, count, 16):
             tiles = [block(base, top // 8), block(base, top // 8 + 1)]
             high = min(16, count - top)
@@ -360,7 +366,15 @@
         return seen * kept.astype(BF)
 
     inner, outer = rims(own_plane)
-    lines, planes = cut(input_lines_kernel, 0, (inner, features.reshape(flat), marks, outer))
+    occupied = pl.pallas_call(
+        occupied_kernel,
+        out_shape=jax.ShapeDtypeStruct((depth, 64, channels), BF),
+        in_specs=[SMEM, VMEM, VMEM],
+        out_specs=VMEM,
+        scratch_shapes=[pltpu.VMEM((depth * EDGE, EDGE, channels), F32)],
+        compiler_params=vmem(12),
+    )(owner, features.reshape(flat), marks)
+    lines, planes = cut(input_lines_kernel, 0, (inner, occupied, outer))
     lines, weight = barrier((lines, weight))
     arrived = exchanged(lines)
     kernel = weight.reshape(27, channels, channels)
@@ -368,7 +382,7 @@
     act, grad, bias_terms, terms = pl.pallas_call(
         functools.partial(forward_kernel, share, regions, n_leaves),
         out_shape=(
-            jax.ShapeDtypeStruct(flat, BF),
+            jax.ShapeDtypeStruct((voxels, channels), BF),
             jax.ShapeDtypeStruct((voxels, channels), BF),
             jax.ShapeDtypeStruct((1, ROWS, 128), BF),
             jax.ShapeDtypeStruct((n_leaves * leaf_units, ROWS, 128), BF),
@@ -415,20 +429,21 @@
     held = [total] + [
         lax.ppermute(total, "region", pairs(regions, flip)) for flip in range(1, regions)
     ]
-    grad_input, total_bias = pl.pallas_call(
+    grad_input, activation, total_bias = pl.pallas_call(
         input_kernel,
         out_shape=(
             jax.ShapeDtypeStruct(flat, BF),
+            jax.ShapeDtypeStruct(flat, BF),
             jax.ShapeDtypeStruct((1, channels), F32),
         ),
-        in_specs=[SMEM] + [VMEM] * 4,
-        out_specs=(VMEM, VMEM),
+        in_specs=[SMEM] + [VMEM] * 5,
+        out_specs=(VMEM, VMEM, VMEM),
         scratch_shapes=scratch,
         compiler_params=vmem(20),
         cost_estimate=pl.CostEstimate(
             flops=2 * 27 * voxels * channels * channels, bytes_accessed=3 << 20, transcendentals=0
         ),
-    )(owner, grad_planes, arrived, kernel, marks)
+    )(owner, grad_planes, arrived, kernel, marks, act)
 
     colours = [
         [jnp.concatenate([h[c * share : (c + 1) * share] for h in held], axis=0)] for c in range(2)
@@ -449,12 +464,13 @@
         out_shape=jax.ShapeDtypeStruct((27, channels * channels), BF),
         in_specs=[SMEM] + [VMEM] * len(near + far),
         out_specs=VMEM,
-        scratch_shapes=[pltpu.VMEM((max(32 * units // 27, n_leaves * leaf_units) * ROWS, 128), F32)],
+        scratch_shapes=[pltpu.VMEM((max(32 * units // 27, n_leaves * leaf_units) * PITCH, 128), F32)],
         compiler_params=vmem(20),
     )(owner, *near, *far)
 
     shape = features.shape
-    return act.reshape(shape), grad_input.reshape(shape), kernel_grad, total_bias.reshape(channels)
+    outs = activation.reshape(shape), grad_input.reshape(shape)
+    return *outs, kernel_grad, total_bias.reshape(channels)
 
 
 def solution(mesh):

time: 101 us -> 99.8 us (0.988)
  starting transfers between devices: 35.7 us -> 33.8 us
  Pallas kernels: 21.7 us -> 20.4 us
  waiting for transfers between devices: 27.5 us -> 28.8 us
    ppermute x5, waiting for transfers between devices: 10.9 us -> 13.6 us  [halve(): got = lax.ppermute(x[half:].astype(BF), axis, pairs(count, flip))]
    ppermute x2, starting transfers between devices: 7.87 us -> 6.1 us  [rims(): inner = lax.ppermute(plane(top * (1 - odd)), 'region', joined[0])]
    pallas_call x1, Pallas kernels: 5.84 us -> 4.41 us  [body(): pl.pallas_call(functools.partial(unfold_kernel, share, regions, n_leaves)...]
    pallas_call x0 -> x1, Pallas kernels: none -> 1.28 us  [body(): pl.pallas_call(occupied_kernel, out_shape=jax.ShapeDtypeStruct((depth, 64...]
    ppermute x2, waiting for transfers between devices: 1.13 us -> 0.01 us  [rims(): inner = lax.ppermute(plane(top * (1 - odd)), 'region', joined[0])]
    unnamed x20 -> x24, local copies, waits for them, and re-layouts: 4.79 us -> 5.76 us
  transfers between devices with their start and end apart: 31 -> 31, of which waited for: 14 -> 12; matrix products, arithmetic and copies ran while one was open for 7% -> 7% of each run, Pallas kernels for 5% -> 6%
where the time goes in v3:
time: 99.8 us; the launch traced here: 99.1 us
  starting transfers between devices  33.8 us (34%)
  waiting for transfers between devices  28.8 us (29%)
  Pallas kernels  20.4 us (20%)
  local copies, waits for them, and re-layouts  12.8 us (13%)
  other arithmetic  2.26 us (2%)
    ppermute x5, waiting for transfers between devices, halve(): got = lax.ppermute(x[half:].astype(BF), axis, pairs(count, flip))  13.6 us
    pallas_call x1, Pallas kernels, body(): pl.pallas_call(functools.partial(forward_kernel, share, regions, n_leaves...  8.08 us
    all_to_all x2, starting transfers between devices, exchanged(): return lax.all_to_all(lines, 'batch', 0, 0, tiled=True)  7.23 us
    all_to_all x2, waiting for transfers between devices, exchanged(): return lax.all_to_all(lines, 'batch', 0, 0, tiled=True)  6.39 us
    ppermute x2, starting transfers between devices, rims(): inner = lax.ppermute(plane(top * (1 - odd)), 'region', joined[0])  6.1 us
    unnamed x24, local copies, waits for them, and re-layouts  5.76 us
    ppermute x6, starting transfers between devices, body(): lax.ppermute(x, 'batch', pairs(tiles, 1 << o[step]))  5.29 us
    ppermute x3, starting transfers between devices, body(): gots.append(lax.ppermute(sent, 'region', pairs(regions, flip)))  4.45 us
  transfers between devices with their start and end apart: 31, of which 12 were waited for; matrix products, arithmetic and copies ran while one was open for 7% of the time, Pallas kernels for 6%

profile of v3, /device:TPU:0, one launch (start us, length us, event | category | flops | bytes accessed | tf_op | source)
XLA Modules:
  0.0 99.1 jit_solution(10412178325966237919)
XLA Ops:
  0.6 0.8 constant_dynamic-slice_fusion.3
  1.4 0.1 reshape.128
  1.5 0.8 fusion.6
  2.3 0.1 broadcast_multiply_fusion
  2.4 0.7 collective-permute-start.1
  3.0 0.1 reshape.125
  3.1 0.1 broadcast_multiply_fusion.1
  3.2 5.9 %collective-permute-start = (bf16[1,64,192]{2,1,0:T(8,128)(2,1)S(1)}, bf16[1,64,192]{2,1,0:T(8,128)(2,1)S(1)}, u32[]{:S(2)}, u32[]{:S(2)}) collective-permute-start(bf16[1,64,192]{2,1,0:T(8,128)(2,1)S(1)} %broadcast_multiply_fusion.1), channel_id=1, source_target_pairs={{0,8},{8,0},{16,24},{24,16},{1,9},{9,1},{17,25},{25,17},{2,10},{10... | collective-permute-start | bytes 73736 | tf_op jit(solution)/shard_map/ppermute | solution.py:335
  9.1 0.8 reshape.127.mask_ref
  9.8 0.9 copy-done.1
  10.8 0.7 copy-done.4
  11.4 1.3 %shard_map.93.x_ref = bf16[8,64,192]{2,1,0:T(8,128)(2,1)S(1)} custom-call(s32[8]{0:T(128)S(1)} %copy-done.4, bf16[64,1536]{1,0:T(8,128)(2,1)S(1)} %bitcast.13, s32[64,8]{1,0:T(8,128)S(1)} %reshape.127.mask_ref), custom_call_target="tpu_custom_call" | custom-call | tf_op jit(solution)/shard_map/pallas_call | solution.py:369
  12.7 1.7 %shard_map.94 = (bf16[8,10,8,192]{3,2,1,0:T(8,128)(2,1)}, bf16[10,64,192]{2,1,0:T(8,128)(2,1)S(1)}) custom-call(s32[8]{0:T(128)S(1)} %copy-done.4, bf16[1,64,192]{2,1,0:T(8,128)(2,1)S(1)} %collective-permute-done.inner_ref, bf16[8,64,192]{2,1,0:T(8,128)(2,1)S(1)} %shard_map.93.x_ref, bf16[1,64,192]{2,1,0:T(8,128)(2,1)S(1)} %collective-permute-done.1.outer_ref), custom_call_target="tpu_custom_call" | custom-call | tf_op jit(solution)/shard_map/pallas_call | solution.py:340
  14.4 3.6 %all-to-all-start = ((bf16[8,10,8,192]{3,2,1,0:T(8,128)(2,1)}), bf16[8,10,8,192]{3,2,1,0:T(8,128)(2,1)S(1)}, u32[]{:S(2)}, u32[]{:S(2)}) async-start(bf16[8,10,8,192]{3,2,1,0:T(8,128)(2,1)} %get-tuple-element.26), calls=%async_computation | async-start | bytes 655360 | tf_op jit(solution)/shard_map/all_to_all | solution.py:353
  18.1 4.4 %reshape.129.w_ref = bf16[27,192,192]{2,1,0:T(8,128)(2,1)S(1)} reshape(bf16[27,36864]{1,0:T(8,128)(2,1)} %param.9) | data formatting | bytes 3981312 | tf_op jit(solution)/shard_map/reshape | solution.py:380
  22.4 3.2 %all-to-all-done.recv_ref = bf16[8,10,8,192]{3,2,1,0:T(8,128)(2,1)S(1)} async-done(((bf16[8,10,8,192]{3,2,1,0:T(8,128)(2,1)}), bf16[8,10,8,192]{3,2,1,0:T(8,128)(2,1)S(1)}, u32[]{:S(2)}, u32[]{:S(2)}) %all-to-all-start) | async-done | bytes 245792 | tf_op jit(solution)/shard_map/all_to_all | solution.py:353
  25.7 8.1 %shard_map.95 = (bf16[512,192]{1,0:T(8,128)(2,1)S(1)}, bf16[512,192]{1,0:T(8,128)(2,1)S(1)}, bf16[1,16,128]{2,1,0:T(8,128)(2,1)S(1)}, bf16[512,16,128]{2,1,0:T(8,128)(2,1)S(1)}) custom-call(s32[8]{0:T(128)S(1)} %copy-done.5, bf16[10,64,192]{2,1,0:T(8,128)(2,1)S(1)} %get-tuple-element.24.x_ref, bf16[8,10,8,192]{3,2,1,0:T(8,128)(2,1)S(1)} %all-to-all-done.recv_ref, ...), custom_call_target="tpu_custom_call" | custom-call | flops 2038431744 | bytes 6291456 | tf_op jit(solution)/shard_map/pallas_call | solution.py:382
  33.8 0.2 slice.104
  34.0 0.1 collective-permute-start.2
  34.1 2.6 %collective-permute-done.2 = bf16[256,16,128]{2,1,0:T(8,128)(2,1)S(1)} collective-permute-done((bf16[256,16,128]{2,1,0:T(8,128)(2,1)S(1)}, bf16[256,16,128]{2,1,0:T(8,128)(2,1)S(1)}, u32[]{:S(2)}, u32[]{:S(2)}) %collective-permute-start.2) | collective-permute-done | bytes 1048608 | tf_op jit(solution)/shard_map/ppermute | solution.py:404
  36.7 0.3 fusion.7
  37.1 0.6 collective-permute-start.3
  37.7 0.6 collective-permute-start.4
  38.3 0.2 collective-permute-start.5
  38.5 0.7 collective-permute-start.6
  39.2 6.3 %collective-permute-done.3 = bf16[64,16,128]{2,1,0:T(8,128)(2,1)S(1)} collective-permute-done((bf16[64,16,128]{2,1,0:T(8,128)(2,1)S(1)}, bf16[64,16,128]{2,1,0:T(8,128)(2,1)S(1)}, u32[]{:S(2)}, u32[]{:S(2)}) %collective-permute-start.3) | collective-permute-done | bytes 262176 | tf_op jit(solution)/shard_map/ppermute | solution.py:404
  45.5 0.3 collective-permute-done.4
  45.8 0.1 slice_add_fusion
  45.9 1.5 %collective-permute-start.8 = (bf16[32,16,128]{2,1,0:T(8,128)(2,1)S(1)}, bf16[32,16,128]{2,1,0:T(8,128)(2,1)S(1)}, u32[]{:S(2)}, u32[]{:S(2)}) collective-permute-start(bf16[32,16,128]{2,1,0:T(8,128)(2,1)S(1)} %slice.169), channel_id=1, source_target_pairs={{0,2},{1,3},{2,0},{3,1},{4,6},{5,7},{6,4},{7,5},{8,10},{9,11},{10,... | collective-permute-start | bytes 393224 | tf_op jit(solution)/shard_map/ppermute | solution.py:404
  47.5 0.6 collective-permute-start.7
  48.1 2.9 %collective-permute-done.8 = bf16[32,16,128]{2,1,0:T(8,128)(2,1)S(1)} collective-permute-done((bf16[32,16,128]{2,1,0:T(8,128)(2,1)S(1)}, bf16[32,16,128]{2,1,0:T(8,128)(2,1)S(1)}, u32[]{:S(2)}, u32[]{:S(2)}) %collective-permute-start.8) | collective-permute-done | bytes 131104 | tf_op jit(solution)/shard_map/ppermute | solution.py:404
  51.0 1.5 %collective-permute-done.7 = bf16[32,16,128]{2,1,0:T(8,128)(2,1)S(1)} collective-permute-done((bf16[32,16,128]{2,1,0:T(8,128)(2,1)S(1)}, bf16[32,16,128]{2,1,0:T(8,128)(2,1)S(1)}, u32[]{:S(2)}, u32[]{:S(2)}) %collective-permute-start.7) | collective-permute-done | bytes 131104 | tf_op jit(solution)/shard_map/ppermute | solution.py:404
  52.6 0.2 collective-permute-start.10
  52.8 1.8 %collective-permute-start.11 = (bf16[17,16,128]{2,1,0:T(8,128)(2,1)S(1)}, bf16[17,16,128]{2,1,0:T(8,128)(2,1)S(1)}, u32[]{:S(2)}, u32[]{:S(2)}) collective-permute-start(bf16[17,16,128]{2,1,0:T(8,128)(2,1)S(1)} %get-tuple-element.72), channel_id=1, source_target_pairs={{0,8},{8,0},{16,24},{24,16},{1,9},{9,1},{17,25},{25,17},{2,10},{10... | collective-permute-start | bytes 208904 | tf_op jit(solution)/shard_map/ppermute | solution.py:423
  54.6 2.5 %collective-permute-start.9 = (bf16[17,16,128]{2,1,0:T(8,128)(2,1)S(1)}, bf16[17,16,128]{2,1,0:T(8,128)(2,1)S(1)}, u32[]{:S(2)}, u32[]{:S(2)}) collective-permute-start(bf16[17,16,128]{2,1,0:T(8,128)(2,1)S(1)} %get-tuple-element.74), channel_id=1, source_target_pairs={{0,24},{8,16},{16,8},{24,0},{1,25},{9,17},{17,9},{25,1},{2,26},{10... | collective-permute-start | bytes 208904 | tf_op jit(solution)/shard_map/ppermute | solution.py:423
  57.1 1.4 %collective-permute-done.10.refs_1_ = bf16[17,16,128]{2,1,0:T(8,128)(2,1)S(1)} collective-permute-done((bf16[17,16,128]{2,1,0:T(8,128)(2,1)S(1)}, bf16[17,16,128]{2,1,0:T(8,128)(2,1)S(1)}, u32[]{:S(2)}, u32[]{:S(2)}) %collective-permute-start.10) | collective-permute-done | bytes 69664 | tf_op jit(solution)/shard_map/ppermute | solution.py:423
  58.5 2.3 %collective-permute-done.9.refs_0_ = bf16[17,16,128]{2,1,0:T(8,128)(2,1)S(1)} collective-permute-done((bf16[17,16,128]{2,1,0:T(8,128)(2,1)S(1)}, bf16[17,16,128]{2,1,0:T(8,128)(2,1)S(1)}, u32[]{:S(2)}, u32[]{:S(2)}) %collective-permute-start.9) | collective-permute-done | bytes 69664 | tf_op jit(solution)/shard_map/ppermute | solution.py:423
  60.9 0.1 collective-permute-start.12
  61.0 3.1 %collective-permute-start.13 = (bf16[16,16,128]{2,1,0:T(8,128)(2,1)S(1)}, bf16[16,16,128]{2,1,0:T(8,128)(2,1)S(1)}, u32[]{:S(2)}, u32[]{:S(2)}) collective-permute-start(bf16[16,16,128]{2,1,0:T(8,128)(2,1)S(1)} %fusion.2), channel_id=1, source_target_pairs={{0,16},{8,24},{16,0},{24,8},{1,17},{9,25},{17,1},{25,9},{2,18},{10... | collective-permute-start | bytes 196616 | tf_op jit(solution)/shard_map/ppermute | solution.py:430
  64.1 1.3 %collective-permute-start.14 = (bf16[16,16,128]{2,1,0:T(8,128)(2,1)S(1)}, bf16[16,16,128]{2,1,0:T(8,128)(2,1)S(1)}, u32[]{:S(2)}, u32[]{:S(2)}) collective-permute-start(bf16[16,16,128]{2,1,0:T(8,128)(2,1)S(1)} %fusion.2), channel_id=1, source_target_pairs={{0,24},{8,16},{16,8},{24,0},{1,25},{9,17},{17,9},{25,1},{2,26},{10... | collective-permute-start | bytes 196616 | tf_op jit(solution)/shard_map/ppermute | solution.py:430
  65.3 0.6 fusion.13
  66.0 1.0 %shard_map.96 = (bf16[8,11,8,192]{3,2,1,0:T(8,128)(2,1)S(1)}, bf16[10,64,192]{2,1,0:T(8,128)(2,1)S(1)}) custom-call(s32[8]{0:T(128)S(1)} %copy-done.5, bf16[1,64,192]{2,1,0:T(8,128)(2,1)S(1)} %collective-permute-done.5.inner_ref, bf16[8,64,192]{2,1,0:T(8,128)(2,1)S(1)} %bitcast.12, bf16[1,64,192]{2,1,0:T(8,128)(2,1)S(1)} %collective-permute-done.6.outer_ref, ...), custom_call_target="tpu_custom_call" | custom-call | tf_op jit(solution)/shard_map/pallas_call | solution.py:340
  67.0 0.7 copy-done
  67.7 0.7 copy-done.6
  68.5 3.6 %all-to-all-start.1 = ((bf16[8,11,8,192]{3,2,1,0:T(8,128)(2,1)}), bf16[8,11,8,192]{3,2,1,0:T(8,128)(2,1)S(1)}, u32[]{:S(2)}, u32[]{:S(2)}) async-start(bf16[8,11,8,192]{3,2,1,0:T(8,128)(2,1)} %copy-done), calls=%async_computation.1 | async-start | bytes 720896 | tf_op jit(solution)/shard_map/all_to_all | solution.py:353
  72.2 1.8 %collective-permute-start.16 = (bf16[32,16,128]{2,1,0:T(8,128)(2,1)S(1)}, bf16[32,16,128]{2,1,0:T(8,128)(2,1)S(1)}, u32[]{:S(2)}, u32[]{:S(2)}) collective-permute-start(bf16[32,16,128]{2,1,0:T(8,128)(2,1)S(1)} %pad_maximum_fusion.1.refs_4_), channel_id=1, source_target_pairs={{0,2},{1,3},{2,0},{3,1},{4,6},{5,7},{6,4},{7,5},{8,10},{9,11},{10,... | collective-permute-start | bytes 393224 | tf_op jit(solution)/shard_map/ppermute | solution.py:453
  74.0 1.5 %collective-permute-start.19 = (bf16[32,16,128]{2,1,0:T(8,128)(2,1)S(1)}, bf16[32,16,128]{2,1,0:T(8,128)(2,1)S(1)}, u32[]{:S(2)}, u32[]{:S(2)}) collective-permute-start(bf16[32,16,128]{2,1,0:T(8,128)(2,1)S(1)} %pad_maximum_fusion.1.refs_4_), channel_id=1, source_target_pairs={{0,4},{1,5},{2,6},{3,7},{4,0},{5,1},{6,2},{7,3},{8,12},{9,13},{10,... | collective-permute-start | bytes 393224 | tf_op jit(solution)/shard_map/ppermute | solution.py:453
  75.5 0.8 pad_maximum_fusion.refs_0_
  76.3 0.6 collective-permute-start.15
  76.9 0.3 collective-permute-start.17
  77.2 3.1 %all-to-all-done.1.recv_ref = bf16[8,11,8,192]{3,2,1,0:T(8,128)(2,1)S(1)} async-done(((bf16[8,11,8,192]{3,2,1,0:T(8,128)(2,1)}), bf16[8,11,8,192]{3,2,1,0:T(8,128)(2,1)S(1)}, u32[]{:S(2)}, u32[]{:S(2)}) %all-to-all-start.1) | async-done | bytes 270368 | tf_op jit(solution)/shard_map/all_to_all | solution.py:353
  80.3 0.8 copy-done.3
  81.1 1.0 copy-done.7
  82.0 0.9 copy-done.11
  83.0 3.9 %shard_map.97 = (bf16[64,1536]{1,0:T(8,128)(2,1)}, bf16[64,1536]{1,0:T(8,128)(2,1)}, f32[1,192]{1,0:T(1,128)}) custom-call(s32[8]{0:T(128)S(1)} %copy-done.5, bf16[10,64,192]{2,1,0:T(8,128)(2,1)S(1)} %copy-done.7, bf16[8,11,8,192]{3,2,1,0:T(8,128)(2,1)S(1)} %all-to-all-done.1.recv_ref, bf16[27,192,192]{2,1,0:T(8,128)(2,1)S(1)} %reshape.129.w_ref, ...), custom_call_target="tpu_custom_call" | custom-call | flops 1019215872 | bytes 3145728 | tf_op jit(solution)/shard_map/pallas_call | solution.py:432
  86.9 0.5 collective-permute-start.27
  87.4 0.1 collective-permute-start.18
  87.6 1.0 collective-permute-start.20
  88.5 0.5 collective-permute-start.22
  89.1 4.0 %collective-permute-done.18.refs_3_ = bf16[32,16,128]{2,1,0:T(8,128)(2,1)S(1)} collective-permute-done((bf16[32,16,128]{2,1,0:T(8,128)(2,1)}, bf16[32,16,128]{2,1,0:T(8,128)(2,1)S(1)}, u32[]{:S(2)}, u32[]{:S(2)}) %collective-permute-start.18) | collective-permute-done | bytes 131104 | tf_op jit(solution)/shard_map/ppermute | solution.py:453
  93.1 0.5 collective-permute-start.28
  93.6 0.8 collective-permute-done.24.refs_11_
  94.5 0.2 collective-permute-done.28.refs_15_
  94.6 4.4 %shard_map.98 = bf16[27,36864]{1,0:T(8,128)(2,1)} custom-call(s32[8]{0:T(128)S(1)} %copy-done.5, bf16[32,16,128]{2,1,0:T(8,128)(2,1)S(1)} %pad_maximum_fusion.refs_0_, bf16[32,16,128]{2,1,0:T(8,128)(2,1)} %collective-permute-done.15.refs_1_, bf16[32,16,128]{2,1,0:T(8,128)(2,1)} %collective-permute-done.17.refs_2_, ...), custom_call_target="tpu_custom_call" | custom-call | tf_op jit(solution)/shard_map/pallas_call | solution.py:462
  (56 shorter events, 0.5 us)
Async XLA Ops:
  2.4 10.3 %collective-permute-start.1 = (bf16[1,64,192]{2,1,0:T(8,128)(2,1)S(1)}, bf16[1,64,192]{2,1,0:T(8,128)(2,1)S(1)}, u32[]{:S(2)}, u32[]{:S(2)}) collective-permute-start(bf16[1,64,192]{2,1,0:T(8,128)(2,1)S(1)} %broadcast_multiply_fusion), channel_id=1, source_target_pairs={{8,16},{16,8},{9,17},{17,9},{10,18},{18,10},{11,19},{19,11},{12,20... | collective-permute-start | bytes 73736 | tf_op jit(solution)/shard_map/ppermute | solution.py:336
  3.2 9.5 %collective-permute-start = (bf16[1,64,192]{2,1,0:T(8,128)(2,1)S(1)}, bf16[1,64,192]{2,1,0:T(8,128)(2,1)S(1)}, u32[]{:S(2)}, u32[]{:S(2)}) collective-permute-start(bf16[1,64,192]{2,1,0:T(8,128)(2,1)S(1)} %broadcast_multiply_fusion.1), channel_id=1, source_target_pairs={{0,8},{8,0},{16,24},{24,16},{1,9},{9,1},{17,25},{25,17},{2,10},{10... | collective-permute-start | bytes 73736 | tf_op jit(solution)/shard_map/ppermute | solution.py:335
  9.8 15.9 %copy-start.2 = (s32[64,8]{1,0:T(8,128)}, s32[64,8]{1,0:T(8,128)S(1)}, u32[]{:S(2)}) copy-start(s32[64,8]{1,0:T(8,128)S(1)} %reshape.127.mask_ref) | copy-start | bytes 6148
  9.8 0.9 copy-start.1
  10.8 0.7 copy-start.4
  14.4 11.2 %all-to-all-start = ((bf16[8,10,8,192]{3,2,1,0:T(8,128)(2,1)}), bf16[8,10,8,192]{3,2,1,0:T(8,128)(2,1)S(1)}, u32[]{:S(2)}, u32[]{:S(2)}) async-start(bf16[8,10,8,192]{3,2,1,0:T(8,128)(2,1)} %get-tuple-element.26), calls=%async_computation | async-start | bytes 655360 | tf_op jit(solution)/shard_map/all_to_all | solution.py:353
  18.1 7.6 %copy-start.5 = (s32[8]{0:T(128)S(1)}, s32[8]{0:T(128)}, u32[]{:S(2)}) copy-start(s32[8]{0:T(128)} %owner.11) | copy-start | bytes 100
  18.1 7.6 %copy-start.8 = (bf16[8,8,1536]{2,1,0:T(8,128)(2,1)S(1)}, bf16[8,8,1536]{2,1,0:T(8,128)(2,1)}, u32[]{:S(2)}) copy-start(bf16[8,8,1536]{2,1,0:T(8,128)(2,1)} %param.11) | copy-start | bytes 589828
  18.1 7.6 %copy-start.9 = (f32[192]{0:T(256)S(1)}, f32[192]{0:T(256)}, u32[]{:S(2)}) copy-start(f32[192]{0:T(256)} %param.10) | copy-start | bytes 2308
  33.8 3.2 %copy-start.10 = (bf16[512,192]{1,0:T(8,128)(2,1)}, bf16[512,192]{1,0:T(8,128)(2,1)S(1)}, u32[]{:S(2)}) copy-start(bf16[512,192]{1,0:T(8,128)(2,1)S(1)} %get-tuple-element.37.pre_ref) | copy-start | bytes 589828
  34.0 2.7 %collective-permute-start.2 = (bf16[256,16,128]{2,1,0:T(8,128)(2,1)S(1)}, bf16[256,16,128]{2,1,0:T(8,128)(2,1)S(1)}, u32[]{:S(2)}, u32[]{:S(2)}) collective-permute-start(bf16[256,16,128]{2,1,0:T(8,128)(2,1)S(1)} %slice.104), channel_id=1, source_target_pairs={{0,1},{1,0},{2,3},{3,2},{4,5},{5,4},{6,7},{7,6},{8,9},{9,8},{10,11... | collective-permute-start | bytes 3145736 | tf_op jit(solution)/shard_map/ppermute | solution.py:404
  37.1 8.4 %collective-permute-start.3 = (bf16[64,16,128]{2,1,0:T(8,128)(2,1)S(1)}, bf16[64,16,128]{2,1,0:T(8,128)(2,1)S(1)}, u32[]{:S(2)}, u32[]{:S(2)}) collective-permute-start(bf16[64,16,128]{2,1,0:T(8,128)(2,1)S(1)} %get-tuple-element.53), channel_id=1, source_target_pairs={{0,2},{1,3},{2,0},{3,1},{4,6},{5,7},{6,4},{7,5},{8,10},{9,11},{10,... | collective-permute-start | bytes 786440 | tf_op jit(solution)/shard_map/ppermute | solution.py:404
  37.7 8.1 %collective-permute-start.4 = (bf16[64,16,128]{2,1,0:T(8,128)(2,1)S(1)}, bf16[64,16,128]{2,1,0:T(8,128)(2,1)S(1)}, u32[]{:S(2)}, u32[]{:S(2)}) collective-permute-start(bf16[64,16,128]{2,1,0:T(8,128)(2,1)S(1)} %get-tuple-element.52), channel_id=1, source_target_pairs={{0,4},{1,5},{2,6},{3,7},{4,0},{5,1},{6,2},{7,3},{8,12},{9,13},{10,... | collective-permute-start | bytes 786440 | tf_op jit(solution)/shard_map/ppermute | solution.py:404
  38.3 7.6 %collective-permute-start.5 = (bf16[1,64,192]{2,1,0:T(8,128)(2,1)S(1)}, bf16[1,64,192]{2,1,0:T(8,128)(2,1)S(1)}, u32[]{:S(2)}, u32[]{:S(2)}) collective-permute-start(bf16[1,64,192]{2,1,0:T(8,128)(2,1)S(1)} %get-tuple-element.55), channel_id=1, source_target_pairs={{0,8},{8,0},{16,24},{24,16},{1,9},{9,1},{17,25},{25,17},{2,10},{10... | collective-permute-start | bytes 73736 | tf_op jit(solution)/shard_map/ppermute | solution.py:335
  38.5 7.4 %collective-permute-start.6 = (bf16[1,64,192]{2,1,0:T(8,128)(2,1)S(1)}, bf16[1,64,192]{2,1,0:T(8,128)(2,1)S(1)}, u32[]{:S(2)}, u32[]{:S(2)}) collective-permute-start(bf16[1,64,192]{2,1,0:T(8,128)(2,1)S(1)} %get-tuple-element.54), channel_id=1, source_target_pairs={{8,16},{16,8},{9,17},{17,9},{10,18},{18,10},{11,19},{19,11},{12,20... | collective-permute-start | bytes 73736 | tf_op jit(solution)/shard_map/ppermute | solution.py:336
  45.9 5.0 %collective-permute-start.8 = (bf16[32,16,128]{2,1,0:T(8,128)(2,1)S(1)}, bf16[32,16,128]{2,1,0:T(8,128)(2,1)S(1)}, u32[]{:S(2)}, u32[]{:S(2)}) collective-permute-start(bf16[32,16,128]{2,1,0:T(8,128)(2,1)S(1)} %slice.169), channel_id=1, source_target_pairs={{0,2},{1,3},{2,0},{3,1},{4,6},{5,7},{6,4},{7,5},{8,10},{9,11},{10,... | collective-permute-start | bytes 393224 | tf_op jit(solution)/shard_map/ppermute | solution.py:404
  47.5 5.0 %collective-permute-start.7 = (bf16[32,16,128]{2,1,0:T(8,128)(2,1)S(1)}, bf16[32,16,128]{2,1,0:T(8,128)(2,1)S(1)}, u32[]{:S(2)}, u32[]{:S(2)}) collective-permute-start(bf16[32,16,128]{2,1,0:T(8,128)(2,1)S(1)} %slice.170), channel_id=1, source_target_pairs={{0,4},{1,5},{2,6},{3,7},{4,0},{5,1},{6,2},{7,3},{8,12},{9,13},{10,... | collective-permute-start | bytes 393224 | tf_op jit(solution)/shard_map/ppermute | solution.py:404
  52.6 5.9 %collective-permute-start.10 = (bf16[17,16,128]{2,1,0:T(8,128)(2,1)S(1)}, bf16[17,16,128]{2,1,0:T(8,128)(2,1)S(1)}, u32[]{:S(2)}, u32[]{:S(2)}) collective-permute-start(bf16[17,16,128]{2,1,0:T(8,128)(2,1)S(1)} %get-tuple-element.73), channel_id=1, source_target_pairs={{0,16},{8,24},{16,0},{24,8},{1,17},{9,25},{17,1},{25,9},{2,18},{10... | collective-permute-start | bytes 208904 | tf_op jit(solution)/shard_map/ppermute | solution.py:423
  52.8 5.7 %collective-permute-start.11 = (bf16[17,16,128]{2,1,0:T(8,128)(2,1)S(1)}, bf16[17,16,128]{2,1,0:T(8,128)(2,1)S(1)}, u32[]{:S(2)}, u32[]{:S(2)}) collective-permute-start(bf16[17,16,128]{2,1,0:T(8,128)(2,1)S(1)} %get-tuple-element.72), channel_id=1, source_target_pairs={{0,8},{8,0},{16,24},{24,16},{1,9},{9,1},{17,25},{25,17},{2,10},{10... | collective-permute-start | bytes 208904 | tf_op jit(solution)/shard_map/ppermute | solution.py:423
  54.6 6.3 %collective-permute-start.9 = (bf16[17,16,128]{2,1,0:T(8,128)(2,1)S(1)}, bf16[17,16,128]{2,1,0:T(8,128)(2,1)S(1)}, u32[]{:S(2)}, u32[]{:S(2)}) collective-permute-start(bf16[17,16,128]{2,1,0:T(8,128)(2,1)S(1)} %get-tuple-element.74), channel_id=1, source_target_pairs={{0,24},{8,16},{16,8},{24,0},{1,25},{9,17},{17,9},{25,1},{2,26},{10... | collective-permute-start | bytes 208904 | tf_op jit(solution)/shard_map/ppermute | solution.py:423
  60.9 11.2 %collective-permute-start.12 = (bf16[16,16,128]{2,1,0:T(8,128)(2,1)S(1)}, bf16[16,16,128]{2,1,0:T(8,128)(2,1)S(1)}, u32[]{:S(2)}, u32[]{:S(2)}) collective-permute-start(bf16[16,16,128]{2,1,0:T(8,128)(2,1)S(1)} %fusion.2), channel_id=1, source_target_pairs={{0,8},{8,0},{16,24},{24,16},{1,9},{9,1},{17,25},{25,17},{2,10},{10... | collective-permute-start | bytes 196616 | tf_op jit(solution)/shard_map/ppermute | solution.py:430
  61.0 11.2 %collective-permute-start.13 = (bf16[16,16,128]{2,1,0:T(8,128)(2,1)S(1)}, bf16[16,16,128]{2,1,0:T(8,128)(2,1)S(1)}, u32[]{:S(2)}, u32[]{:S(2)}) collective-permute-start(bf16[16,16,128]{2,1,0:T(8,128)(2,1)S(1)} %fusion.2), channel_id=1, source_target_pairs={{0,16},{8,24},{16,0},{24,8},{1,17},{9,25},{17,1},{25,9},{2,18},{10... | collective-permute-start | bytes 196616 | tf_op jit(solution)/shard_map/ppermute | solution.py:430
  64.1 8.1 %collective-permute-start.14 = (bf16[16,16,128]{2,1,0:T(8,128)(2,1)S(1)}, bf16[16,16,128]{2,1,0:T(8,128)(2,1)S(1)}, u32[]{:S(2)}, u32[]{:S(2)}) collective-permute-start(bf16[16,16,128]{2,1,0:T(8,128)(2,1)S(1)} %fusion.2), channel_id=1, source_target_pairs={{0,24},{8,16},{16,8},{24,0},{1,25},{9,17},{17,9},{25,1},{2,26},{10... | collective-permute-start | bytes 196616 | tf_op jit(solution)/shard_map/ppermute | solution.py:430
  67.0 0.7 copy-start
  67.7 0.7 copy-start.6
  68.5 11.8 %all-to-all-start.1 = ((bf16[8,11,8,192]{3,2,1,0:T(8,128)(2,1)}), bf16[8,11,8,192]{3,2,1,0:T(8,128)(2,1)S(1)}, u32[]{:S(2)}, u32[]{:S(2)}) async-start(bf16[8,11,8,192]{3,2,1,0:T(8,128)(2,1)} %copy-done), calls=%async_computation.1 | async-start | bytes 720896 | tf_op jit(solution)/shard_map/all_to_all | solution.py:353
  72.2 14.7 %collective-permute-start.16 = (bf16[32,16,128]{2,1,0:T(8,128)(2,1)S(1)}, bf16[32,16,128]{2,1,0:T(8,128)(2,1)S(1)}, u32[]{:S(2)}, u32[]{:S(2)}) collective-permute-start(bf16[32,16,128]{2,1,0:T(8,128)(2,1)S(1)} %pad_maximum_fusion.1.refs_4_), channel_id=1, source_target_pairs={{0,2},{1,3},{2,0},{3,1},{4,6},{5,7},{6,4},{7,5},{8,10},{9,11},{10,... | collective-permute-start | bytes 393224 | tf_op jit(solution)/shard_map/ppermute | solution.py:453
  74.0 12.9 %collective-permute-start.19 = (bf16[32,16,128]{2,1,0:T(8,128)(2,1)S(1)}, bf16[32,16,128]{2,1,0:T(8,128)(2,1)S(1)}, u32[]{:S(2)}, u32[]{:S(2)}) collective-permute-start(bf16[32,16,128]{2,1,0:T(8,128)(2,1)S(1)} %pad_maximum_fusion.1.refs_4_), channel_id=1, source_target_pairs={{0,4},{1,5},{2,6},{3,7},{4,0},{5,1},{6,2},{7,3},{8,12},{9,13},{10,... | collective-permute-start | bytes 393224 | tf_op jit(solution)/shard_map/ppermute | solution.py:453
  76.3 11.1 %collective-permute-start.15 = (bf16[32,16,128]{2,1,0:T(8,128)(2,1)S(1)}, bf16[32,16,128]{2,1,0:T(8,128)(2,1)}, u32[]{:S(2)}, u32[]{:S(2)}) collective-permute-start(bf16[32,16,128]{2,1,0:T(8,128)(2,1)S(1)} %pad_maximum_fusion.refs_0_), channel_id=1, source_target_pairs={{0,4},{1,5},{2,6},{3,7},{4,0},{5,1},{6,2},{7,3},{8,12},{9,13},{10,... | collective-permute-start | bytes 393224 | tf_op jit(solution)/shard_map/ppermute | solution.py:453
  76.9 10.7 %collective-permute-start.25 = (bf16[32,16,128]{2,1,0:T(8,128)(2,1)S(1)}, bf16[32,16,128]{2,1,0:T(8,128)(2,1)}, u32[]{:S(2)}, u32[]{:S(2)}) collective-permute-start(bf16[32,16,128]{2,1,0:T(8,128)(2,1)S(1)} %pad_maximum_fusion.1.refs_4_), channel_id=1, source_target_pairs={{0,1},{1,0},{2,3},{3,2},{4,5},{5,4},{6,7},{7,6},{8,9},{9,8},{10,11... | collective-permute-start | bytes 393224 | tf_op jit(solution)/shard_map/ppermute | solution.py:461
  76.9 11.7 %collective-permute-start.17 = (bf16[32,16,128]{2,1,0:T(8,128)(2,1)S(1)}, bf16[32,16,128]{2,1,0:T(8,128)(2,1)}, u32[]{:S(2)}, u32[]{:S(2)}) collective-permute-start(bf16[32,16,128]{2,1,0:T(8,128)(2,1)S(1)} %pad_maximum_fusion.refs_0_), channel_id=1, source_target_pairs={{0,2},{1,3},{2,0},{3,1},{4,6},{5,7},{6,4},{7,5},{8,10},{9,11},{10,... | collective-permute-start | bytes 393224 | tf_op jit(solution)/shard_map/ppermute | solution.py:453
  80.3 0.8 copy-start.3
  81.1 1.0 copy-start.7
  82.0 0.9 copy-start.11
  86.9 1.6 %collective-permute-start.21 = (bf16[32,16,128]{2,1,0:T(8,128)(2,1)S(1)}, bf16[32,16,128]{2,1,0:T(8,128)(2,1)S(1)}, u32[]{:S(2)}, u32[]{:S(2)}) collective-permute-start(bf16[32,16,128]{2,1,0:T(8,128)(2,1)S(1)} %pad_maximum_fusion.refs_0_), channel_id=1, source_target_pairs={{0,1},{1,0},{2,3},{3,2},{4,5},{5,4},{6,7},{7,6},{8,9},{9,8},{10,11... | collective-permute-start | bytes 393224 | tf_op jit(solution)/shard_map/ppermute | solution.py:461
  86.9 2.1 %collective-permute-start.27 = (bf16[32,16,128]{2,1,0:T(8,128)(2,1)S(1)}, bf16[32,16,128]{2,1,0:T(8,128)(2,1)S(1)}, u32[]{:S(2)}, u32[]{:S(2)}) collective-permute-start(bf16[32,16,128]{2,1,0:T(8,128)(2,1)S(1)} %collective-permute-done.19.refs_6_), channel_id=1, source_target_pairs={{0,1},{1,0},{2,3},{3,2},{4,5},{5,4},{6,7},{7,6},{8,9},{9,8},{10,11... | collective-permute-start | bytes 393224 | tf_op jit(solution)/shard_map/ppermute | solution.py:461
  87.4 5.7 %collective-permute-start.18 = (bf16[32,16,128]{2,1,0:T(8,128)(2,1)}, bf16[32,16,128]{2,1,0:T(8,128)(2,1)S(1)}, u32[]{:S(2)}, u32[]{:S(2)}) collective-permute-start(bf16[32,16,128]{2,1,0:T(8,128)(2,1)} %collective-permute-done.15.refs_1_), channel_id=1, source_target_pairs={{0,2},{1,3},{2,0},{3,1},{4,6},{5,7},{6,4},{7,5},{8,10},{9,11},{10,... | collective-permute-start | bytes 393224 | tf_op jit(solution)/shard_map/ppermute | solution.py:453
  87.6 5.6 %collective-permute-start.20 = (bf16[32,16,128]{2,1,0:T(8,128)(2,1)S(1)}, bf16[32,16,128]{2,1,0:T(8,128)(2,1)S(1)}, u32[]{:S(2)}, u32[]{:S(2)}) collective-permute-start(bf16[32,16,128]{2,1,0:T(8,128)(2,1)S(1)} %collective-permute-done.16.refs_5_), channel_id=1, source_target_pairs={{0,4},{1,5},{2,6},{3,7},{4,0},{5,1},{6,2},{7,3},{8,12},{9,13},{10,... | collective-permute-start | bytes 393224 | tf_op jit(solution)/shard_map/ppermute | solution.py:453
  88.5 5.1 %collective-permute-start.23 = (bf16[32,16,128]{2,1,0:T(8,128)(2,1)}, bf16[32,16,128]{2,1,0:T(8,128)(2,1)S(1)}, u32[]{:S(2)}, u32[]{:S(2)}) collective-permute-start(bf16[32,16,128]{2,1,0:T(8,128)(2,1)} %collective-permute-done.17.refs_2_), channel_id=1, source_target_pairs={{0,1},{1,0},{2,3},{3,2},{4,5},{5,4},{6,7},{7,6},{8,9},{9,8},{10,11... | collective-permute-start | bytes 393224 | tf_op jit(solution)/shard_map/ppermute | solution.py:461
  88.5 5.1 %collective-permute-start.22 = (bf16[32,16,128]{2,1,0:T(8,128)(2,1)}, bf16[32,16,128]{2,1,0:T(8,128)(2,1)S(1)}, u32[]{:S(2)}, u32[]{:S(2)}) collective-permute-start(bf16[32,16,128]{2,1,0:T(8,128)(2,1)} %collective-permute-done.15.refs_1_), channel_id=1, source_target_pairs={{0,1},{1,0},{2,3},{3,2},{4,5},{5,4},{6,7},{7,6},{8,9},{9,8},{10,11... | collective-permute-start | bytes 393224 | tf_op jit(solution)/shard_map/ppermute | solution.py:461
  89.1 4.6 %collective-permute-start.26 = (bf16[32,16,128]{2,1,0:T(8,128)(2,1)S(1)}, bf16[32,16,128]{2,1,0:T(8,128)(2,1)S(1)}, u32[]{:S(2)}, u32[]{:S(2)}) collective-permute-start(bf16[32,16,128]{2,1,0:T(8,128)(2,1)S(1)} %collective-permute-done.16.refs_5_), channel_id=1, source_target_pairs={{0,1},{1,0},{2,3},{3,2},{4,5},{5,4},{6,7},{7,6},{8,9},{9,8},{10,11... | collective-permute-start | bytes 393224 | tf_op jit(solution)/shard_map/ppermute | solution.py:461
  93.1 1.3 %collective-permute-start.24 = (bf16[32,16,128]{2,1,0:T(8,128)(2,1)S(1)}, bf16[32,16,128]{2,1,0:T(8,128)(2,1)S(1)}, u32[]{:S(2)}, u32[]{:S(2)}) collective-permute-start(bf16[32,16,128]{2,1,0:T(8,128)(2,1)S(1)} %collective-permute-done.18.refs_3_), channel_id=1, source_target_pairs={{0,1},{1,0},{2,3},{3,2},{4,5},{5,4},{6,7},{7,6},{8,9},{9,8},{10,11... | collective-permute-start | bytes 393224 | tf_op jit(solution)/shard_map/ppermute | solution.py:461
  93.1 1.5 %collective-permute-start.28 = (bf16[32,16,128]{2,1,0:T(8,128)(2,1)S(1)}, bf16[32,16,128]{2,1,0:T(8,128)(2,1)S(1)}, u32[]{:S(2)}, u32[]{:S(2)}) collective-permute-start(bf16[32,16,128]{2,1,0:T(8,128)(2,1)S(1)} %collective-permute-done.20.refs_7_), channel_id=1, source_target_pairs={{0,1},{1,0},{2,3},{3,2},{4,5},{5,4},{6,7},{7,6},{8,9},{9,8},{10,11... | collective-permute-start | bytes 393224 | tf_op jit(solution)/shard_map/ppermute | solution.py:461

commit v4 on v3

--- a/solution.py
+++ b/solution.py
@@ -119,24 +119,8 @@
     lines_ref[...] = jnp.zeros(lines_ref.shape, BF)
 
 
-def input_lines_kernel(owner, inner_ref, x_ref, outer_ref, lines_ref, planes_ref, rim):
+def lines_kernel(owner, inner_ref, x_ref, outer_ref, lines_ref, planes_ref, rim):
     fill_planes(x_ref, planes_ref, lines_ref, rim)
-    cut_lines(owner, inner_ref, outer_ref, lines_ref, planes_ref, rim)
-
-
-def grad_lines_kernel(owner, inner_ref, x_ref, outer_ref, bias_ref, *refs):
-    *got_refs, lines_ref, planes_ref, rim = refs
-    depth, _, channels = x_ref.shape
-    fill_planes(x_ref, planes_ref, lines_ref, rim)
-    terms = bias_ref[0].astype(F32)
-    for ref in got_refs:
-        terms = terms + ref[ref.shape[0] - 1].astype(F32)
-    low = split_in_three(terms[0:1] + terms[2:3] + terms[4:5])
-    high = split_in_three(terms[1:2] + terms[3:4] + terms[5:6])
-    rows = [jnp.concatenate([a, b[:, : channels - 128]], axis=1) for a, b in zip(low, high)]
-    extra = jnp.concatenate(rows + [jnp.zeros((EDGE - 3, channels), F32)], axis=0).astype(BF)
-    for q in range(lines_ref.shape[0]):
-        lines_ref[q, depth + 2] = extra
     cut_lines(owner, inner_ref, outer_ref, lines_ref, planes_ref, rim)
 
 
@@ -229,16 +213,11 @@
         put(unit, jnp.zeros((ROWS, 128), BF))
 
 
-def input_kernel(owner, x_ref, recv_ref, w_ref, mask_ref, pre_ref, out_ref, act_ref, gb_ref,
+def input_kernel(owner, x_ref, recv_ref, w_ref, mask_ref, pre_ref, out_ref, act_ref,
                  rim, patch, rows):
     channels = w_ref.shape[1]
     voxels = (x_ref.shape[0] - 2) * 64
     gather_windows(owner, x_ref, recv_ref, rim, patch)
-    last = recv_ref.shape[1] - 1
-    terms = recv_ref[0, last].astype(F32)
-    for q in range(1, recv_ref.shape[0]):
-        terms = terms + recv_ref[q, last].astype(F32)
-    gb_ref[...] = jnp.sum(terms, axis=0, keepdims=True)
     total = jnp.zeros((voxels, channels), F32)
     for dz in range(3):
         for k in range(9):
@@ -255,18 +234,26 @@
 
 
 def unfold_kernel(share, regions, n_leaves, owner, *refs):
-    *pieces, out_ref, flat = refs
+    *pieces, out_ref, gb_ref, flat = refs
     code = leaf_codes(owner.shape[0])
     slab = lax.axis_index("region")
     part = 0
     for piece in pieces:
-        for first in range(0, piece.shape[0], share):
+        for first in range(0, regions * share, share):
             rel, level = divmod(part, regions)
             colour = (rel // (n_leaves // 4)) % 2
             row = ((rel ^ code[colour]) * regions + (level ^ slab)) * (share * PITCH)
             for n in range(share):
                 flat[pl.ds(row + n * PITCH, ROWS), :] = piece[first + n].astype(F32)
             part += 1
+    terms = jnp.zeros((ROWS, 128), F32)
+    for piece in pieces:
+        if piece.shape[0] > regions * share:
+            terms = terms + piece[regions * share].astype(F32)
+    low_lanes = terms[0:1] + terms[2:3] + terms[4:5]
+    high_lanes = terms[1:2] + terms[3:4] + terms[5:6]
+    channels = gb_ref.shape[1]
+    gb_ref[...] = jnp.concatenate([low_lanes, high_lanes[:, : channels - 128]], axis=1)
     pitch = out_ref.shape[1] // (128 * ROWS) * PITCH
     low = lax.broadcasted_iota(jnp.int32, (8, 128), 1) < 64
 
@@ -336,11 +323,11 @@
         outer = lax.ppermute(plane(top * odd), "region", joined[1])
         return inner, outer
 
-    def cut(kernel, extra_planes, operands):
+    def cut(*operands):
         return pl.pallas_call(
-            kernel,
+            lines_kernel,
             out_shape=(
-                jax.ShapeDtypeStruct((tiles, depth + 2 + extra_planes, EDGE, channels), BF),
+                jax.ShapeDtypeStruct((tiles, depth + 2, EDGE, channels), BF),
                 jax.ShapeDtypeStruct((depth + 2, 64, channels), BF),
             ),
             in_specs=[SMEM] + [VMEM] * len(operands),
@@ -374,7 +361,7 @@
         scratch_shapes=[pltpu.VMEM((depth * EDGE, EDGE, channels), F32)],
         compiler_params=vmem(12),
     )(owner, features.reshape(flat), marks)
-    lines, planes = cut(input_lines_kernel, 0, (inner, occupied, outer))
+    lines, planes = cut(inner, occupied, outer)
     lines, weight = barrier((lines, weight))
     arrived = exchanged(lines)
     kernel = weight.reshape(27, channels, channels)
@@ -411,7 +398,9 @@
     for step in range(bits - 1):
         colours = [halve(c, "batch", tiles, 1 << o[step]) for c, o in zip(colours, orders)]
         if step == 0:
-            colours, inner, outer = barrier((colours, inner, outer))
+            lines, grad_planes = cut(inner, grad, outer)
+            colours, lines = barrier((colours, lines))
+            arrived = exchanged(lines)
 
     def level(k):
         return [c[k * share : (k + 1) * share] for c in colours]
@@ -423,21 +412,25 @@
         gots.append(lax.ppermute(sent, "region", pairs(regions, flip)))
         total = total + gots[-1][:-1].astype(F32)
     total = total.astype(BF)
-    lines, grad_planes = cut(grad_lines_kernel, 1, (inner, grad, outer, bias_terms, *gots))
-    arrived = exchanged(lines)
+    terms = bias_terms[0].astype(F32) + sum(got[-1].astype(F32) for got in gots)
+    terms = jnp.sum(terms[:6].reshape(3, 2, 128), axis=0)
+    columns = []
+    for _ in range(3):
+        columns.append(lax.reduce_precision(terms, 8, 7))
+        terms = terms - columns[-1]
+    column = jnp.pad(jnp.concatenate(columns, axis=0), ((0, ROWS - 6), (0, 0))).astype(BF)
 
     held = [total] + [
         lax.ppermute(total, "region", pairs(regions, flip)) for flip in range(1, regions)
     ]
-    grad_input, activation, total_bias = pl.pallas_call(
+    grad_input, activation = pl.pallas_call(
         input_kernel,
         out_shape=(
             jax.ShapeDtypeStruct(flat, BF),
             jax.ShapeDtypeStruct(flat, BF),
-            jax.ShapeDtypeStruct((1, channels), F32),
         ),
         in_specs=[SMEM] + [VMEM] * 5,
-        out_specs=(VMEM, VMEM, VMEM),
+        out_specs=(VMEM, VMEM),
         scratch_shapes=scratch,
         compiler_params=vmem(20),
         cost_estimate=pl.CostEstimate(
@@ -445,25 +438,26 @@
         ),
     )(owner, grad_planes, arrived, kernel, marks, act)
 
+    held, grad_input, activation = barrier((held, grad_input, activation))
     colours = [
-        [jnp.concatenate([h[c * share : (c + 1) * share] for h in held], axis=0)] for c in range(2)
+        [jnp.concatenate([h[c * share : (c + 1) * share] for h in held] + [column[None]][c:])]
+        for c in range(2)
     ]
     for step in reversed(range(bits - 1)):
         colours = [
             c + [lax.ppermute(x, "batch", pairs(tiles, 1 << o[step])) for x in c]
             for c, o in zip(colours, orders)
         ]
-        if step == bits - 2:
-            first = [c[1] for c in colours]
-            first, grad_input = barrier((first, grad_input))
-            colours = [[c[0], f] for c, f in zip(colours, first)]
     near = colours[0] + colours[1]
     far = [lax.ppermute(c, "batch", pairs(tiles, 1)) for c in near]
-    kernel_grad = pl.pallas_call(
+    kernel_grad, total_bias = pl.pallas_call(
         functools.partial(unfold_kernel, share, regions, n_leaves),
-        out_shape=jax.ShapeDtypeStruct((27, channels * channels), BF),
+        out_shape=(
+            jax.ShapeDtypeStruct((27, channels * channels), BF),
+            jax.ShapeDtypeStruct((1, channels), F32),
+        ),
         in_specs=[SMEM] + [VMEM] * len(near + far),
-        out_specs=VMEM,
+        out_specs=(VMEM, VMEM),
         scratch_shapes=[pltpu.VMEM((max(32 * units // 27, n_leaves * leaf_units) * PITCH, 128), F32)],
         compiler_params=vmem(20),
     )(owner, *near, *far)

time: 99.8 us -> 98.4 us (0.986)
  waiting for transfers between devices: 28.8 us -> 18.6 us
  starting transfers between devices: 33.8 us -> 38.9 us
  other arithmetic: 2.26 us -> 4.99 us
    ppermute x5, waiting for transfers between devices: 13.6 us -> 5.41 us  [halve(): got = lax.ppermute(x[half:].astype(BF), axis, pairs(count, flip))]
    ppermute x3, waiting for transfers between devices: 3.76 us -> 0.01 us  [body(): gots.append(lax.ppermute(sent, 'region', pairs(regions, flip)))]
    ppermute x6, waiting for transfers between devices: 4 us -> 7.61 us  [body(): lax.ppermute(x, 'batch', pairs(tiles, 1 << o[step]))]
    unnamed x24 -> x16, local copies, waits for them, and re-layouts: 5.76 us -> 2.56 us
    all_to_all x2, waiting for transfers between devices: 6.39 us -> 3.25 us  [exchanged(): return lax.all_to_all(lines, 'batch', 0, 0, tiled=True)]
    slice x0 -> x3, local copies, waits for them, and re-layouts: none -> 2.04 us  [body(): got[-1].astype(F32)]
    another operation x3 -> x4, other arithmetic: 0.36 us -> 2.29 us
    ppermute x3, starting transfers between devices: 4.45 us -> 6.28 us  [body(): gots.append(lax.ppermute(sent, 'region', pairs(regions, flip)))]
  transfers between devices with their start and end apart: 31 -> 31, of which waited for: 12 -> 11; matrix products, arithmetic and copies ran while one was open for 7% -> 12% of each run, Pallas kernels for 6% -> 7%
where the time goes in v4:
time: 98.4 us; the launch traced here: 97.4 us
  starting transfers between devices  38.9 us (40%)
  Pallas kernels  20.6 us (21%)
  waiting for transfers between devices  18.6 us (19%)
  local copies, waits for them, and re-layouts  13.5 us (14%)
  other arithmetic  4.99 us (5%)
    pallas_call x1, Pallas kernels, body(): pl.pallas_call(functools.partial(forward_kernel, share, regions, n_leaves...  8.08 us
    ppermute x6, waiting for transfers between devices, body(): lax.ppermute(x, 'batch', pairs(tiles, 1 << o[step]))  7.61 us
    ppermute x2, starting transfers between devices, rims(): inner = lax.ppermute(plane(top * (1 - odd)), 'region', joined[0])  7.43 us
    all_to_all x2, starting transfers between devices, exchanged(): return lax.all_to_all(lines, 'batch', 0, 0, tiled=True)  7.22 us
    ppermute x6, starting transfers between devices, body(): lax.ppermute(x, 'batch', pairs(tiles, 1 << o[step]))  6.69 us
    ppermute x3, starting transfers between devices, body(): gots.append(lax.ppermute(sent, 'region', pairs(regions, flip)))  6.28 us
    ppermute x5, waiting for transfers between devices, halve(): got = lax.ppermute(x[half:].astype(BF), axis, pairs(count, flip))  5.41 us
    ppermute x3, starting transfers between devices, body(): lax.ppermute(total, 'region', pairs(regions, flip))  4.45 us
  transfers between devices with their start and end apart: 31, of which 11 were waited for; matrix products, arithmetic and copies ran while one was open for 12% of the time, Pallas kernels for 7%

profile of v4, /device:TPU:0, one launch (start us, length us, event | category | flops | bytes accessed | tf_op | source)
XLA Modules:
  0.0 97.4 jit_solution(6955123572287506763)
XLA Ops:
  0.6 0.8 constant_dynamic-slice_fusion.3
  1.4 0.1 reshape.137
  1.5 0.8 fusion.14
  2.4 3.0 %collective-permute-start = (bf16[1,64,192]{2,1,0:T(8,128)(2,1)S(1)}, bf16[1,64,192]{2,1,0:T(8,128)(2,1)S(1)}, u32[]{:S(2)}, u32[]{:S(2)}) collective-permute-start(bf16[1,64,192]{2,1,0:T(8,128)(2,1)S(1)} %broadcast_multiply_fusion.1), channel_id=1, source_target_pairs={{0,8},{8,0},{16,24},{24,16},{1,9},{9,1},{17,25},{25,17},{2,10},{10... | collective-permute-start | bytes 73736 | tf_op jit(solution)/shard_map/ppermute | solution.py:322
  5.4 0.1 reshape.140
  5.6 0.7 collective-permute-start.1
  6.2 0.8 reshape.139.mask_ref
  7.0 0.9 copy-done
  7.9 0.7 copy-done.1
  8.6 1.3 %shard_map.93.x_ref = bf16[8,64,192]{2,1,0:T(8,128)(2,1)S(1)} custom-call(s32[8]{0:T(128)S(1)} %copy-done.1, bf16[64,1536]{1,0:T(8,128)(2,1)S(1)} %bitcast.17, s32[64,8]{1,0:T(8,128)S(1)} %reshape.139.mask_ref), custom_call_target="tpu_custom_call" | custom-call | tf_op jit(solution)/shard_map/pallas_call | solution.py:356
  9.9 1.7 %shard_map.94 = (bf16[8,10,8,192]{3,2,1,0:T(8,128)(2,1)}, bf16[10,64,192]{2,1,0:T(8,128)(2,1)S(1)}) custom-call(s32[8]{0:T(128)S(1)} %copy-done.1, bf16[1,64,192]{2,1,0:T(8,128)(2,1)S(1)} %collective-permute-done.inner_ref, bf16[8,64,192]{2,1,0:T(8,128)(2,1)S(1)} %shard_map.93.x_ref, bf16[1,64,192]{2,1,0:T(8,128)(2,1)S(1)} %collective-permute-done.1.outer_ref), custom_call_target="tpu_custom_call" | custom-call | tf_op jit(solution)/shard_map/pallas_call | solution.py:327
  11.6 3.6 %all-to-all-start = ((bf16[8,10,8,192]{3,2,1,0:T(8,128)(2,1)}), bf16[8,10,8,192]{3,2,1,0:T(8,128)(2,1)S(1)}, u32[]{:S(2)}, u32[]{:S(2)}) async-start(bf16[8,10,8,192]{3,2,1,0:T(8,128)(2,1)} %get-tuple-element.29), calls=%async_computation | async-start | bytes 655360 | tf_op jit(solution)/shard_map/all_to_all | solution.py:340
  15.2 4.4 %reshape.141.w_ref = bf16[27,192,192]{2,1,0:T(8,128)(2,1)S(1)} reshape(bf16[27,36864]{1,0:T(8,128)(2,1)} %param.9) | data formatting | bytes 3981312 | tf_op jit(solution)/shard_map/reshape | solution.py:367
  19.6 3.2 %all-to-all-done.recv_ref = bf16[8,10,8,192]{3,2,1,0:T(8,128)(2,1)S(1)} async-done(((bf16[8,10,8,192]{3,2,1,0:T(8,128)(2,1)}), bf16[8,10,8,192]{3,2,1,0:T(8,128)(2,1)S(1)}, u32[]{:S(2)}, u32[]{:S(2)}) %all-to-all-start) | async-done | bytes 245792 | tf_op jit(solution)/shard_map/all_to_all | solution.py:340
  22.9 8.1 %shard_map.95 = (bf16[512,192]{1,0:T(8,128)(2,1)S(1)}, bf16[512,192]{1,0:T(8,128)(2,1)S(1)}, bf16[1,16,128]{2,1,0:T(8,128)(2,1)S(1)}, bf16[512,16,128]{2,1,0:T(8,128)(2,1)S(1)}) custom-call(s32[8]{0:T(128)S(1)} %copy-done.2, bf16[10,64,192]{2,1,0:T(8,128)(2,1)S(1)} %get-tuple-element.27.x_ref, bf16[8,10,8,192]{3,2,1,0:T(8,128)(2,1)S(1)} %all-to-all-done.recv_ref, ...), custom_call_target="tpu_custom_call" | custom-call | flops 2038431744 | bytes 6291456 | tf_op jit(solution)/shard_map/pallas_call | solution.py:369
  31.0 0.2 slice.117
  31.2 2.6 %collective-permute-done.2 = bf16[256,16,128]{2,1,0:T(8,128)(2,1)S(1)} collective-permute-done((bf16[256,16,128]{2,1,0:T(8,128)(2,1)S(1)}, bf16[256,16,128]{2,1,0:T(8,128)(2,1)S(1)}, u32[]{:S(2)}, u32[]{:S(2)}) %collective-permute-start.2) | collective-permute-done | bytes 1048608 | tf_op jit(solution)/shard_map/ppermute | solution.py:391
  33.9 0.3 fusion.15
  34.2 0.6 collective-permute-start.4
  34.8 0.6 collective-permute-start.3
  35.4 4.4 %collective-permute-start.5 = (bf16[1,64,192]{2,1,0:T(8,128)(2,1)S(1)}, bf16[1,64,192]{2,1,0:T(8,128)(2,1)S(1)}, u32[]{:S(2)}, u32[]{:S(2)}) collective-permute-start(bf16[1,64,192]{2,1,0:T(8,128)(2,1)S(1)} %get-tuple-element.61), channel_id=1, source_target_pairs={{0,8},{8,0},{16,24},{24,16},{1,9},{9,1},{17,25},{25,17},{2,10},{10... | collective-permute-start | bytes 73736 | tf_op jit(solution)/shard_map/ppermute | solution.py:322
  39.8 0.7 collective-permute-start.6
  40.5 1.2 %collective-permute-done.5.inner_ref = bf16[1,64,192]{2,1,0:T(8,128)(2,1)S(1)} collective-permute-done((bf16[1,64,192]{2,1,0:T(8,128)(2,1)S(1)}, bf16[1,64,192]{2,1,0:T(8,128)(2,1)S(1)}, u32[]{:S(2)}, u32[]{:S(2)}) %collective-permute-start.5) | collective-permute-done | bytes 24608 | tf_op jit(solution)/shard_map/ppermute | solution.py:322
  41.7 1.7 %shard_map.96 = (bf16[8,10,8,192]{3,2,1,0:T(8,128)(2,1)}, bf16[10,64,192]{2,1,0:T(8,128)(2,1)S(1)}) custom-call(s32[8]{0:T(128)S(1)} %copy-done.2, bf16[1,64,192]{2,1,0:T(8,128)(2,1)S(1)} %collective-permute-done.5.inner_ref, bf16[8,64,192]{2,1,0:T(8,128)(2,1)S(1)} %bitcast.16, bf16[1,64,192]{2,1,0:T(8,128)(2,1)S(1)} %collective-permute-done.6.outer_ref), custom_call_target="tpu_custom_call" | custom-call | tf_op jit(solution)/shard_map/pallas_call | solution.py:327
  43.4 0.1 slice_add_fusion
  43.6 1.4 %collective-permute-start.8 = (bf16[32,16,128]{2,1,0:T(8,128)(2,1)S(1)}, bf16[32,16,128]{2,1,0:T(8,128)(2,1)S(1)}, u32[]{:S(2)}, u32[]{:S(2)}) collective-permute-start(bf16[32,16,128]{2,1,0:T(8,128)(2,1)S(1)} %slice.193), channel_id=1, source_target_pairs={{0,2},{1,3},{2,0},{3,1},{4,6},{5,7},{6,4},{7,5},{8,10},{9,11},{10,... | collective-permute-start | bytes 393224 | tf_op jit(solution)/shard_map/ppermute | solution.py:391
  45.0 1.5 %collective-permute-start.7 = (bf16[32,16,128]{2,1,0:T(8,128)(2,1)S(1)}, bf16[32,16,128]{2,1,0:T(8,128)(2,1)S(1)}, u32[]{:S(2)}, u32[]{:S(2)}) collective-permute-start(bf16[32,16,128]{2,1,0:T(8,128)(2,1)S(1)} %slice.194), channel_id=1, source_target_pairs={{0,4},{1,5},{2,6},{3,7},{4,0},{5,1},{6,2},{7,3},{8,12},{9,13},{10,... | collective-permute-start | bytes 393224 | tf_op jit(solution)/shard_map/ppermute | solution.py:391
  46.5 2.1 %collective-permute-done.8 = bf16[32,16,128]{2,1,0:T(8,128)(2,1)S(1)} collective-permute-done((bf16[32,16,128]{2,1,0:T(8,128)(2,1)S(1)}, bf16[32,16,128]{2,1,0:T(8,128)(2,1)S(1)}, u32[]{:S(2)}, u32[]{:S(2)}) %collective-permute-start.8) | collective-permute-done | bytes 131104 | tf_op jit(solution)/shard_map/ppermute | solution.py:391
  48.6 0.7 fusion.17
  49.4 0.7 collective-permute-done.7
  50.0 0.8 fusion.16
  50.8 0.7 pad_maximum_fusion.3
  51.5 3.9 %collective-permute-start.11 = (bf16[17,16,128]{2,1,0:T(8,128)(2,1)}, bf16[17,16,128]{2,1,0:T(8,128)(2,1)}, u32[]{:S(2)}, u32[]{:S(2)}) collective-permute-start(bf16[17,16,128]{2,1,0:T(8,128)(2,1)} %get-tuple-element.80), channel_id=1, source_target_pairs={{0,8},{8,0},{16,24},{24,16},{1,9},{9,1},{17,25},{25,17},{2,10},{10... | collective-permute-start | bytes 208904 | tf_op jit(solution)/shard_map/ppermute | solution.py:412
  55.4 2.4 %collective-permute-start.9 = (bf16[17,16,128]{2,1,0:T(8,128)(2,1)S(1)}, bf16[17,16,128]{2,1,0:T(8,128)(2,1)}, u32[]{:S(2)}, u32[]{:S(2)}) collective-permute-start(bf16[17,16,128]{2,1,0:T(8,128)(2,1)S(1)} %get-tuple-element.78), channel_id=1, source_target_pairs={{0,24},{8,16},{16,8},{24,0},{1,25},{9,17},{17,9},{25,1},{2,26},{10... | collective-permute-start | bytes 208904 | tf_op jit(solution)/shard_map/ppermute | solution.py:412
  57.8 3.6 %all-to-all-start.1 = ((bf16[8,10,8,192]{3,2,1,0:T(8,128)(2,1)}), bf16[8,10,8,192]{3,2,1,0:T(8,128)(2,1)S(1)}, u32[]{:S(2)}, u32[]{:S(2)}) async-start(bf16[8,10,8,192]{3,2,1,0:T(8,128)(2,1)} %get-tuple-element.38), calls=%async_computation.1 | async-start | bytes 655360 | tf_op jit(solution)/shard_map/all_to_all | solution.py:340
  61.4 0.8 slice.156
  62.2 0.8 slice.154
  63.1 0.9 fusion.2
  64.0 1.2 %collective-permute-start.12 = (bf16[16,16,128]{2,1,0:T(8,128)(2,1)S(1)}, bf16[16,16,128]{2,1,0:T(8,128)(2,1)}, u32[]{:S(2)}, u32[]{:S(2)}) collective-permute-start(bf16[16,16,128]{2,1,0:T(8,128)(2,1)S(1)} %fusion.2), channel_id=1, source_target_pairs={{0,8},{8,0},{16,24},{24,16},{1,9},{9,1},{17,25},{25,17},{2,10},{10... | collective-permute-start | bytes 196616 | tf_op jit(solution)/shard_map/ppermute | solution.py:424
  65.2 0.9 collective-permute-start.13
  66.1 2.4 %collective-permute-start.14 = (bf16[16,16,128]{2,1,0:T(8,128)(2,1)S(1)}, bf16[16,16,128]{2,1,0:T(8,128)(2,1)S(1)}, u32[]{:S(2)}, u32[]{:S(2)}) collective-permute-start(bf16[16,16,128]{2,1,0:T(8,128)(2,1)S(1)} %fusion.2), channel_id=1, source_target_pairs={{0,24},{8,16},{16,8},{24,0},{1,25},{9,17},{17,9},{25,1},{2,26},{10... | collective-permute-start | bytes 196616 | tf_op jit(solution)/shard_map/ppermute | solution.py:424
  68.5 0.7 slice.168
  69.2 0.7 slice.167
  69.9 0.7 slice.166
  70.6 0.5 reduce-precision_convert_fusion.1
  71.1 0.9 copy-done.6
  72.0 3.9 %shard_map.97 = (bf16[64,1536]{1,0:T(8,128)(2,1)}, bf16[64,1536]{1,0:T(8,128)(2,1)}) custom-call(s32[8]{0:T(128)S(1)} %copy-done.2, bf16[10,64,192]{2,1,0:T(8,128)(2,1)S(1)} %get-tuple-element.37.x_ref, bf16[8,10,8,192]{3,2,1,0:T(8,128)(2,1)S(1)} %all-to-all-done.1.recv_ref, bf16[27,192,192]{2,1,0:T(8,128)(2,1)S(1)} %reshape.141.w_ref, ...), custom_call_target="tpu_custom_call" | custom-call | flops 1019215872 | bytes 3145728 | tf_op jit(solution)/shard_map/pallas_call | solution.py:426
  76.0 0.8 fusion.22
  76.8 1.8 %collective-permute-start.15 = (bf16[33,16,128]{2,1,0:T(8,128)(2,1)S(1)}, bf16[33,16,128]{2,1,0:T(8,128)(2,1)S(1)}, u32[]{:S(2)}, u32[]{:S(2)}) collective-permute-start(bf16[33,16,128]{2,1,0:T(8,128)(2,1)S(1)} %constant_dynamic-update-slice_fusion.refs_0_), channel_id=1, source_target_pairs={{0,4},{1,5},{2,6},{3,7},{4,0},{5,1},{6,2},{7,3},{8,12},{9,13},{10,... | collective-permute-start | bytes 405512 | tf_op jit(solution)/shard_map/ppermute | solution.py:448
  78.7 1.5 %collective-permute-start.18 = (bf16[32,16,128]{2,1,0:T(8,128)(2,1)S(1)}, bf16[32,16,128]{2,1,0:T(8,128)(2,1)S(1)}, u32[]{:S(2)}, u32[]{:S(2)}) collective-permute-start(bf16[32,16,128]{2,1,0:T(8,128)(2,1)S(1)} %pad_maximum_fusion.refs_4_), channel_id=1, source_target_pairs={{0,2},{1,3},{2,0},{3,1},{4,6},{5,7},{6,4},{7,5},{8,10},{9,11},{10,... | collective-permute-start | bytes 393224 | tf_op jit(solution)/shard_map/ppermute | solution.py:448
  80.2 0.5 collective-permute-start.19
  80.8 0.3 collective-permute-start.16
  81.0 2.8 %collective-permute-done.18.refs_5_ = bf16[32,16,128]{2,1,0:T(8,128)(2,1)S(1)} collective-permute-done((bf16[32,16,128]{2,1,0:T(8,128)(2,1)S(1)}, bf16[32,16,128]{2,1,0:T(8,128)(2,1)S(1)}, u32[]{:S(2)}, u32[]{:S(2)}) %collective-permute-start.18) | collective-permute-done | bytes 131104 | tf_op jit(solution)/shard_map/ppermute | solution.py:448
  83.8 2.5 %collective-permute-start.17 = (bf16[33,16,128]{2,1,0:T(8,128)(2,1)S(1)}, bf16[33,16,128]{2,1,0:T(8,128)(2,1)S(1)}, u32[]{:S(2)}, u32[]{:S(2)}) collective-permute-start(bf16[33,16,128]{2,1,0:T(8,128)(2,1)S(1)} %collective-permute-done.15.refs_1_), channel_id=1, source_target_pairs={{0,2},{1,3},{2,0},{3,1},{4,6},{5,7},{6,4},{7,5},{8,10},{9,11},{10,... | collective-permute-start | bytes 405512 | tf_op jit(solution)/shard_map/ppermute | solution.py:448
  86.4 0.3 collective-permute-start.26
  86.6 0.1 collective-permute-done.16.refs_2_
  86.8 0.2 collective-permute-start.22
  86.9 0.4 collective-permute-start.23
  87.3 3.3 %collective-permute-done.17.refs_3_ = bf16[33,16,128]{2,1,0:T(8,128)(2,1)S(1)} collective-permute-done((bf16[33,16,128]{2,1,0:T(8,128)(2,1)S(1)}, bf16[33,16,128]{2,1,0:T(8,128)(2,1)S(1)}, u32[]{:S(2)}, u32[]{:S(2)}) %collective-permute-start.17) | collective-permute-done | bytes 135200 | tf_op jit(solution)/shard_map/ppermute | solution.py:448
  90.6 1.4 %collective-permute-done.20.refs_7_ = bf16[32,16,128]{2,1,0:T(8,128)(2,1)S(1)} collective-permute-done((bf16[32,16,128]{2,1,0:T(8,128)(2,1)S(1)}, bf16[32,16,128]{2,1,0:T(8,128)(2,1)S(1)}, u32[]{:S(2)}, u32[]{:S(2)}) %collective-permute-start.20) | collective-permute-done | bytes 131104 | tf_op jit(solution)/shard_map/ppermute | solution.py:448
  92.0 0.5 collective-permute-start.28
  92.5 0.8 collective-permute-done.27.refs_14_
  93.3 0.2 collective-permute-done.28.refs_15_
  93.5 3.9 %shard_map.98 = (bf16[27,36864]{1,0:T(8,128)(2,1)}, f32[1,192]{1,0:T(1,128)}) custom-call(s32[8]{0:T(128)S(1)} %copy-done.2, bf16[33,16,128]{2,1,0:T(8,128)(2,1)S(1)} %constant_dynamic-update-slice_fusion.refs_0_, bf16[33,16,128]{2,1,0:T(8,128)(2,1)S(1)} %collective-permute-done.15.refs_1_, bf16[33,16,128]{2,1,0:T(8,128)(2,1)S(1)} %collective-permute-done.16.refs_2_, ...), custom_call_target="tpu_custom_call" | custom-call | tf_op jit(solution)/shard_map/pallas_call | solution.py:453
  (55 shorter events, 0.5 us)
Async XLA Ops:
  2.4 7.5 %collective-permute-start = (bf16[1,64,192]{2,1,0:T(8,128)(2,1)S(1)}, bf16[1,64,192]{2,1,0:T(8,128)(2,1)S(1)}, u32[]{:S(2)}, u32[]{:S(2)}) collective-permute-start(bf16[1,64,192]{2,1,0:T(8,128)(2,1)S(1)} %broadcast_multiply_fusion.1), channel_id=1, source_target_pairs={{0,8},{8,0},{16,24},{24,16},{1,9},{9,1},{17,25},{25,17},{2,10},{10... | collective-permute-start | bytes 73736 | tf_op jit(solution)/shard_map/ppermute | solution.py:322
  5.6 4.3 %collective-permute-start.1 = (bf16[1,64,192]{2,1,0:T(8,128)(2,1)S(1)}, bf16[1,64,192]{2,1,0:T(8,128)(2,1)S(1)}, u32[]{:S(2)}, u32[]{:S(2)}) collective-permute-start(bf16[1,64,192]{2,1,0:T(8,128)(2,1)S(1)} %broadcast_multiply_fusion), channel_id=1, source_target_pairs={{8,16},{16,8},{9,17},{17,9},{10,18},{18,10},{11,19},{19,11},{12,20... | collective-permute-start | bytes 73736 | tf_op jit(solution)/shard_map/ppermute | solution.py:323
  7.0 0.9 copy-start
  7.9 0.7 copy-start.1
  11.6 11.2 %all-to-all-start = ((bf16[8,10,8,192]{3,2,1,0:T(8,128)(2,1)}), bf16[8,10,8,192]{3,2,1,0:T(8,128)(2,1)S(1)}, u32[]{:S(2)}, u32[]{:S(2)}) async-start(bf16[8,10,8,192]{3,2,1,0:T(8,128)(2,1)} %get-tuple-element.29), calls=%async_computation | async-start | bytes 655360 | tf_op jit(solution)/shard_map/all_to_all | solution.py:340
  15.2 7.6 %copy-start.2 = (s32[8]{0:T(128)S(1)}, s32[8]{0:T(128)}, u32[]{:S(2)}) copy-start(s32[8]{0:T(128)} %owner.11) | copy-start | bytes 100
  15.2 7.6 %copy-start.3 = (bf16[8,8,1536]{2,1,0:T(8,128)(2,1)S(1)}, bf16[8,8,1536]{2,1,0:T(8,128)(2,1)}, u32[]{:S(2)}) copy-start(bf16[8,8,1536]{2,1,0:T(8,128)(2,1)} %param.11) | copy-start | bytes 589828
  15.2 7.6 %copy-start.4 = (f32[192]{0:T(256)S(1)}, f32[192]{0:T(256)}, u32[]{:S(2)}) copy-start(f32[192]{0:T(256)} %param.10) | copy-start | bytes 2308
  31.0 3.2 %copy-start.5 = (bf16[512,192]{1,0:T(8,128)(2,1)}, bf16[512,192]{1,0:T(8,128)(2,1)S(1)}, u32[]{:S(2)}) copy-start(bf16[512,192]{1,0:T(8,128)(2,1)S(1)} %get-tuple-element.39.pre_ref) | copy-start | bytes 589828
  31.2 2.7 %collective-permute-start.2 = (bf16[256,16,128]{2,1,0:T(8,128)(2,1)S(1)}, bf16[256,16,128]{2,1,0:T(8,128)(2,1)S(1)}, u32[]{:S(2)}, u32[]{:S(2)}) collective-permute-start(bf16[256,16,128]{2,1,0:T(8,128)(2,1)S(1)} %slice.117), channel_id=1, source_target_pairs={{0,1},{1,0},{2,3},{3,2},{4,5},{5,4},{6,7},{7,6},{8,9},{9,8},{10,11... | collective-permute-start | bytes 3145736 | tf_op jit(solution)/shard_map/ppermute | solution.py:391
  34.2 9.2 %collective-permute-start.4 = (bf16[64,16,128]{2,1,0:T(8,128)(2,1)S(1)}, bf16[64,16,128]{2,1,0:T(8,128)(2,1)S(1)}, u32[]{:S(2)}, u32[]{:S(2)}) collective-permute-start(bf16[64,16,128]{2,1,0:T(8,128)(2,1)S(1)} %get-tuple-element.58), channel_id=1, source_target_pairs={{0,4},{1,5},{2,6},{3,7},{4,0},{5,1},{6,2},{7,3},{8,12},{9,13},{10,... | collective-permute-start | bytes 786440 | tf_op jit(solution)/shard_map/ppermute | solution.py:391
  34.8 8.6 %collective-permute-start.3 = (bf16[64,16,128]{2,1,0:T(8,128)(2,1)S(1)}, bf16[64,16,128]{2,1,0:T(8,128)(2,1)S(1)}, u32[]{:S(2)}, u32[]{:S(2)}) collective-permute-start(bf16[64,16,128]{2,1,0:T(8,128)(2,1)S(1)} %get-tuple-element.59), channel_id=1, source_target_pairs={{0,2},{1,3},{2,0},{3,1},{4,6},{5,7},{6,4},{7,5},{8,10},{9,11},{10,... | collective-permute-start | bytes 786440 | tf_op jit(solution)/shard_map/ppermute | solution.py:391
  35.4 6.3 %collective-permute-start.5 = (bf16[1,64,192]{2,1,0:T(8,128)(2,1)S(1)}, bf16[1,64,192]{2,1,0:T(8,128)(2,1)S(1)}, u32[]{:S(2)}, u32[]{:S(2)}) collective-permute-start(bf16[1,64,192]{2,1,0:T(8,128)(2,1)S(1)} %get-tuple-element.61), channel_id=1, source_target_pairs={{0,8},{8,0},{16,24},{24,16},{1,9},{9,1},{17,25},{25,17},{2,10},{10... | collective-permute-start | bytes 73736 | tf_op jit(solution)/shard_map/ppermute | solution.py:322
  39.8 1.9 %collective-permute-start.6 = (bf16[1,64,192]{2,1,0:T(8,128)(2,1)S(1)}, bf16[1,64,192]{2,1,0:T(8,128)(2,1)S(1)}, u32[]{:S(2)}, u32[]{:S(2)}) collective-permute-start(bf16[1,64,192]{2,1,0:T(8,128)(2,1)S(1)} %get-tuple-element.60), channel_id=1, source_target_pairs={{8,16},{16,8},{9,17},{17,9},{10,18},{18,10},{11,19},{19,11},{12,20... | collective-permute-start | bytes 73736 | tf_op jit(solution)/shard_map/ppermute | solution.py:323
  43.6 5.0 %collective-permute-start.8 = (bf16[32,16,128]{2,1,0:T(8,128)(2,1)S(1)}, bf16[32,16,128]{2,1,0:T(8,128)(2,1)S(1)}, u32[]{:S(2)}, u32[]{:S(2)}) collective-permute-start(bf16[32,16,128]{2,1,0:T(8,128)(2,1)S(1)} %slice.193), channel_id=1, source_target_pairs={{0,2},{1,3},{2,0},{3,1},{4,6},{5,7},{6,4},{7,5},{8,10},{9,11},{10,... | collective-permute-start | bytes 393224 | tf_op jit(solution)/shard_map/ppermute | solution.py:391
  45.0 5.0 %collective-permute-start.7 = (bf16[32,16,128]{2,1,0:T(8,128)(2,1)S(1)}, bf16[32,16,128]{2,1,0:T(8,128)(2,1)S(1)}, u32[]{:S(2)}, u32[]{:S(2)}) collective-permute-start(bf16[32,16,128]{2,1,0:T(8,128)(2,1)S(1)} %slice.194), channel_id=1, source_target_pairs={{0,4},{1,5},{2,6},{3,7},{4,0},{5,1},{6,2},{7,3},{8,12},{9,13},{10,... | collective-permute-start | bytes 393224 | tf_op jit(solution)/shard_map/ppermute | solution.py:391
  51.5 11.6 %collective-permute-start.11 = (bf16[17,16,128]{2,1,0:T(8,128)(2,1)}, bf16[17,16,128]{2,1,0:T(8,128)(2,1)}, u32[]{:S(2)}, u32[]{:S(2)}) collective-permute-start(bf16[17,16,128]{2,1,0:T(8,128)(2,1)} %get-tuple-element.80), channel_id=1, source_target_pairs={{0,8},{8,0},{16,24},{24,16},{1,9},{9,1},{17,25},{25,17},{2,10},{10... | collective-permute-start | bytes 208904 | tf_op jit(solution)/shard_map/ppermute | solution.py:412
  55.4 7.7 %collective-permute-start.10 = (bf16[17,16,128]{2,1,0:T(8,128)(2,1)S(1)}, bf16[17,16,128]{2,1,0:T(8,128)(2,1)}, u32[]{:S(2)}, u32[]{:S(2)}) collective-permute-start(bf16[17,16,128]{2,1,0:T(8,128)(2,1)S(1)} %get-tuple-element.79), channel_id=1, source_target_pairs={{0,16},{8,24},{16,0},{24,8},{1,17},{9,25},{17,1},{25,9},{2,18},{10... | collective-permute-start | bytes 208904 | tf_op jit(solution)/shard_map/ppermute | solution.py:412
  55.4 7.7 %collective-permute-start.9 = (bf16[17,16,128]{2,1,0:T(8,128)(2,1)S(1)}, bf16[17,16,128]{2,1,0:T(8,128)(2,1)}, u32[]{:S(2)}, u32[]{:S(2)}) collective-permute-start(bf16[17,16,128]{2,1,0:T(8,128)(2,1)S(1)} %get-tuple-element.78), channel_id=1, source_target_pairs={{0,24},{8,16},{16,8},{24,0},{1,25},{9,17},{17,9},{25,1},{2,26},{10... | collective-permute-start | bytes 208904 | tf_op jit(solution)/shard_map/ppermute | solution.py:412
  57.8 13.3 %all-to-all-start.1 = ((bf16[8,10,8,192]{3,2,1,0:T(8,128)(2,1)}), bf16[8,10,8,192]{3,2,1,0:T(8,128)(2,1)S(1)}, u32[]{:S(2)}, u32[]{:S(2)}) async-start(bf16[8,10,8,192]{3,2,1,0:T(8,128)(2,1)} %get-tuple-element.38), calls=%async_computation.1 | async-start | bytes 655360 | tf_op jit(solution)/shard_map/all_to_all | solution.py:340
  64.0 11.9 %collective-permute-start.12 = (bf16[16,16,128]{2,1,0:T(8,128)(2,1)S(1)}, bf16[16,16,128]{2,1,0:T(8,128)(2,1)}, u32[]{:S(2)}, u32[]{:S(2)}) collective-permute-start(bf16[16,16,128]{2,1,0:T(8,128)(2,1)S(1)} %fusion.2), channel_id=1, source_target_pairs={{0,8},{8,0},{16,24},{24,16},{1,9},{9,1},{17,25},{25,17},{2,10},{10... | collective-permute-start | bytes 196616 | tf_op jit(solution)/shard_map/ppermute | solution.py:424
  65.2 10.7 %collective-permute-start.13 = (bf16[16,16,128]{2,1,0:T(8,128)(2,1)S(1)}, bf16[16,16,128]{2,1,0:T(8,128)(2,1)S(1)}, u32[]{:S(2)}, u32[]{:S(2)}) collective-permute-start(bf16[16,16,128]{2,1,0:T(8,128)(2,1)S(1)} %fusion.2), channel_id=1, source_target_pairs={{0,16},{8,24},{16,0},{24,8},{1,17},{9,25},{17,1},{25,9},{2,18},{10... | collective-permute-start | bytes 196616 | tf_op jit(solution)/shard_map/ppermute | solution.py:424
  66.1 9.8 %collective-permute-start.14 = (bf16[16,16,128]{2,1,0:T(8,128)(2,1)S(1)}, bf16[16,16,128]{2,1,0:T(8,128)(2,1)S(1)}, u32[]{:S(2)}, u32[]{:S(2)}) collective-permute-start(bf16[16,16,128]{2,1,0:T(8,128)(2,1)S(1)} %fusion.2), channel_id=1, source_target_pairs={{0,24},{8,16},{16,8},{24,0},{1,25},{9,17},{17,9},{25,1},{2,26},{10... | collective-permute-start | bytes 196616 | tf_op jit(solution)/shard_map/ppermute | solution.py:424
  71.1 1.0 copy-start.6
  72.0 4.8 %copy-start.7 = (bf16[2,128]{1,0:T(2,128)(2,1)S(1)}, bf16[2,128]{1,0:T(2,128)(2,1)}, u32[]{:S(2)}) copy-start(bf16[2,128]{1,0:T(2,128)(2,1)} %get-tuple-element.85) | copy-start | bytes 1540
  76.8 7.0 %collective-permute-start.15 = (bf16[33,16,128]{2,1,0:T(8,128)(2,1)S(1)}, bf16[33,16,128]{2,1,0:T(8,128)(2,1)S(1)}, u32[]{:S(2)}, u32[]{:S(2)}) collective-permute-start(bf16[33,16,128]{2,1,0:T(8,128)(2,1)S(1)} %constant_dynamic-update-slice_fusion.refs_0_), channel_id=1, source_target_pairs={{0,4},{1,5},{2,6},{3,7},{4,0},{5,1},{6,2},{7,3},{8,12},{9,13},{10,... | collective-permute-start | bytes 405512 | tf_op jit(solution)/shard_map/ppermute | solution.py:448
  78.7 5.2 %collective-permute-start.18 = (bf16[32,16,128]{2,1,0:T(8,128)(2,1)S(1)}, bf16[32,16,128]{2,1,0:T(8,128)(2,1)S(1)}, u32[]{:S(2)}, u32[]{:S(2)}) collective-permute-start(bf16[32,16,128]{2,1,0:T(8,128)(2,1)S(1)} %pad_maximum_fusion.refs_4_), channel_id=1, source_target_pairs={{0,2},{1,3},{2,0},{3,1},{4,6},{5,7},{6,4},{7,5},{8,10},{9,11},{10,... | collective-permute-start | bytes 393224 | tf_op jit(solution)/shard_map/ppermute | solution.py:448
  80.2 6.1 %collective-permute-start.19 = (bf16[32,16,128]{2,1,0:T(8,128)(2,1)S(1)}, bf16[32,16,128]{2,1,0:T(8,128)(2,1)S(1)}, u32[]{:S(2)}, u32[]{:S(2)}) collective-permute-start(bf16[32,16,128]{2,1,0:T(8,128)(2,1)S(1)} %pad_maximum_fusion.refs_4_), channel_id=1, source_target_pairs={{0,4},{1,5},{2,6},{3,7},{4,0},{5,1},{6,2},{7,3},{8,12},{9,13},{10,... | collective-permute-start | bytes 393224 | tf_op jit(solution)/shard_map/ppermute | solution.py:448
  80.8 5.6 %collective-permute-start.25 = (bf16[32,16,128]{2,1,0:T(8,128)(2,1)S(1)}, bf16[32,16,128]{2,1,0:T(8,128)(2,1)S(1)}, u32[]{:S(2)}, u32[]{:S(2)}) collective-permute-start(bf16[32,16,128]{2,1,0:T(8,128)(2,1)S(1)} %pad_maximum_fusion.refs_4_), channel_id=1, source_target_pairs={{0,1},{1,0},{2,3},{3,2},{4,5},{5,4},{6,7},{7,6},{8,9},{9,8},{10,11... | collective-permute-start | bytes 393224 | tf_op jit(solution)/shard_map/ppermute | solution.py:452
  80.8 6.0 %collective-permute-start.16 = (bf16[33,16,128]{2,1,0:T(8,128)(2,1)S(1)}, bf16[33,16,128]{2,1,0:T(8,128)(2,1)S(1)}, u32[]{:S(2)}, u32[]{:S(2)}) collective-permute-start(bf16[33,16,128]{2,1,0:T(8,128)(2,1)S(1)} %constant_dynamic-update-slice_fusion.refs_0_), channel_id=1, source_target_pairs={{0,2},{1,3},{2,0},{3,1},{4,6},{5,7},{6,4},{7,5},{8,10},{9,11},{10,... | collective-permute-start | bytes 405512 | tf_op jit(solution)/shard_map/ppermute | solution.py:448
  83.8 3.1 %collective-permute-start.21 = (bf16[33,16,128]{2,1,0:T(8,128)(2,1)S(1)}, bf16[33,16,128]{2,1,0:T(8,128)(2,1)S(1)}, u32[]{:S(2)}, u32[]{:S(2)}) collective-permute-start(bf16[33,16,128]{2,1,0:T(8,128)(2,1)S(1)} %constant_dynamic-update-slice_fusion.refs_0_), channel_id=1, source_target_pairs={{0,1},{1,0},{2,3},{3,2},{4,5},{5,4},{6,7},{7,6},{8,9},{9,8},{10,11... | collective-permute-start | bytes 405512 | tf_op jit(solution)/shard_map/ppermute | solution.py:452
  83.8 6.7 %collective-permute-start.17 = (bf16[33,16,128]{2,1,0:T(8,128)(2,1)S(1)}, bf16[33,16,128]{2,1,0:T(8,128)(2,1)S(1)}, u32[]{:S(2)}, u32[]{:S(2)}) collective-permute-start(bf16[33,16,128]{2,1,0:T(8,128)(2,1)S(1)} %collective-permute-done.15.refs_1_), channel_id=1, source_target_pairs={{0,2},{1,3},{2,0},{3,1},{4,6},{5,7},{6,4},{7,5},{8,10},{9,11},{10,... | collective-permute-start | bytes 405512 | tf_op jit(solution)/shard_map/ppermute | solution.py:448
  86.3 5.6 %collective-permute-start.20 = (bf16[32,16,128]{2,1,0:T(8,128)(2,1)S(1)}, bf16[32,16,128]{2,1,0:T(8,128)(2,1)S(1)}, u32[]{:S(2)}, u32[]{:S(2)}) collective-permute-start(bf16[32,16,128]{2,1,0:T(8,128)(2,1)S(1)} %collective-permute-done.18.refs_5_), channel_id=1, source_target_pairs={{0,4},{1,5},{2,6},{3,7},{4,0},{5,1},{6,2},{7,3},{8,12},{9,13},{10,... | collective-permute-start | bytes 393224 | tf_op jit(solution)/shard_map/ppermute | solution.py:448
  86.4 5.6 %collective-permute-start.26 = (bf16[32,16,128]{2,1,0:T(8,128)(2,1)S(1)}, bf16[32,16,128]{2,1,0:T(8,128)(2,1)S(1)}, u32[]{:S(2)}, u32[]{:S(2)}) collective-permute-start(bf16[32,16,128]{2,1,0:T(8,128)(2,1)S(1)} %collective-permute-done.18.refs_5_), channel_id=1, source_target_pairs={{0,1},{1,0},{2,3},{3,2},{4,5},{5,4},{6,7},{7,6},{8,9},{9,8},{10,11... | collective-permute-start | bytes 393224 | tf_op jit(solution)/shard_map/ppermute | solution.py:452
  86.8 6.6 %collective-permute-start.22 = (bf16[33,16,128]{2,1,0:T(8,128)(2,1)S(1)}, bf16[33,16,128]{2,1,0:T(8,128)(2,1)S(1)}, u32[]{:S(2)}, u32[]{:S(2)}) collective-permute-start(bf16[33,16,128]{2,1,0:T(8,128)(2,1)S(1)} %collective-permute-done.15.refs_1_), channel_id=1, source_target_pairs={{0,1},{1,0},{2,3},{3,2},{4,5},{5,4},{6,7},{7,6},{8,9},{9,8},{10,11... | collective-permute-start | bytes 405512 | tf_op jit(solution)/shard_map/ppermute | solution.py:452
  86.9 6.4 %collective-permute-start.23 = (bf16[33,16,128]{2,1,0:T(8,128)(2,1)S(1)}, bf16[33,16,128]{2,1,0:T(8,128)(2,1)S(1)}, u32[]{:S(2)}, u32[]{:S(2)}) collective-permute-start(bf16[33,16,128]{2,1,0:T(8,128)(2,1)S(1)} %collective-permute-done.16.refs_2_), channel_id=1, source_target_pairs={{0,1},{1,0},{2,3},{3,2},{4,5},{5,4},{6,7},{7,6},{8,9},{9,8},{10,11... | collective-permute-start | bytes 405512 | tf_op jit(solution)/shard_map/ppermute | solution.py:452
  90.6 2.9 %collective-permute-start.24 = (bf16[33,16,128]{2,1,0:T(8,128)(2,1)S(1)}, bf16[33,16,128]{2,1,0:T(8,128)(2,1)S(1)}, u32[]{:S(2)}, u32[]{:S(2)}) collective-permute-start(bf16[33,16,128]{2,1,0:T(8,128)(2,1)S(1)} %collective-permute-done.17.refs_3_), channel_id=1, source_target_pairs={{0,1},{1,0},{2,3},{3,2},{4,5},{5,4},{6,7},{7,6},{8,9},{9,8},{10,11... | collective-permute-start | bytes 405512 | tf_op jit(solution)/shard_map/ppermute | solution.py:452
  92.0 1.3 %collective-permute-start.27 = (bf16[32,16,128]{2,1,0:T(8,128)(2,1)S(1)}, bf16[32,16,128]{2,1,0:T(8,128)(2,1)S(1)}, u32[]{:S(2)}, u32[]{:S(2)}) collective-permute-start(bf16[32,16,128]{2,1,0:T(8,128)(2,1)S(1)} %collective-permute-done.19.refs_6_), channel_id=1, source_target_pairs={{0,1},{1,0},{2,3},{3,2},{4,5},{5,4},{6,7},{7,6},{8,9},{9,8},{10,11... | collective-permute-start | bytes 393224 | tf_op jit(solution)/shard_map/ppermute | solution.py:452
  92.0 1.5 %collective-permute-start.28 = (bf16[32,16,128]{2,1,0:T(8,128)(2,1)S(1)}, bf16[32,16,128]{2,1,0:T(8,128)(2,1)S(1)}, u32[]{:S(2)}, u32[]{:S(2)}) collective-permute-start(bf16[32,16,128]{2,1,0:T(8,128)(2,1)S(1)} %collective-permute-done.20.refs_7_), channel_id=1, source_target_pairs={{0,1},{1,0},{2,3},{3,2},{4,5},{5,4},{6,7},{7,6},{8,9},{9,8},{10,11... | collective-permute-start | bytes 393224 | tf_op jit(solution)/shard_map/ppermute | solution.py:452

commit v5 on v4

--- a/solution.py
+++ b/solution.py
@@ -295,7 +295,7 @@
                 out_ref[top : top + high, pl.ds(lane, 128)] = both[:high]
         return carry
 
-    lax.fori_loop(0, span // 384, pair, 0, unroll=8)
+    lax.fori_loop(0, span // 384, pair, 0, unroll=16)
 
 
 def body(features, mask, owner, weight, bias, cotangent):

time: 98.4 us -> 98.2 us (level)
  no operation moved by 1% of the time
where the time goes in v5:
time: 98.2 us; the launch traced here: 97.4 us
  starting transfers between devices  38.9 us (40%)
  Pallas kernels  20.4 us (21%)
  waiting for transfers between devices  18.7 us (19%)
  local copies, waits for them, and re-layouts  13.5 us (14%)
  other arithmetic  4.99 us (5%)
    pallas_call x1, Pallas kernels, body(): pl.pallas_call(functools.partial(forward_kernel, share, regions, n_leaves...  8.08 us
    ppermute x6, waiting for transfers between devices, body(): lax.ppermute(x, 'batch', pairs(tiles, 1 << o[step]))  7.62 us
    ppermute x2, starting transfers between devices, rims(): inner = lax.ppermute(plane(top * (1 - odd)), 'region', joined[0])  7.43 us
    all_to_all x2, starting transfers between devices, exchanged(): return lax.all_to_all(lines, 'batch', 0, 0, tiled=True)  7.22 us
    ppermute x6, starting transfers between devices, body(): lax.ppermute(x, 'batch', pairs(tiles, 1 << o[step]))  6.68 us
    ppermute x3, starting transfers between devices, body(): gots.append(lax.ppermute(sent, 'region', pairs(regions, flip)))  6.28 us
    ppermute x5, waiting for transfers between devices, halve(): got = lax.ppermute(x[half:].astype(BF), axis, pairs(count, flip))  5.52 us
    ppermute x3, starting transfers between devices, body(): lax.ppermute(total, 'region', pairs(regions, flip))  4.45 us
  transfers between devices with their start and end apart: 31, of which 11 were waited for; matrix products, arithmetic and copies ran while one was open for 12% of the time, Pallas kernels for 7%

profile of v5, /device:TPU:0, one launch (start us, length us, event | category | flops | bytes accessed | tf_op | source)
XLA Modules:
  0.0 97.4 jit_solution(4619887228340027950)
XLA Ops:
  0.6 0.8 constant_dynamic-slice_fusion.3
  1.4 0.1 reshape.137
  1.5 0.8 fusion.14
  2.4 3.0 %collective-permute-start = (bf16[1,64,192]{2,1,0:T(8,128)(2,1)S(1)}, bf16[1,64,192]{2,1,0:T(8,128)(2,1)S(1)}, u32[]{:S(2)}, u32[]{:S(2)}) collective-permute-start(bf16[1,64,192]{2,1,0:T(8,128)(2,1)S(1)} %broadcast_multiply_fusion.1), channel_id=1, source_target_pairs={{0,8},{8,0},{16,24},{24,16},{1,9},{9,1},{17,25},{25,17},{2,10},{10... | collective-permute-start | bytes 73736 | tf_op jit(solution)/shard_map/ppermute | solution.py:322
  5.4 0.1 reshape.140
  5.6 0.7 collective-permute-start.1
  6.2 0.8 reshape.139.mask_ref
  7.0 0.9 copy-done
  7.9 0.7 copy-done.1
  8.6 1.3 %shard_map.93.x_ref = bf16[8,64,192]{2,1,0:T(8,128)(2,1)S(1)} custom-call(s32[8]{0:T(128)S(1)} %copy-done.1, bf16[64,1536]{1,0:T(8,128)(2,1)S(1)} %bitcast.17, s32[64,8]{1,0:T(8,128)S(1)} %reshape.139.mask_ref), custom_call_target="tpu_custom_call" | custom-call | tf_op jit(solution)/shard_map/pallas_call | solution.py:356
  9.9 1.7 %shard_map.94 = (bf16[8,10,8,192]{3,2,1,0:T(8,128)(2,1)}, bf16[10,64,192]{2,1,0:T(8,128)(2,1)S(1)}) custom-call(s32[8]{0:T(128)S(1)} %copy-done.1, bf16[1,64,192]{2,1,0:T(8,128)(2,1)S(1)} %collective-permute-done.inner_ref, bf16[8,64,192]{2,1,0:T(8,128)(2,1)S(1)} %shard_map.93.x_ref, bf16[1,64,192]{2,1,0:T(8,128)(2,1)S(1)} %collective-permute-done.1.outer_ref), custom_call_target="tpu_custom_call" | custom-call | tf_op jit(solution)/shard_map/pallas_call | solution.py:327
  11.6 3.6 %all-to-all-start = ((bf16[8,10,8,192]{3,2,1,0:T(8,128)(2,1)}), bf16[8,10,8,192]{3,2,1,0:T(8,128)(2,1)S(1)}, u32[]{:S(2)}, u32[]{:S(2)}) async-start(bf16[8,10,8,192]{3,2,1,0:T(8,128)(2,1)} %get-tuple-element.29), calls=%async_computation | async-start | bytes 655360 | tf_op jit(solution)/shard_map/all_to_all | solution.py:340
  15.2 4.4 %reshape.141.w_ref = bf16[27,192,192]{2,1,0:T(8,128)(2,1)S(1)} reshape(bf16[27,36864]{1,0:T(8,128)(2,1)} %param.9) | data formatting | bytes 3981312 | tf_op jit(solution)/shard_map/reshape | solution.py:367
  19.6 3.2 %all-to-all-done.recv_ref = bf16[8,10,8,192]{3,2,1,0:T(8,128)(2,1)S(1)} async-done(((bf16[8,10,8,192]{3,2,1,0:T(8,128)(2,1)}), bf16[8,10,8,192]{3,2,1,0:T(8,128)(2,1)S(1)}, u32[]{:S(2)}, u32[]{:S(2)}) %all-to-all-start) | async-done | bytes 245792 | tf_op jit(solution)/shard_map/all_to_all | solution.py:340
  22.9 8.1 %shard_map.95 = (bf16[512,192]{1,0:T(8,128)(2,1)S(1)}, bf16[512,192]{1,0:T(8,128)(2,1)S(1)}, bf16[1,16,128]{2,1,0:T(8,128)(2,1)S(1)}, bf16[512,16,128]{2,1,0:T(8,128)(2,1)S(1)}) custom-call(s32[8]{0:T(128)S(1)} %copy-done.2, bf16[10,64,192]{2,1,0:T(8,128)(2,1)S(1)} %get-tuple-element.27.x_ref, bf16[8,10,8,192]{3,2,1,0:T(8,128)(2,1)S(1)} %all-to-all-done.recv_ref, ...), custom_call_target="tpu_custom_call" | custom-call | flops 2038431744 | bytes 6291456 | tf_op jit(solution)/shard_map/pallas_call | solution.py:369
  31.0 0.2 slice.117
  31.2 2.6 %collective-permute-done.2 = bf16[256,16,128]{2,1,0:T(8,128)(2,1)S(1)} collective-permute-done((bf16[256,16,128]{2,1,0:T(8,128)(2,1)S(1)}, bf16[256,16,128]{2,1,0:T(8,128)(2,1)S(1)}, u32[]{:S(2)}, u32[]{:S(2)}) %collective-permute-start.2) | collective-permute-done | bytes 1048608 | tf_op jit(solution)/shard_map/ppermute | solution.py:391
  33.9 0.3 fusion.15
  34.2 0.6 collective-permute-start.4
  34.8 0.6 collective-permute-start.3
  35.4 4.4 %collective-permute-start.5 = (bf16[1,64,192]{2,1,0:T(8,128)(2,1)S(1)}, bf16[1,64,192]{2,1,0:T(8,128)(2,1)S(1)}, u32[]{:S(2)}, u32[]{:S(2)}) collective-permute-start(bf16[1,64,192]{2,1,0:T(8,128)(2,1)S(1)} %get-tuple-element.61), channel_id=1, source_target_pairs={{0,8},{8,0},{16,24},{24,16},{1,9},{9,1},{17,25},{25,17},{2,10},{10... | collective-permute-start | bytes 73736 | tf_op jit(solution)/shard_map/ppermute | solution.py:322
  39.8 0.7 collective-permute-start.6
  40.5 1.2 %collective-permute-done.5.inner_ref = bf16[1,64,192]{2,1,0:T(8,128)(2,1)S(1)} collective-permute-done((bf16[1,64,192]{2,1,0:T(8,128)(2,1)S(1)}, bf16[1,64,192]{2,1,0:T(8,128)(2,1)S(1)}, u32[]{:S(2)}, u32[]{:S(2)}) %collective-permute-start.5) | collective-permute-done | bytes 24608 | tf_op jit(solution)/shard_map/ppermute | solution.py:322
  41.7 1.7 %shard_map.96 = (bf16[8,10,8,192]{3,2,1,0:T(8,128)(2,1)}, bf16[10,64,192]{2,1,0:T(8,128)(2,1)S(1)}) custom-call(s32[8]{0:T(128)S(1)} %copy-done.2, bf16[1,64,192]{2,1,0:T(8,128)(2,1)S(1)} %collective-permute-done.5.inner_ref, bf16[8,64,192]{2,1,0:T(8,128)(2,1)S(1)} %bitcast.16, bf16[1,64,192]{2,1,0:T(8,128)(2,1)S(1)} %collective-permute-done.6.outer_ref), custom_call_target="tpu_custom_call" | custom-call | tf_op jit(solution)/shard_map/pallas_call | solution.py:327
  43.4 0.1 slice_add_fusion
  43.6 1.5 %collective-permute-start.8 = (bf16[32,16,128]{2,1,0:T(8,128)(2,1)S(1)}, bf16[32,16,128]{2,1,0:T(8,128)(2,1)S(1)}, u32[]{:S(2)}, u32[]{:S(2)}) collective-permute-start(bf16[32,16,128]{2,1,0:T(8,128)(2,1)S(1)} %slice.193), channel_id=1, source_target_pairs={{0,2},{1,3},{2,0},{3,1},{4,6},{5,7},{6,4},{7,5},{8,10},{9,11},{10,... | collective-permute-start | bytes 393224 | tf_op jit(solution)/shard_map/ppermute | solution.py:391
  45.1 1.4 %collective-permute-start.7 = (bf16[32,16,128]{2,1,0:T(8,128)(2,1)S(1)}, bf16[32,16,128]{2,1,0:T(8,128)(2,1)S(1)}, u32[]{:S(2)}, u32[]{:S(2)}) collective-permute-start(bf16[32,16,128]{2,1,0:T(8,128)(2,1)S(1)} %slice.194), channel_id=1, source_target_pairs={{0,4},{1,5},{2,6},{3,7},{4,0},{5,1},{6,2},{7,3},{8,12},{9,13},{10,... | collective-permute-start | bytes 393224 | tf_op jit(solution)/shard_map/ppermute | solution.py:391
  46.5 2.1 %collective-permute-done.8 = bf16[32,16,128]{2,1,0:T(8,128)(2,1)S(1)} collective-permute-done((bf16[32,16,128]{2,1,0:T(8,128)(2,1)S(1)}, bf16[32,16,128]{2,1,0:T(8,128)(2,1)S(1)}, u32[]{:S(2)}, u32[]{:S(2)}) %collective-permute-start.8) | collective-permute-done | bytes 131104 | tf_op jit(solution)/shard_map/ppermute | solution.py:391
  48.6 0.7 fusion.17
  49.4 0.8 collective-permute-done.7
  50.2 0.8 fusion.16
  50.9 0.7 pad_maximum_fusion.3
  51.6 3.9 %collective-permute-start.11 = (bf16[17,16,128]{2,1,0:T(8,128)(2,1)}, bf16[17,16,128]{2,1,0:T(8,128)(2,1)}, u32[]{:S(2)}, u32[]{:S(2)}) collective-permute-start(bf16[17,16,128]{2,1,0:T(8,128)(2,1)} %get-tuple-element.80), channel_id=1, source_target_pairs={{0,8},{8,0},{16,24},{24,16},{1,9},{9,1},{17,25},{25,17},{2,10},{10... | collective-permute-start | bytes 208904 | tf_op jit(solution)/shard_map/ppermute | solution.py:412
  55.5 2.4 %collective-permute-start.9 = (bf16[17,16,128]{2,1,0:T(8,128)(2,1)S(1)}, bf16[17,16,128]{2,1,0:T(8,128)(2,1)}, u32[]{:S(2)}, u32[]{:S(2)}) collective-permute-start(bf16[17,16,128]{2,1,0:T(8,128)(2,1)S(1)} %get-tuple-element.78), channel_id=1, source_target_pairs={{0,24},{8,16},{16,8},{24,0},{1,25},{9,17},{17,9},{25,1},{2,26},{10... | collective-permute-start | bytes 208904 | tf_op jit(solution)/shard_map/ppermute | solution.py:412
  57.9 3.6 %all-to-all-start.1 = ((bf16[8,10,8,192]{3,2,1,0:T(8,128)(2,1)}), bf16[8,10,8,192]{3,2,1,0:T(8,128)(2,1)S(1)}, u32[]{:S(2)}, u32[]{:S(2)}) async-start(bf16[8,10,8,192]{3,2,1,0:T(8,128)(2,1)} %get-tuple-element.38), calls=%async_computation.1 | async-start | bytes 655360 | tf_op jit(solution)/shard_map/all_to_all | solution.py:340
  61.5 0.8 slice.156
  62.3 0.8 slice.154
  63.2 0.9 fusion.2
  64.2 1.2 %collective-permute-start.12 = (bf16[16,16,128]{2,1,0:T(8,128)(2,1)S(1)}, bf16[16,16,128]{2,1,0:T(8,128)(2,1)}, u32[]{:S(2)}, u32[]{:S(2)}) collective-permute-start(bf16[16,16,128]{2,1,0:T(8,128)(2,1)S(1)} %fusion.2), channel_id=1, source_target_pairs={{0,8},{8,0},{16,24},{24,16},{1,9},{9,1},{17,25},{25,17},{2,10},{10... | collective-permute-start | bytes 196616 | tf_op jit(solution)/shard_map/ppermute | solution.py:424
  65.3 0.9 collective-permute-start.13
  66.2 2.4 %collective-permute-start.14 = (bf16[16,16,128]{2,1,0:T(8,128)(2,1)S(1)}, bf16[16,16,128]{2,1,0:T(8,128)(2,1)S(1)}, u32[]{:S(2)}, u32[]{:S(2)}) collective-permute-start(bf16[16,16,128]{2,1,0:T(8,128)(2,1)S(1)} %fusion.2), channel_id=1, source_target_pairs={{0,24},{8,16},{16,8},{24,0},{1,25},{9,17},{17,9},{25,1},{2,26},{10... | collective-permute-start | bytes 196616 | tf_op jit(solution)/shard_map/ppermute | solution.py:424
  68.6 0.7 slice.168
  69.3 0.7 slice.167
  70.0 0.7 slice.166
  70.7 0.5 reduce-precision_convert_fusion.1
  71.2 0.9 copy-done.6
  72.2 3.9 %shard_map.97 = (bf16[64,1536]{1,0:T(8,128)(2,1)}, bf16[64,1536]{1,0:T(8,128)(2,1)}) custom-call(s32[8]{0:T(128)S(1)} %copy-done.2, bf16[10,64,192]{2,1,0:T(8,128)(2,1)S(1)} %get-tuple-element.37.x_ref, bf16[8,10,8,192]{3,2,1,0:T(8,128)(2,1)S(1)} %all-to-all-done.1.recv_ref, bf16[27,192,192]{2,1,0:T(8,128)(2,1)S(1)} %reshape.141.w_ref, ...), custom_call_target="tpu_custom_call" | custom-call | flops 1019215872 | bytes 3145728 | tf_op jit(solution)/shard_map/pallas_call | solution.py:426
  76.1 0.8 fusion.22
  76.9 1.8 %collective-permute-start.15 = (bf16[33,16,128]{2,1,0:T(8,128)(2,1)S(1)}, bf16[33,16,128]{2,1,0:T(8,128)(2,1)S(1)}, u32[]{:S(2)}, u32[]{:S(2)}) collective-permute-start(bf16[33,16,128]{2,1,0:T(8,128)(2,1)S(1)} %constant_dynamic-update-slice_fusion.refs_0_), channel_id=1, source_target_pairs={{0,4},{1,5},{2,6},{3,7},{4,0},{5,1},{6,2},{7,3},{8,12},{9,13},{10,... | collective-permute-start | bytes 405512 | tf_op jit(solution)/shard_map/ppermute | solution.py:448
  78.8 1.5 %collective-permute-start.18 = (bf16[32,16,128]{2,1,0:T(8,128)(2,1)S(1)}, bf16[32,16,128]{2,1,0:T(8,128)(2,1)S(1)}, u32[]{:S(2)}, u32[]{:S(2)}) collective-permute-start(bf16[32,16,128]{2,1,0:T(8,128)(2,1)S(1)} %pad_maximum_fusion.refs_4_), channel_id=1, source_target_pairs={{0,2},{1,3},{2,0},{3,1},{4,6},{5,7},{6,4},{7,5},{8,10},{9,11},{10,... | collective-permute-start | bytes 393224 | tf_op jit(solution)/shard_map/ppermute | solution.py:448
  80.3 0.5 collective-permute-start.19
  80.9 0.3 collective-permute-start.16
  81.2 2.8 %collective-permute-done.18.refs_5_ = bf16[32,16,128]{2,1,0:T(8,128)(2,1)S(1)} collective-permute-done((bf16[32,16,128]{2,1,0:T(8,128)(2,1)S(1)}, bf16[32,16,128]{2,1,0:T(8,128)(2,1)S(1)}, u32[]{:S(2)}, u32[]{:S(2)}) %collective-permute-start.18) | collective-permute-done | bytes 131104 | tf_op jit(solution)/shard_map/ppermute | solution.py:448
  84.0 2.5 %collective-permute-start.17 = (bf16[33,16,128]{2,1,0:T(8,128)(2,1)S(1)}, bf16[33,16,128]{2,1,0:T(8,128)(2,1)S(1)}, u32[]{:S(2)}, u32[]{:S(2)}) collective-permute-start(bf16[33,16,128]{2,1,0:T(8,128)(2,1)S(1)} %collective-permute-done.15.refs_1_), channel_id=1, source_target_pairs={{0,2},{1,3},{2,0},{3,1},{4,6},{5,7},{6,4},{7,5},{8,10},{9,11},{10,... | collective-permute-start | bytes 405512 | tf_op jit(solution)/shard_map/ppermute | solution.py:448
  86.5 0.3 collective-permute-start.26
  86.8 0.1 collective-permute-done.16.refs_2_
  86.9 0.2 collective-permute-start.22
  87.0 0.3 collective-permute-start.23
  87.4 3.3 %collective-permute-done.17.refs_3_ = bf16[33,16,128]{2,1,0:T(8,128)(2,1)S(1)} collective-permute-done((bf16[33,16,128]{2,1,0:T(8,128)(2,1)S(1)}, bf16[33,16,128]{2,1,0:T(8,128)(2,1)S(1)}, u32[]{:S(2)}, u32[]{:S(2)}) %collective-permute-start.17) | collective-permute-done | bytes 135200 | tf_op jit(solution)/shard_map/ppermute | solution.py:448
  90.7 1.4 %collective-permute-done.20.refs_7_ = bf16[32,16,128]{2,1,0:T(8,128)(2,1)S(1)} collective-permute-done((bf16[32,16,128]{2,1,0:T(8,128)(2,1)S(1)}, bf16[32,16,128]{2,1,0:T(8,128)(2,1)S(1)}, u32[]{:S(2)}, u32[]{:S(2)}) %collective-permute-start.20) | collective-permute-done | bytes 131104 | tf_op jit(solution)/shard_map/ppermute | solution.py:448
  92.1 0.5 collective-permute-start.28
  92.6 0.8 collective-permute-done.27.refs_14_
  93.4 0.2 collective-permute-done.28.refs_15_
  93.6 3.7 %shard_map.98 = (bf16[27,36864]{1,0:T(8,128)(2,1)}, f32[1,192]{1,0:T(1,128)}) custom-call(s32[8]{0:T(128)S(1)} %copy-done.2, bf16[33,16,128]{2,1,0:T(8,128)(2,1)S(1)} %constant_dynamic-update-slice_fusion.refs_0_, bf16[33,16,128]{2,1,0:T(8,128)(2,1)S(1)} %collective-permute-done.15.refs_1_, bf16[33,16,128]{2,1,0:T(8,128)(2,1)S(1)} %collective-permute-done.16.refs_2_, ...), custom_call_target="tpu_custom_call" | custom-call | tf_op jit(solution)/shard_map/pallas_call | solution.py:453
  (55 shorter events, 0.5 us)
Async XLA Ops:
  2.4 7.5 %collective-permute-start = (bf16[1,64,192]{2,1,0:T(8,128)(2,1)S(1)}, bf16[1,64,192]{2,1,0:T(8,128)(2,1)S(1)}, u32[]{:S(2)}, u32[]{:S(2)}) collective-permute-start(bf16[1,64,192]{2,1,0:T(8,128)(2,1)S(1)} %broadcast_multiply_fusion.1), channel_id=1, source_target_pairs={{0,8},{8,0},{16,24},{24,16},{1,9},{9,1},{17,25},{25,17},{2,10},{10... | collective-permute-start | bytes 73736 | tf_op jit(solution)/shard_map/ppermute | solution.py:322
  5.6 4.3 %collective-permute-start.1 = (bf16[1,64,192]{2,1,0:T(8,128)(2,1)S(1)}, bf16[1,64,192]{2,1,0:T(8,128)(2,1)S(1)}, u32[]{:S(2)}, u32[]{:S(2)}) collective-permute-start(bf16[1,64,192]{2,1,0:T(8,128)(2,1)S(1)} %broadcast_multiply_fusion), channel_id=1, source_target_pairs={{8,16},{16,8},{9,17},{17,9},{10,18},{18,10},{11,19},{19,11},{12,20... | collective-permute-start | bytes 73736 | tf_op jit(solution)/shard_map/ppermute | solution.py:323
  7.0 0.9 copy-start
  7.9 0.7 copy-start.1
  11.6 11.2 %all-to-all-start = ((bf16[8,10,8,192]{3,2,1,0:T(8,128)(2,1)}), bf16[8,10,8,192]{3,2,1,0:T(8,128)(2,1)S(1)}, u32[]{:S(2)}, u32[]{:S(2)}) async-start(bf16[8,10,8,192]{3,2,1,0:T(8,128)(2,1)} %get-tuple-element.29), calls=%async_computation | async-start | bytes 655360 | tf_op jit(solution)/shard_map/all_to_all | solution.py:340
  15.2 7.6 %copy-start.2 = (s32[8]{0:T(128)S(1)}, s32[8]{0:T(128)}, u32[]{:S(2)}) copy-start(s32[8]{0:T(128)} %owner.11) | copy-start | bytes 100
  15.2 7.6 %copy-start.3 = (bf16[8,8,1536]{2,1,0:T(8,128)(2,1)S(1)}, bf16[8,8,1536]{2,1,0:T(8,128)(2,1)}, u32[]{:S(2)}) copy-start(bf16[8,8,1536]{2,1,0:T(8,128)(2,1)} %param.11) | copy-start | bytes 589828
  15.2 7.6 %copy-start.4 = (f32[192]{0:T(256)S(1)}, f32[192]{0:T(256)}, u32[]{:S(2)}) copy-start(f32[192]{0:T(256)} %param.10) | copy-start | bytes 2308
  31.0 3.2 %copy-start.5 = (bf16[512,192]{1,0:T(8,128)(2,1)}, bf16[512,192]{1,0:T(8,128)(2,1)S(1)}, u32[]{:S(2)}) copy-start(bf16[512,192]{1,0:T(8,128)(2,1)S(1)} %get-tuple-element.39.pre_ref) | copy-start | bytes 589828
  31.2 2.7 %collective-permute-start.2 = (bf16[256,16,128]{2,1,0:T(8,128)(2,1)S(1)}, bf16[256,16,128]{2,1,0:T(8,128)(2,1)S(1)}, u32[]{:S(2)}, u32[]{:S(2)}) collective-permute-start(bf16[256,16,128]{2,1,0:T(8,128)(2,1)S(1)} %slice.117), channel_id=1, source_target_pairs={{0,1},{1,0},{2,3},{3,2},{4,5},{5,4},{6,7},{7,6},{8,9},{9,8},{10,11... | collective-permute-start | bytes 3145736 | tf_op jit(solution)/shard_map/ppermute | solution.py:391
  34.2 9.2 %collective-permute-start.4 = (bf16[64,16,128]{2,1,0:T(8,128)(2,1)S(1)}, bf16[64,16,128]{2,1,0:T(8,128)(2,1)S(1)}, u32[]{:S(2)}, u32[]{:S(2)}) collective-permute-start(bf16[64,16,128]{2,1,0:T(8,128)(2,1)S(1)} %get-tuple-element.58), channel_id=1, source_target_pairs={{0,4},{1,5},{2,6},{3,7},{4,0},{5,1},{6,2},{7,3},{8,12},{9,13},{10,... | collective-permute-start | bytes 786440 | tf_op jit(solution)/shard_map/ppermute | solution.py:391
  34.8 8.6 %collective-permute-start.3 = (bf16[64,16,128]{2,1,0:T(8,128)(2,1)S(1)}, bf16[64,16,128]{2,1,0:T(8,128)(2,1)S(1)}, u32[]{:S(2)}, u32[]{:S(2)}) collective-permute-start(bf16[64,16,128]{2,1,0:T(8,128)(2,1)S(1)} %get-tuple-element.59), channel_id=1, source_target_pairs={{0,2},{1,3},{2,0},{3,1},{4,6},{5,7},{6,4},{7,5},{8,10},{9,11},{10,... | collective-permute-start | bytes 786440 | tf_op jit(solution)/shard_map/ppermute | solution.py:391
  35.4 6.3 %collective-permute-start.5 = (bf16[1,64,192]{2,1,0:T(8,128)(2,1)S(1)}, bf16[1,64,192]{2,1,0:T(8,128)(2,1)S(1)}, u32[]{:S(2)}, u32[]{:S(2)}) collective-permute-start(bf16[1,64,192]{2,1,0:T(8,128)(2,1)S(1)} %get-tuple-element.61), channel_id=1, source_target_pairs={{0,8},{8,0},{16,24},{24,16},{1,9},{9,1},{17,25},{25,17},{2,10},{10... | collective-permute-start | bytes 73736 | tf_op jit(solution)/shard_map/ppermute | solution.py:322
  39.8 1.9 %collective-permute-start.6 = (bf16[1,64,192]{2,1,0:T(8,128)(2,1)S(1)}, bf16[1,64,192]{2,1,0:T(8,128)(2,1)S(1)}, u32[]{:S(2)}, u32[]{:S(2)}) collective-permute-start(bf16[1,64,192]{2,1,0:T(8,128)(2,1)S(1)} %get-tuple-element.60), channel_id=1, source_target_pairs={{8,16},{16,8},{9,17},{17,9},{10,18},{18,10},{11,19},{19,11},{12,20... | collective-permute-start | bytes 73736 | tf_op jit(solution)/shard_map/ppermute | solution.py:323
  43.6 5.0 %collective-permute-start.8 = (bf16[32,16,128]{2,1,0:T(8,128)(2,1)S(1)}, bf16[32,16,128]{2,1,0:T(8,128)(2,1)S(1)}, u32[]{:S(2)}, u32[]{:S(2)}) collective-permute-start(bf16[32,16,128]{2,1,0:T(8,128)(2,1)S(1)} %slice.193), channel_id=1, source_target_pairs={{0,2},{1,3},{2,0},{3,1},{4,6},{5,7},{6,4},{7,5},{8,10},{9,11},{10,... | collective-permute-start | bytes 393224 | tf_op jit(solution)/shard_map/ppermute | solution.py:391
  45.1 5.0 %collective-permute-start.7 = (bf16[32,16,128]{2,1,0:T(8,128)(2,1)S(1)}, bf16[32,16,128]{2,1,0:T(8,128)(2,1)S(1)}, u32[]{:S(2)}, u32[]{:S(2)}) collective-permute-start(bf16[32,16,128]{2,1,0:T(8,128)(2,1)S(1)} %slice.194), channel_id=1, source_target_pairs={{0,4},{1,5},{2,6},{3,7},{4,0},{5,1},{6,2},{7,3},{8,12},{9,13},{10,... | collective-permute-start | bytes 393224 | tf_op jit(solution)/shard_map/ppermute | solution.py:391
  51.6 11.6 %collective-permute-start.11 = (bf16[17,16,128]{2,1,0:T(8,128)(2,1)}, bf16[17,16,128]{2,1,0:T(8,128)(2,1)}, u32[]{:S(2)}, u32[]{:S(2)}) collective-permute-start(bf16[17,16,128]{2,1,0:T(8,128)(2,1)} %get-tuple-element.80), channel_id=1, source_target_pairs={{0,8},{8,0},{16,24},{24,16},{1,9},{9,1},{17,25},{25,17},{2,10},{10... | collective-permute-start | bytes 208904 | tf_op jit(solution)/shard_map/ppermute | solution.py:412
  55.5 7.7 %collective-permute-start.10 = (bf16[17,16,128]{2,1,0:T(8,128)(2,1)S(1)}, bf16[17,16,128]{2,1,0:T(8,128)(2,1)}, u32[]{:S(2)}, u32[]{:S(2)}) collective-permute-start(bf16[17,16,128]{2,1,0:T(8,128)(2,1)S(1)} %get-tuple-element.79), channel_id=1, source_target_pairs={{0,16},{8,24},{16,0},{24,8},{1,17},{9,25},{17,1},{25,9},{2,18},{10... | collective-permute-start | bytes 208904 | tf_op jit(solution)/shard_map/ppermute | solution.py:412
  55.5 7.7 %collective-permute-start.9 = (bf16[17,16,128]{2,1,0:T(8,128)(2,1)S(1)}, bf16[17,16,128]{2,1,0:T(8,128)(2,1)}, u32[]{:S(2)}, u32[]{:S(2)}) collective-permute-start(bf16[17,16,128]{2,1,0:T(8,128)(2,1)S(1)} %get-tuple-element.78), channel_id=1, source_target_pairs={{0,24},{8,16},{16,8},{24,0},{1,25},{9,17},{17,9},{25,1},{2,26},{10... | collective-permute-start | bytes 208904 | tf_op jit(solution)/shard_map/ppermute | solution.py:412
  57.9 13.3 %all-to-all-start.1 = ((bf16[8,10,8,192]{3,2,1,0:T(8,128)(2,1)}), bf16[8,10,8,192]{3,2,1,0:T(8,128)(2,1)S(1)}, u32[]{:S(2)}, u32[]{:S(2)}) async-start(bf16[8,10,8,192]{3,2,1,0:T(8,128)(2,1)} %get-tuple-element.38), calls=%async_computation.1 | async-start | bytes 655360 | tf_op jit(solution)/shard_map/all_to_all | solution.py:340
  64.2 11.9 %collective-permute-start.12 = (bf16[16,16,128]{2,1,0:T(8,128)(2,1)S(1)}, bf16[16,16,128]{2,1,0:T(8,128)(2,1)}, u32[]{:S(2)}, u32[]{:S(2)}) collective-permute-start(bf16[16,16,128]{2,1,0:T(8,128)(2,1)S(1)} %fusion.2), channel_id=1, source_target_pairs={{0,8},{8,0},{16,24},{24,16},{1,9},{9,1},{17,25},{25,17},{2,10},{10... | collective-permute-start | bytes 196616 | tf_op jit(solution)/shard_map/ppermute | solution.py:424
  65.3 10.7 %collective-permute-start.13 = (bf16[16,16,128]{2,1,0:T(8,128)(2,1)S(1)}, bf16[16,16,128]{2,1,0:T(8,128)(2,1)S(1)}, u32[]{:S(2)}, u32[]{:S(2)}) collective-permute-start(bf16[16,16,128]{2,1,0:T(8,128)(2,1)S(1)} %fusion.2), channel_id=1, source_target_pairs={{0,16},{8,24},{16,0},{24,8},{1,17},{9,25},{17,1},{25,9},{2,18},{10... | collective-permute-start | bytes 196616 | tf_op jit(solution)/shard_map/ppermute | solution.py:424
  66.2 9.8 %collective-permute-start.14 = (bf16[16,16,128]{2,1,0:T(8,128)(2,1)S(1)}, bf16[16,16,128]{2,1,0:T(8,128)(2,1)S(1)}, u32[]{:S(2)}, u32[]{:S(2)}) collective-permute-start(bf16[16,16,128]{2,1,0:T(8,128)(2,1)S(1)} %fusion.2), channel_id=1, source_target_pairs={{0,24},{8,16},{16,8},{24,0},{1,25},{9,17},{17,9},{25,1},{2,26},{10... | collective-permute-start | bytes 196616 | tf_op jit(solution)/shard_map/ppermute | solution.py:424
  71.2 1.0 copy-start.6
  72.2 4.8 %copy-start.7 = (bf16[2,128]{1,0:T(2,128)(2,1)S(1)}, bf16[2,128]{1,0:T(2,128)(2,1)}, u32[]{:S(2)}) copy-start(bf16[2,128]{1,0:T(2,128)(2,1)} %get-tuple-element.85) | copy-start | bytes 1540
  76.9 7.0 %collective-permute-start.15 = (bf16[33,16,128]{2,1,0:T(8,128)(2,1)S(1)}, bf16[33,16,128]{2,1,0:T(8,128)(2,1)S(1)}, u32[]{:S(2)}, u32[]{:S(2)}) collective-permute-start(bf16[33,16,128]{2,1,0:T(8,128)(2,1)S(1)} %constant_dynamic-update-slice_fusion.refs_0_), channel_id=1, source_target_pairs={{0,4},{1,5},{2,6},{3,7},{4,0},{5,1},{6,2},{7,3},{8,12},{9,13},{10,... | collective-permute-start | bytes 405512 | tf_op jit(solution)/shard_map/ppermute | solution.py:448
  78.8 5.2 %collective-permute-start.18 = (bf16[32,16,128]{2,1,0:T(8,128)(2,1)S(1)}, bf16[32,16,128]{2,1,0:T(8,128)(2,1)S(1)}, u32[]{:S(2)}, u32[]{:S(2)}) collective-permute-start(bf16[32,16,128]{2,1,0:T(8,128)(2,1)S(1)} %pad_maximum_fusion.refs_4_), channel_id=1, source_target_pairs={{0,2},{1,3},{2,0},{3,1},{4,6},{5,7},{6,4},{7,5},{8,10},{9,11},{10,... | collective-permute-start | bytes 393224 | tf_op jit(solution)/shard_map/ppermute | solution.py:448
  80.3 6.1 %collective-permute-start.19 = (bf16[32,16,128]{2,1,0:T(8,128)(2,1)S(1)}, bf16[32,16,128]{2,1,0:T(8,128)(2,1)S(1)}, u32[]{:S(2)}, u32[]{:S(2)}) collective-permute-start(bf16[32,16,128]{2,1,0:T(8,128)(2,1)S(1)} %pad_maximum_fusion.refs_4_), channel_id=1, source_target_pairs={{0,4},{1,5},{2,6},{3,7},{4,0},{5,1},{6,2},{7,3},{8,12},{9,13},{10,... | collective-permute-start | bytes 393224 | tf_op jit(solution)/shard_map/ppermute | solution.py:448
  80.9 5.6 %collective-permute-start.25 = (bf16[32,16,128]{2,1,0:T(8,128)(2,1)S(1)}, bf16[32,16,128]{2,1,0:T(8,128)(2,1)S(1)}, u32[]{:S(2)}, u32[]{:S(2)}) collective-permute-start(bf16[32,16,128]{2,1,0:T(8,128)(2,1)S(1)} %pad_maximum_fusion.refs_4_), channel_id=1, source_target_pairs={{0,1},{1,0},{2,3},{3,2},{4,5},{5,4},{6,7},{7,6},{8,9},{9,8},{10,11... | collective-permute-start | bytes 393224 | tf_op jit(solution)/shard_map/ppermute | solution.py:452
  80.9 6.0 %collective-permute-start.16 = (bf16[33,16,128]{2,1,0:T(8,128)(2,1)S(1)}, bf16[33,16,128]{2,1,0:T(8,128)(2,1)S(1)}, u32[]{:S(2)}, u32[]{:S(2)}) collective-permute-start(bf16[33,16,128]{2,1,0:T(8,128)(2,1)S(1)} %constant_dynamic-update-slice_fusion.refs_0_), channel_id=1, source_target_pairs={{0,2},{1,3},{2,0},{3,1},{4,6},{5,7},{6,4},{7,5},{8,10},{9,11},{10,... | collective-permute-start | bytes 405512 | tf_op jit(solution)/shard_map/ppermute | solution.py:448
  84.0 3.1 %collective-permute-start.21 = (bf16[33,16,128]{2,1,0:T(8,128)(2,1)S(1)}, bf16[33,16,128]{2,1,0:T(8,128)(2,1)S(1)}, u32[]{:S(2)}, u32[]{:S(2)}) collective-permute-start(bf16[33,16,128]{2,1,0:T(8,128)(2,1)S(1)} %constant_dynamic-update-slice_fusion.refs_0_), channel_id=1, source_target_pairs={{0,1},{1,0},{2,3},{3,2},{4,5},{5,4},{6,7},{7,6},{8,9},{9,8},{10,11... | collective-permute-start | bytes 405512 | tf_op jit(solution)/shard_map/ppermute | solution.py:452
  84.0 6.7 %collective-permute-start.17 = (bf16[33,16,128]{2,1,0:T(8,128)(2,1)S(1)}, bf16[33,16,128]{2,1,0:T(8,128)(2,1)S(1)}, u32[]{:S(2)}, u32[]{:S(2)}) collective-permute-start(bf16[33,16,128]{2,1,0:T(8,128)(2,1)S(1)} %collective-permute-done.15.refs_1_), channel_id=1, source_target_pairs={{0,2},{1,3},{2,0},{3,1},{4,6},{5,7},{6,4},{7,5},{8,10},{9,11},{10,... | collective-permute-start | bytes 405512 | tf_op jit(solution)/shard_map/ppermute | solution.py:448
  86.5 5.6 %collective-permute-start.20 = (bf16[32,16,128]{2,1,0:T(8,128)(2,1)S(1)}, bf16[32,16,128]{2,1,0:T(8,128)(2,1)S(1)}, u32[]{:S(2)}, u32[]{:S(2)}) collective-permute-start(bf16[32,16,128]{2,1,0:T(8,128)(2,1)S(1)} %collective-permute-done.18.refs_5_), channel_id=1, source_target_pairs={{0,4},{1,5},{2,6},{3,7},{4,0},{5,1},{6,2},{7,3},{8,12},{9,13},{10,... | collective-permute-start | bytes 393224 | tf_op jit(solution)/shard_map/ppermute | solution.py:448
  86.5 5.6 %collective-permute-start.26 = (bf16[32,16,128]{2,1,0:T(8,128)(2,1)S(1)}, bf16[32,16,128]{2,1,0:T(8,128)(2,1)S(1)}, u32[]{:S(2)}, u32[]{:S(2)}) collective-permute-start(bf16[32,16,128]{2,1,0:T(8,128)(2,1)S(1)} %collective-permute-done.18.refs_5_), channel_id=1, source_target_pairs={{0,1},{1,0},{2,3},{3,2},{4,5},{5,4},{6,7},{7,6},{8,9},{9,8},{10,11... | collective-permute-start | bytes 393224 | tf_op jit(solution)/shard_map/ppermute | solution.py:452
  86.9 6.6 %collective-permute-start.22 = (bf16[33,16,128]{2,1,0:T(8,128)(2,1)S(1)}, bf16[33,16,128]{2,1,0:T(8,128)(2,1)S(1)}, u32[]{:S(2)}, u32[]{:S(2)}) collective-permute-start(bf16[33,16,128]{2,1,0:T(8,128)(2,1)S(1)} %collective-permute-done.15.refs_1_), channel_id=1, source_target_pairs={{0,1},{1,0},{2,3},{3,2},{4,5},{5,4},{6,7},{7,6},{8,9},{9,8},{10,11... | collective-permute-start | bytes 405512 | tf_op jit(solution)/shard_map/ppermute | solution.py:452
  87.0 6.4 %collective-permute-start.23 = (bf16[33,16,128]{2,1,0:T(8,128)(2,1)S(1)}, bf16[33,16,128]{2,1,0:T(8,128)(2,1)S(1)}, u32[]{:S(2)}, u32[]{:S(2)}) collective-permute-start(bf16[33,16,128]{2,1,0:T(8,128)(2,1)S(1)} %collective-permute-done.16.refs_2_), channel_id=1, source_target_pairs={{0,1},{1,0},{2,3},{3,2},{4,5},{5,4},{6,7},{7,6},{8,9},{9,8},{10,11... | collective-permute-start | bytes 405512 | tf_op jit(solution)/shard_map/ppermute | solution.py:452
  90.7 2.9 %collective-permute-start.24 = (bf16[33,16,128]{2,1,0:T(8,128)(2,1)S(1)}, bf16[33,16,128]{2,1,0:T(8,128)(2,1)S(1)}, u32[]{:S(2)}, u32[]{:S(2)}) collective-permute-start(bf16[33,16,128]{2,1,0:T(8,128)(2,1)S(1)} %collective-permute-done.17.refs_3_), channel_id=1, source_target_pairs={{0,1},{1,0},{2,3},{3,2},{4,5},{5,4},{6,7},{7,6},{8,9},{9,8},{10,11... | collective-permute-start | bytes 405512 | tf_op jit(solution)/shard_map/ppermute | solution.py:452
  92.1 1.3 %collective-permute-start.27 = (bf16[32,16,128]{2,1,0:T(8,128)(2,1)S(1)}, bf16[32,16,128]{2,1,0:T(8,128)(2,1)S(1)}, u32[]{:S(2)}, u32[]{:S(2)}) collective-permute-start(bf16[32,16,128]{2,1,0:T(8,128)(2,1)S(1)} %collective-permute-done.19.refs_6_), channel_id=1, source_target_pairs={{0,1},{1,0},{2,3},{3,2},{4,5},{5,4},{6,7},{7,6},{8,9},{9,8},{10,11... | collective-permute-start | bytes 393224 | tf_op jit(solution)/shard_map/ppermute | solution.py:452
  92.1 1.5 %collective-permute-start.28 = (bf16[32,16,128]{2,1,0:T(8,128)(2,1)S(1)}, bf16[32,16,128]{2,1,0:T(8,128)(2,1)S(1)}, u32[]{:S(2)}, u32[]{:S(2)}) collective-permute-start(bf16[32,16,128]{2,1,0:T(8,128)(2,1)S(1)} %collective-permute-done.20.refs_7_), channel_id=1, source_target_pairs={{0,1},{1,0},{2,3},{3,2},{4,5},{5,4},{6,7},{7,6},{8,9},{9,8},{10,11... | collective-permute-start | bytes 393224 | tf_op jit(solution)/shard_map/ppermute | solution.py:452
